TPU v7x, 128 devices: a whole 4x4x4 slice. The times are simulated.
128 devices in a mesh: cp: 16 (over y_hi, x, core), hd: 8 (over z, y_lo).
Axes of the slice: x: 4, y: 4 (y_hi: 2, y_lo: 2; y = y_hi * 2 + y_lo), z: 4, core: 2. Of those that a mesh axis runs over, the one named last changes fastest.
Arguments:
- hidden_in: bfloat16 [2, 8192, 1024], P(None, ('cp', 'hd')), may hold values from -6 to 6
- doc_ids: int32 [2, 8192], replicated, may hold values from 0 to 2, as said below
- w_query: bfloat16 [1024, 1024], P('cp'), may hold values from -0.1875 to 0.1875
- w_key: bfloat16 [1024, 1024], P('cp'), may hold values from -0.1875 to 0.1875
- w_value: bfloat16 [1024, 2048], P('cp'), may hold values from -0.1875 to 0.1875
- w_decay: bfloat16 [1024, 8], P('cp'), may hold values from -0.1875 to 0.1875
- w_beta: bfloat16 [1024, 8], P('cp'), may hold values from -0.1875 to 0.1875
- w_gate_out: bfloat16 [1024, 2048], P('cp'), may hold values from -0.1875 to 0.1875
- w_output: bfloat16 [2048, 1024], P('cp'), may hold values from -0.25 to 0.25
- w_ffn_gate: bfloat16 [1024, 2816], P('cp'), may hold values from -0.1875 to 0.1875
- w_ffn_up: bfloat16 [1024, 2816], P('cp'), may hold values from -0.1875 to 0.1875
- w_ffn_down: bfloat16 [2816, 1024], P('cp'), may hold values from -0.21875 to 0.21875
- conv_query: bfloat16 [4, 1024], P(None, 'hd'), may hold values from -3 to 3
- conv_key: bfloat16 [4, 1024], P(None, 'hd'), may hold values from -3 to 3
- conv_value: bfloat16 [4, 2048], P(None, 'hd'), may hold values from -3 to 3
- decay_log: bfloat16 [8], P('hd'), may hold values from -9 to -3
- decay_bias: bfloat16 [8], P('hd'), may hold values from -1 to 1
- gain_attn: bfloat16 [1024], P('cp'), may hold values from 0.5 to 1.5
- gain_ffn: bfloat16 [1024], P('cp'), may hold values from 0.5 to 1.5
- gain_head: bfloat16 [256], P('cp'), may hold values from 0.5 to 1.5
- cotangent: bfloat16 [2, 8192, 1024], P(None, ('cp', 'hd')), may hold values from -6 to 6
Outputs:
- block_out: bfloat16 [2, 8192, 1024], P(None, ('cp', 'hd'))
- grad_in: bfloat16 [2, 8192, 1024], P(None, ('cp', 'hd'))
- grad_w_query: float32 [1024, 1024], P('cp')
- grad_w_key: float32 [1024, 1024], P('cp')
- grad_w_value: float32 [1024, 2048], P('cp')
- grad_w_decay: float32 [1024, 8], P('cp')
- grad_w_beta: float32 [1024, 8], P('cp')
- grad_w_gate_out: float32 [1024, 2048], P('cp')
- grad_w_output: float32 [2048, 1024], P('cp')
- grad_w_ffn_gate: float32 [1024, 2816], P('cp')
- grad_w_ffn_up: float32 [1024, 2816], P('cp')
- grad_w_ffn_down: float32 [2816, 1024], P('cp')
- grad_conv_query: float32 [4, 1024], P(None, 'hd')
- grad_conv_key: float32 [4, 1024], P(None, 'hd')
- grad_conv_value: float32 [4, 2048], P(None, 'hd')
- grad_decay_log: float32 [8], P('hd')
- grad_decay_bias: float32 [8], P('hd')
- grad_gain_attn: float32 [1024], P('cp')
- grad_gain_ffn: float32 [1024], P('cp')
- grad_gain_head: float32 [256], P('cp')
Inputs may be any that keep to these rules, and one draw needn't show every extreme that they name: `doc_ids`: each row never falls; document 0 ends within the first 64 tokens of a sequence and document 2 starts within its last 63 tokens.
All inputs are finite; a program needn't handle non-finite values.
Results may differ from a plain program's by a relative error of at most 0.025.
Values may be sent and summed in bfloat16 or wider, within the bound.
A program may use at most 256 MiB of HBM per device.

v0:
```python
import jax
import jax.numpy as jnp
from jax import lax
from jax.sharding import PartitionSpec as P

STRETCH = 64


HIGHEST = lax.Precision.HIGHEST
EPSILON = 1e-06


def passed_along(block, axis, distance):
    devices = range(lax.axis_size(axis))
    route = [(i - distance, i) for i in devices if i - distance in devices]
    return lax.ppermute(block, axis, route)


def carried_in(part, axis, combine, identity):
    place = lax.axis_index(axis)
    gathered = jax.tree.map(lambda a: lax.all_gather(a, axis), part)
    state = jax.tree.map(lambda a, e: jnp.zeros_like(a) + jnp.asarray(e, a.dtype), part, identity)

    def carried_one(hop, state):
        return combine(
            state, jax.tree.map(lambda a: lax.dynamic_index_in_dim(a, hop, 0, False), gathered)
        )

    return lax.fori_loop(0, place, carried_one, state)


def prefix(value, axis, join, neutral):
    count = lax.axis_size(axis)
    place = lax.axis_index(axis)
    ahead = count - 1 - place
    gathered = jax.tree.map(
        lambda a, kind: lax.all_gather(a.astype(kind), axis),
        value,
        jax.tree.map(lambda a: jnp.bfloat16 if a.dtype == jnp.float32 else a.dtype, value),
    )
    state = jax.tree.map(lambda a, e: jnp.zeros_like(a) + jnp.asarray(e, a.dtype), value, neutral)

    def prefix_one(hop, state):
        source = count - 1 - hop
        return join(
            state,
            jax.tree.map(
                lambda a, own: lax.dynamic_index_in_dim(a, source, 0, False).astype(own.dtype),
                gathered,
                value,
            ),
        )

    return lax.fori_loop(0, ahead, prefix_one, state)


def norm_gain(source, gain_vec):
    return source * lax.rsqrt(jnp.mean(source * source, -1, keepdims=True) + EPSILON) * gain_vec


def unit_rows(source):
    return source * lax.rsqrt(jnp.sum(source * source, -1, keepdims=True) + EPSILON)


def gated_norm(mixed_head, gate_pre, gain_vec):
    scale = lax.rsqrt(jnp.mean(mixed_head * mixed_head, -1, keepdims=True) + EPSILON)
    return mixed_head * scale * gain_vec * jax.nn.silu(gate_pre.reshape(mixed_head.shape))


def block_terms(key_rows, beta_rows, decays, doc_rows, doc_before):
    length = key_rows.shape[0]
    cumulative = jnp.cumsum(decays)
    survive = jnp.exp(cumulative) * (doc_rows == doc_before).astype(jnp.float32)
    places = jnp.arange(length)
    linked = (places[:, None] >= places[None, :]) & (doc_rows[:, None] == doc_rows[None, :])
    between = jnp.where(
        linked, jnp.exp(jnp.where(linked, cumulative[:, None] - cumulative[None, :], 0.0)), 0.0
    )
    strict = (places[:, None] > places[None, :]).astype(jnp.float32)
    system = jnp.eye(length, dtype=jnp.float32) + beta_rows[:, None] * between * strict * jnp.dot(
        key_rows, key_rows.T, precision=HIGHEST
    )
    return (survive, between, system)


def unit_inverse(system):
    width = system.shape[-1]
    unit_mat = jnp.eye(width, dtype=jnp.float32)
    powered = unit_mat - system
    inverse = unit_mat + powered
    for level in range(width.bit_length() - 2):
        powered = jnp.einsum("bij,bjk->bik", powered, powered, precision=HIGHEST)
        inverse = inverse + jnp.einsum("bij,bjk->bik", inverse, powered, precision=HIGHEST)
    return inverse


def compose_local(earlier, later):
    return (
        jnp.einsum("bij,bjk->bik", later[0], earlier[0], precision=HIGHEST),
        jnp.einsum("bij,bjk->bik", later[0], earlier[1], precision=HIGHEST) + later[1],
    )


def block_maps(key_rows, values, beta_rows, decays, doc_rows, doc_before):
    blocks = doc_rows.shape[0] // STRETCH
    starts = jnp.concatenate([doc_before[None], doc_rows[:-1]]).reshape(blocks, STRETCH)[:, 0]
    key_blocks = key_rows.reshape(blocks, STRETCH, -1)
    beta_blocks = beta_rows.reshape(blocks, STRETCH)
    survive, between, system = jax.vmap(block_terms)(
        key_blocks,
        beta_blocks,
        decays.reshape(blocks, STRETCH),
        doc_rows.reshape(blocks, STRETCH),
        starts,
    )
    inverse = unit_inverse(system)
    weighted = jnp.einsum(
        "bij,bjk->bik", inverse, (beta_blocks * survive)[:, :, None] * key_blocks, precision=HIGHEST
    )
    written = jnp.einsum(
        "bij,bjk->bik",
        inverse,
        beta_blocks[:, :, None] * values.reshape(blocks, STRETCH, -1),
        precision=HIGHEST,
    )
    last_row = between[:, -1][:, :, None]
    folded_key = jnp.einsum("bci,bcj->bij", key_blocks, last_row * weighted, precision=HIGHEST)
    folded_value = jnp.einsum("bci,bcj->bij", key_blocks, last_row * written, precision=HIGHEST)
    unit_mat = jnp.eye(key_blocks.shape[2], dtype=jnp.float32)
    step_map = survive[:, -1][:, None, None] * unit_mat - folded_key
    maps = lax.associative_scan(compose_local, (step_map, folded_value))
    return (key_blocks, survive, between, weighted, written, maps)


def segment_map(key_rows, values, beta_rows, decays, doc_rows, doc_before):
    maps = block_maps(key_rows, values, beta_rows, decays, doc_rows, doc_before)[5]
    return (maps[0][-1], maps[1][-1])


def segment_run(queries, key_rows, values, beta_rows, decays, doc_rows, doc_before, state_now):
    key_blocks, survive, between, weighted, written, maps = block_maps(
        key_rows, values, beta_rows, decays, doc_rows, doc_before
    )
    blocks = key_blocks.shape[0]
    entered = jnp.einsum("bij,jk->bik", maps[0], state_now, precision=HIGHEST) + maps[1]
    states = jnp.concatenate([state_now[None], entered[:-1]], 0)
    query_blocks = queries.reshape(blocks, STRETCH, -1)
    updates = written - jnp.einsum("bcj,bjk->bck", weighted, states, precision=HIGHEST)
    scores = jnp.einsum("bcj,bdj->bcd", query_blocks, key_blocks, precision=HIGHEST) * between
    output = survive[:, :, None] * jnp.einsum(
        "bcj,bjk->bck", query_blocks, states, precision=HIGHEST
    ) + jnp.einsum("bcd,bdk->bck", scores, updates, precision=HIGHEST)
    return (output.reshape(doc_rows.shape[0], -1), entered[-1])


def conv_core(padded, weight, doc_pad):
    tap_count = weight.shape[0]
    length = padded.shape[1] - (tap_count - 1)
    current = doc_pad[:, tap_count - 1 :]
    summed = jnp.zeros((padded.shape[0], length, padded.shape[2]), jnp.float32)
    for offset in range(tap_count):
        first_row = tap_count - 1 - offset
        window = padded[:, first_row : first_row + length]
        same_doc = (doc_pad[:, first_row : first_row + length] == current).astype(jnp.float32)
        summed = summed + weight[offset] * window * same_doc[:, :, None]
    return jax.nn.silu(summed)


def prepare(
    query_ext,
    key_ext,
    value_ext,
    decay_head,
    beta_head,
    conv_query,
    conv_key,
    conv_value,
    decay_log,
    decay_bias,
    doc_ext,
):
    head_count = decay_log.shape[0]
    queries = conv_core(query_ext, conv_query, doc_ext)
    sequences, length = (queries.shape[0], queries.shape[1])
    queries = queries.reshape(sequences, length, head_count, -1)
    key_rows = conv_core(key_ext, conv_key, doc_ext).reshape(sequences, length, head_count, -1)
    values = conv_core(value_ext, conv_value, doc_ext).reshape(sequences, length, head_count, -1)
    queries = unit_rows(queries) * queries.shape[-1] ** (-0.5)
    key_rows = unit_rows(key_rows)
    beta_rows = jax.nn.sigmoid(beta_head)
    decays = -jnp.exp(decay_log) * jax.nn.softplus(decay_head + decay_bias)
    return (
        jnp.moveaxis(queries, 2, 1),
        jnp.moveaxis(key_rows, 2, 1),
        jnp.moveaxis(values, 2, 1),
        jnp.moveaxis(beta_rows, 2, 1),
        jnp.moveaxis(decays, 2, 1),
    )


def compose(earlier, later):
    return (
        jnp.einsum("shij,shjk->shik", later[0], earlier[0], precision=HIGHEST),
        jnp.einsum("shij,shjk->shik", later[0], earlier[1], precision=HIGHEST) + later[1],
    )


def on_device(
    hidden_in,
    doc_ids,
    w_query,
    w_key,
    w_value,
    w_decay,
    w_beta,
    w_gate_out,
    w_output,
    w_ffn_gate,
    w_ffn_up,
    w_ffn_down,
    conv_query,
    conv_key,
    conv_value,
    decay_log,
    decay_bias,
    gain_attn,
    gain_ffn,
    gain_head,
    cotangent,
):
    weights_full = (
        lax.all_gather(w_query, "cp", axis=0, tiled=True),
        lax.all_gather(w_key, "cp", axis=0, tiled=True),
        lax.all_gather(w_value, "cp", axis=0, tiled=True),
        lax.all_gather(w_decay, "cp", axis=0, tiled=True),
        lax.all_gather(w_beta, "cp", axis=0, tiled=True),
        lax.all_gather(w_gate_out, "cp", axis=0, tiled=True),
        lax.all_gather(w_output, "cp", axis=0, tiled=True),
        lax.all_gather(w_ffn_gate, "cp", axis=0, tiled=True),
        lax.all_gather(w_ffn_up, "cp", axis=0, tiled=True),
        lax.all_gather(w_ffn_down, "cp", axis=0, tiled=True),
        lax.all_gather(gain_attn, "cp", axis=0, tiled=True),
        lax.all_gather(gain_ffn, "cp", axis=0, tiled=True),
        lax.all_gather(gain_head, "cp", axis=0, tiled=True),
    )
    (
        query_full,
        key_full,
        value_full,
        decay_full,
        beta_full,
        gate_full,
        output_full,
        ffn_gate_full,
        ffn_up_full,
        ffn_down_full,
    ) = weights_full[:10]
    attn_gain = weights_full[10].astype(jnp.float32)
    ffn_gain = weights_full[11].astype(jnp.float32)
    head_gain = weights_full[12].astype(jnp.float32)
    sequences, tokens = (hidden_in.shape[0], hidden_in.shape[1])
    head_count = decay_full.shape[1]
    inputs = hidden_in.astype(jnp.float32)
    normed = norm_gain(inputs, attn_gain).astype(jnp.bfloat16)

    def project(matrix):
        return jnp.einsum("std,de->ste", normed, matrix, preferred_element_type=jnp.float32)

    query_pre = project(query_full).astype(jnp.bfloat16)
    key_pre = project(key_full).astype(jnp.bfloat16)
    value_pre = project(value_full).astype(jnp.bfloat16)
    decay_pre = project(decay_full).astype(jnp.bfloat16)
    beta_pre = project(beta_full).astype(jnp.bfloat16)
    gate_pre = project(gate_full)
    query_head, key_head, value_head, decay_head, beta_head = (
        lax.all_to_all(query_pre, "hd", split_axis=2, concat_axis=1, tiled=True),
        lax.all_to_all(key_pre, "hd", split_axis=2, concat_axis=1, tiled=True),
        lax.all_to_all(value_pre, "hd", split_axis=2, concat_axis=1, tiled=True),
        lax.all_to_all(decay_pre, "hd", split_axis=2, concat_axis=1, tiled=True),
        lax.all_to_all(beta_pre, "hd", split_axis=2, concat_axis=1, tiled=True),
    )
    margin = conv_query.shape[0] - 1
    span_tokens = query_head.shape[1]
    rim_query, rim_key, rim_value = passed_along(
        (query_head[:, -margin:], key_head[:, -margin:], value_head[:, -margin:]), "cp", 1
    )
    doc_pad = jnp.concatenate([jnp.full((doc_ids.shape[0], margin), -1, jnp.int32), doc_ids], 1)
    doc_ext = lax.dynamic_slice_in_dim(
        doc_pad, lax.axis_index("cp") * span_tokens, span_tokens + margin, 1
    )
    doc_span = doc_ext[:, margin:]
    doc_before = doc_ext[:, margin - 1]
    head_floats = (
        jnp.concatenate([rim_query, query_head], 1).astype(jnp.float32),
        jnp.concatenate([rim_key, key_head], 1).astype(jnp.float32),
        jnp.concatenate([rim_value, value_head], 1).astype(jnp.float32),
        decay_head.astype(jnp.float32),
        beta_head.astype(jnp.float32),
        conv_query.astype(jnp.float32),
        conv_key.astype(jnp.float32),
        conv_value.astype(jnp.float32),
        decay_log.astype(jnp.float32),
        decay_bias.astype(jnp.float32),
    )
    prepared, prepare_pull = jax.vjp(lambda *entries: prepare(*entries, doc_ext), *head_floats)
    queries, key_rows, values, beta_rows, decays = prepared
    run_heads = jax.vmap(
        jax.vmap(segment_run, (0, 0, 0, 0, 0, None, None, 0)), (0, 0, 0, 0, 0, 0, 0, 0)
    )
    map_heads = jax.vmap(jax.vmap(segment_map, (0, 0, 0, 0, None, None)), (0, 0, 0, 0, 0, 0))
    transfer, offset = map_heads(key_rows, values, beta_rows, decays, doc_span, doc_before)
    identity = (
        jnp.broadcast_to(jnp.eye(transfer.shape[-1], dtype=jnp.float32), transfer.shape),
        jnp.zeros_like(offset),
    )
    _, entry_state = carried_in((transfer, offset), "cp", compose, identity)
    mixed_head, _ = run_heads(
        queries, key_rows, values, beta_rows, decays, doc_span, doc_before, entry_state
    )
    mixed_low = (
        jnp.moveaxis(mixed_head, 1, 2).reshape(sequences, span_tokens, -1).astype(jnp.bfloat16)
    )
    mixed_tok = lax.all_to_all(mixed_low, "hd", split_axis=1, concat_axis=2, tiled=True)
    mixed_float = mixed_tok.astype(jnp.float32).reshape(sequences, tokens, head_count, -1)
    normed_head = (
        gated_norm(mixed_float, gate_pre, head_gain)
        .reshape(sequences, tokens, -1)
        .astype(jnp.bfloat16)
    )
    attention = jnp.einsum(
        "ste,ed->std", normed_head, output_full, preferred_element_type=jnp.float32
    )
    middle = inputs + attention
    ffn_in = norm_gain(middle, ffn_gain).astype(jnp.bfloat16)
    gate_val = jnp.einsum("std,df->stf", ffn_in, ffn_gate_full, preferred_element_type=jnp.float32)
    up_val = jnp.einsum("std,df->stf", ffn_in, ffn_up_full, preferred_element_type=jnp.float32)
    inner_act = (jax.nn.silu(gate_val) * up_val).astype(jnp.bfloat16)
    block_out = (
        middle
        + jnp.einsum("stf,fd->std", inner_act, ffn_down_full, preferred_element_type=jnp.float32)
    ).astype(jnp.bfloat16)
    grad_inner = jnp.einsum(
        "std,fd->stf", cotangent, ffn_down_full, preferred_element_type=jnp.float32
    )
    _, swiglu_pull = jax.vjp(lambda first, second: jax.nn.silu(first) * second, gate_val, up_val)
    grad_gate_val, grad_up_val = swiglu_pull(grad_inner)
    grad_gate_low = grad_gate_val.astype(jnp.bfloat16)
    grad_up_low = grad_up_val.astype(jnp.bfloat16)
    grad_ffn_in = jnp.einsum(
        "stf,df->std", grad_gate_low, ffn_gate_full, preferred_element_type=jnp.float32
    ) + jnp.einsum("stf,df->std", grad_up_low, ffn_up_full, preferred_element_type=jnp.float32)
    _, middle_pull = jax.vjp(norm_gain, middle, ffn_gain)
    grad_middle_norm, grad_ffn_gain = middle_pull(grad_ffn_in)
    grad_middle = cotangent.astype(jnp.float32) + grad_middle_norm
    grad_attention = grad_middle.astype(jnp.bfloat16)
    grad_normed_head = jnp.einsum(
        "std,ed->ste", grad_attention, output_full, preferred_element_type=jnp.float32
    )
    _, gated_pull = jax.vjp(gated_norm, mixed_float, gate_pre, head_gain)
    grad_mixed, grad_gate_pre, grad_head_gain = gated_pull(
        grad_normed_head.reshape(mixed_float.shape)
    )
    grad_gate_pre_low = grad_gate_pre.astype(jnp.bfloat16)
    grad_mixed_low = grad_mixed.reshape(sequences, tokens, -1).astype(jnp.bfloat16)
    grad_mixed_head = lax.all_to_all(grad_mixed_low, "hd", split_axis=2, concat_axis=1, tiled=True)
    grad_mixed_float = jnp.moveaxis(
        grad_mixed_head.astype(jnp.float32).reshape(sequences, span_tokens, decay_log.shape[0], -1),
        2,
        1,
    )
    _, state_pull = jax.vjp(
        lambda state_now: run_heads(
            queries, key_rows, values, beta_rows, decays, doc_span, doc_before, state_now
        ),
        entry_state,
    )
    local_grad = state_pull((grad_mixed_float, jnp.zeros_like(entry_state)))[0]
    _, carried = prefix((jnp.swapaxes(transfer, -1, -2), local_grad), "cp", compose, identity)
    _, run_pull = jax.vjp(
        lambda q_in, k_in, v_in, b_in, d_in: run_heads(
            q_in, k_in, v_in, b_in, d_in, doc_span, doc_before, entry_state
        ),
        queries,
        key_rows,
        values,
        beta_rows,
        decays,
    )
    grad_prepared = run_pull((grad_mixed_float, carried))
    grads_head = prepare_pull(grad_prepared)
    grad_query_ext, grad_key_ext, grad_value_ext, grad_decay_head, grad_beta_head = grads_head[:5]
    back_query, back_key, back_value = passed_along(
        (grad_query_ext[:, :margin], grad_key_ext[:, :margin], grad_value_ext[:, :margin]), "cp", -1
    )

    def settle(grad_ext, incoming):
        return grad_ext[:, margin:].at[:, -margin:].add(incoming).astype(jnp.bfloat16)

    tok_query, tok_key, tok_value, tok_decay, tok_beta = (
        lax.all_to_all(
            settle(grad_query_ext, back_query), "hd", split_axis=1, concat_axis=2, tiled=True
        ),
        lax.all_to_all(
            settle(grad_key_ext, back_key), "hd", split_axis=1, concat_axis=2, tiled=True
        ),
        lax.all_to_all(
            settle(grad_value_ext, back_value), "hd", split_axis=1, concat_axis=2, tiled=True
        ),
        lax.all_to_all(
            grad_decay_head.astype(jnp.bfloat16), "hd", split_axis=1, concat_axis=2, tiled=True
        ),
        lax.all_to_all(
            grad_beta_head.astype(jnp.bfloat16), "hd", split_axis=1, concat_axis=2, tiled=True
        ),
    )
    head_sums = lax.psum(
        (grads_head[5], grads_head[6], grads_head[7], grads_head[8], grads_head[9]), "cp"
    )

    def weight_grad(left_side, right_side):
        return jnp.einsum("std,ste->de", left_side, right_side, preferred_element_type=jnp.float32)

    def input_grad(grad_low, matrix):
        return jnp.einsum("ste,de->std", grad_low, matrix, preferred_element_type=jnp.float32)

    grad_normed = (
        input_grad(tok_query, query_full)
        + input_grad(tok_key, key_full)
        + input_grad(tok_value, value_full)
        + input_grad(tok_decay, decay_full)
        + input_grad(tok_beta, beta_full)
        + input_grad(grad_gate_pre_low, gate_full)
    )
    _, input_pull = jax.vjp(norm_gain, inputs, attn_gain)
    grad_norm_in, grad_attn_gain = input_pull(grad_normed)
    grad_in = (grad_middle + grad_norm_in).astype(jnp.bfloat16)
    scattered = (
        lax.psum_scatter(
            weight_grad(normed, tok_query).astype(jnp.bfloat16),
            "cp",
            scatter_dimension=0,
            tiled=True,
        ).astype(jnp.float32),
        lax.psum_scatter(
            weight_grad(normed, tok_key).astype(jnp.bfloat16), "cp", scatter_dimension=0, tiled=True
        ).astype(jnp.float32),
        lax.psum_scatter(
            weight_grad(normed, tok_value).astype(jnp.bfloat16),
            "cp",
            scatter_dimension=0,
            tiled=True,
        ).astype(jnp.float32),
        lax.psum_scatter(
            weight_grad(normed, tok_decay).astype(jnp.bfloat16),
            "cp",
            scatter_dimension=0,
            tiled=True,
        ).astype(jnp.float32),
        lax.psum_scatter(
            weight_grad(normed, tok_beta).astype(jnp.bfloat16),
            "cp",
            scatter_dimension=0,
            tiled=True,
        ).astype(jnp.float32),
        lax.psum_scatter(
            weight_grad(normed, grad_gate_pre_low).astype(jnp.bfloat16),
            "cp",
            scatter_dimension=0,
            tiled=True,
        ).astype(jnp.float32),
        lax.psum_scatter(
            weight_grad(normed_head, grad_attention).astype(jnp.bfloat16),
            "cp",
            scatter_dimension=0,
            tiled=True,
        ).astype(jnp.float32),
        lax.psum_scatter(
            weight_grad(ffn_in, grad_gate_low).astype(jnp.bfloat16),
            "cp",
            scatter_dimension=0,
            tiled=True,
        ).astype(jnp.float32),
        lax.psum_scatter(
            weight_grad(ffn_in, grad_up_low).astype(jnp.bfloat16),
            "cp",
            scatter_dimension=0,
            tiled=True,
        ).astype(jnp.float32),
        lax.psum_scatter(
            weight_grad(inner_act, cotangent).astype(jnp.bfloat16),
            "cp",
            scatter_dimension=0,
            tiled=True,
        ).astype(jnp.float32),
        lax.psum_scatter(
            grad_attn_gain.astype(jnp.bfloat16), "cp", scatter_dimension=0, tiled=True
        ).astype(jnp.float32),
        lax.psum_scatter(
            grad_ffn_gain.astype(jnp.bfloat16), "cp", scatter_dimension=0, tiled=True
        ).astype(jnp.float32),
        lax.psum_scatter(
            grad_head_gain.astype(jnp.bfloat16), "cp", scatter_dimension=0, tiled=True
        ).astype(jnp.float32),
    )
    summed = (
        lax.psum(scattered[0].astype(jnp.bfloat16), "hd").astype(jnp.float32),
        lax.psum(scattered[1].astype(jnp.bfloat16), "hd").astype(jnp.float32),
        lax.psum(scattered[2].astype(jnp.bfloat16), "hd").astype(jnp.float32),
        lax.psum(scattered[3].astype(jnp.bfloat16), "hd").astype(jnp.float32),
        lax.psum(scattered[4].astype(jnp.bfloat16), "hd").astype(jnp.float32),
        lax.psum(scattered[5].astype(jnp.bfloat16), "hd").astype(jnp.float32),
        lax.psum(scattered[6].astype(jnp.bfloat16), "hd").astype(jnp.float32),
        lax.psum(scattered[7].astype(jnp.bfloat16), "hd").astype(jnp.float32),
        lax.psum(scattered[8].astype(jnp.bfloat16), "hd").astype(jnp.float32),
        lax.psum(scattered[9].astype(jnp.bfloat16), "hd").astype(jnp.float32),
        lax.psum(scattered[10].astype(jnp.bfloat16), "hd").astype(jnp.float32),
        lax.psum(scattered[11].astype(jnp.bfloat16), "hd").astype(jnp.float32),
        lax.psum(scattered[12].astype(jnp.bfloat16), "hd").astype(jnp.float32),
    )
    weight_list = summed[:10]
    gain_list = summed[10:]
    return (
        block_out,
        grad_in,
        weight_list[0],
        weight_list[1],
        weight_list[2],
        weight_list[3],
        weight_list[4],
        weight_list[5],
        weight_list[6],
        weight_list[7],
        weight_list[8],
        weight_list[9],
        head_sums[0],
        head_sums[1],
        head_sums[2],
        head_sums[3],
        head_sums[4],
        gain_list[0],
        gain_list[1],
        gain_list[2],
    )


def solution(mesh):
    placed = (
        P(None, ("cp", "hd"), None),
        P(),
        P("cp", None),
        P("cp", None),
        P("cp", None),
        P("cp", None),
        P("cp", None),
        P("cp", None),
        P("cp", None),
        P("cp", None),
        P("cp", None),
        P("cp", None),
        P(None, "hd"),
        P(None, "hd"),
        P(None, "hd"),
        P("hd"),
        P("hd"),
        P("cp"),
        P("cp"),
        P("cp"),
        P(None, ("cp", "hd"), None),
    )
    return jax.shard_map(
        on_device,
        mesh=mesh,
        in_specs=placed,
        out_specs=(
            P(None, ("cp", "hd"), None),
            P(None, ("cp", "hd"), None),
            P("cp", None),
            P("cp", None),
            P("cp", None),
            P("cp", None),
            P("cp", None),
            P("cp", None),
            P("cp", None),
            P("cp", None),
            P("cp", None),
            P("cp", None),
            P(None, "hd"),
            P(None, "hd"),
            P(None, "hd"),
            P("hd"),
            P("hd"),
            P("cp"),
            P("cp"),
            P("cp"),
        ),
        check_vma=False,
    )
```

profile of v0, /device:TPU:8, one launch (start us, length us, event | category | flops | bytes accessed | tf_op | source)
XLA Modules:
  0.0 1879.9 jit_solution(3025577807203437146)
XLA Ops:
  13.9 38.4 %all-reduce.73 = (bf16[1024]{0:T(1024)(128)(2,1)S(1)}, bf16[256]{0:T(256)(128)(2,1)}, bf16[1024]{0:T(1024)(128)(2,1)}) all-reduce(bf16[1024]{0:T(1024)(128)(2,1)S(1)} %dynamic-update-slice.9, bf16[256]{0:T(256)(128)(2,1)S(1)} %dynamic-update-slice.10, bf16[1024]{0:T(1024)(128)(2,1)S(1)} %dynamic-update-slice.11), channel_id=1, replica_groups=mesh['cp'=16,'hd'=8] {'cp'}, use_global_device_ids=true, to_apply=%add.65 | all-reduce | flops 2304 | bytes 9216
  52.2 19.3 %all-gather.4 = bf16[16,64,8]{1,2,0:T(8,128)(2,1)S(1)} all-gather(bf16[1,64,8]{1,2,0:T(8,128)(2,1)} %bitcast.1116), channel_id=1, replica_groups=mesh['cp'=16,'hd'=8] {'cp'}, dimensions={0}, use_global_device_ids=true | all-gather | bytes 17408 | tf_op jit(solution)/shard_map/all_gather | solution.py:235
  74.6 6.7 all-to-all-start
  86.0 21.3 %all-gather.5 = bf16[16,64,8]{1,2,0:T(8,128)(2,1)S(1)} all-gather(bf16[1,64,8]{1,2,0:T(8,128)(2,1)} %bitcast.1117), channel_id=1, replica_groups=mesh['cp'=16,'hd'=8] {'cp'}, dimensions={0}, use_global_device_ids=true | all-gather | bytes 17408 | tf_op jit(solution)/shard_map/all_gather | solution.py:236
  111.6 5.7 all-to-all-start.3
  127.2 4.8 all-to-all-start.2
  188.0 5.8 pad.292
  213.0 14.8 all_to_all.186
  262.6 6.5 pad.297
  269.2 6.5 pad.298
  287.6 6.5 pad.383
  294.1 44.2 %all-gather.37.cloned.1.call-done = f32[32,1,1,128,256]{4,3,2,1,0:T(8,128)} async-done(((f32[2,1,1,128,256]{4,3,2,1,0:T(8,128)}), f32[32,1,1,128,256]{4,3,2,1,0:T(8,128)}) %all-gather.37.cloned.1.call-update) | async-done | bytes 4194320 | tf_op jit(solution)/shard_map/all_gather | solution.py:21
  348.7 5.9 all-to-all-start.5
  355.1 45.4 %all-gather.25.cloned.1.call-done = bf16[1024,2048]{1,0:T(8,128)(2,1)} async-done(((bf16[64,2048]{1,0:T(8,128)(2,1)}), bf16[1024,2048]{1,0:T(8,128)(2,1)}) %all-gather.25.cloned.1.call-update) | async-done | bytes 4194320 | tf_op jit(solution)/shard_map/all_gather | solution.py:237
  404.8 59.0 %all-gather.33.cloned.1.call-done = bf16[2816,1024]{1,0:T(8,128)(2,1)} async-done(((bf16[176,1024]{1,0:T(8,128)(2,1)}), bf16[2816,1024]{1,0:T(8,128)(2,1)}) %all-gather.33.cloned.1.call-update) | async-done | bytes 5767184 | tf_op jit(solution)/shard_map/all_gather | solution.py:241
  463.8 5.8 fusion.10
  478.0 43.0 %all-gather.27.cloned.1.call-done = bf16[2048,1024]{1,0:T(8,128)(2,1)} async-done(((bf16[128,1024]{1,0:T(8,128)(2,1)}), bf16[2048,1024]{1,0:T(8,128)(2,1)}) %all-gather.27.cloned.1.call-update) | async-done | bytes 4194320 | tf_op jit(solution)/shard_map/all_gather | solution.py:238
  525.4 58.8 %all-gather.31.cloned.1.call-done = bf16[1024,2816]{1,0:T(8,128)(2,1)} async-done(((bf16[64,2816]{1,0:T(8,128)(2,1)}), bf16[1024,2816]{1,0:T(8,128)(2,1)}) %all-gather.31.cloned.1.call-update) | async-done | bytes 5767184 | tf_op jit(solution)/shard_map/all_gather | solution.py:240
  584.2 4.7 fusion.16
  588.9 58.3 %all-gather.29.cloned.1.call-done = bf16[1024,2816]{1,0:T(8,128)(2,1)} async-done(((bf16[64,2816]{1,0:T(8,128)(2,1)}), bf16[1024,2816]{1,0:T(8,128)(2,1)}) %all-gather.29.cloned.1.call-update) | async-done | bytes 5767184 | tf_op jit(solution)/shard_map/all_gather | solution.py:239
  647.2 5.8 fusion.57
  675.4 15.4 all_to_all.187
  720.3 40.0 %all-gather.41.cloned.1.call-done = bf16[32,1,128,256]{3,2,1,0:T(8,128)(2,1)} async-done(((bf16[2,1,128,256]{3,2,1,0:T(8,128)(2,1)}), bf16[32,1,128,256]{3,2,1,0:T(8,128)(2,1)}) %all-gather.41.cloned.1.call-update) | async-done | bytes 2097168 | tf_op jit(solution)/shard_map/all_gather | solution.py:37
  760.4 20.0 %while.30 = (s32[]{:T(128)}, f32[2,1,128,256]{3,2,0,1:T(8,128)S(1)}, s32[]{:T(128)}, bf16[16,2,1,128,128]{4,3,1,2,0:T(8,128)(2,1)}, bf16[16,2,1,128,256]{4,3,1,2...) while((s32[]{:T(128)}, f32[2,1,128,256]{3,2,0,1:T(8,128)S(1)}, s32[]{:T(128)}, ...), condition=%wide.region_12.13_spmd, body=%wide.region_11.12_spmd.sunk | while | flops 100794376 | bytes 1246347 | solution.py:54
  823.3 6.5 pad.321
  829.8 6.5 pad.322
  836.3 5.6 pad.307
  873.2 4.8 pad.325
  878.1 5.7 pad.339
  883.8 6.1 pad.340
  928.0 5.9 all-to-all-start.11
  940.0 5.6 all-to-all-start.10
  945.9 6.0 all-to-all-done.10
  989.5 10.6 all_to_all.188
  1011.5 10.6 all_to_all.189
  1047.6 14.3 all_to_all.190
  1072.5 35.0 %all-reduce.71 = (f32[4,128]{1,0:T(4,128)}, f32[4,128]{1,0:T(4,128)}, f32[4,256]{1,0:T(4,128)}, f32[1]{0:T(128)}, f32[1]{0:T(128)}) all-reduce(f32[4,128]{1,0:T(4,128)S(1)} %pad_add_fusion.18, f32[4,128]{1,0:T(4,128)S(1)} %pad_add_fusion.17, f32[4,256]{1,0:T(4,128)S(1)} %pad_add_fusion.16, ...), channel_id=1, replica_groups=mesh['cp'=16,'hd'=8] {'cp'}, use_global_device_ids=true, to_apply=%region_49.50 | all-reduce | flops 2050 | bytes 16400 | tf_op jit(solution)/shard_map/psum | solution.py:416
  1109.1 56.6 %reduce-scatter.23.cloned.1.call-done = bf16[128,1024]{1,0:T(8,128)(2,1)} async-done(((bf16[2048,1024]{1,0:T(8,128)(2,1)}), bf16[128,1024]{1,0:T(8,128)(2,1)}) %reduce-scatter.23.cloned.1.call-update) | async-done | bytes 262160 | tf_op jit(solution)/shard_map/reduce_scatter | solution.py:471
  1165.8 83.7 %reduce-scatter.21.cloned.1.call-done = bf16[64,2048]{1,0:T(8,128)(2,1)} async-done(((bf16[1024,2048]{1,0:T(8,128)(2,1)}), bf16[64,2048]{1,0:T(8,128)(2,1)}) %reduce-scatter.21.cloned.1.call-update) | async-done | bytes 262160 | tf_op jit(solution)/shard_map/reduce_scatter | solution.py:465
  1249.5 73.7 %reduce-scatter.15.cloned.1.call-done = bf16[64,1024]{1,0:T(8,128)(2,1)} async-done(((bf16[1024,1024]{1,0:T(8,128)(2,1)}), bf16[64,1024]{1,0:T(8,128)(2,1)}) %reduce-scatter.15.cloned.1.call-update) | async-done | bytes 131088 | tf_op jit(solution)/shard_map/reduce_scatter | solution.py:438
  1323.1 73.8 %reduce-scatter.17.cloned.1.call-done = bf16[64,1024]{1,0:T(8,128)(2,1)} async-done(((bf16[1024,1024]{1,0:T(8,128)(2,1)}), bf16[64,1024]{1,0:T(8,128)(2,1)}) %reduce-scatter.17.cloned.1.call-update) | async-done | bytes 131088 | tf_op jit(solution)/shard_map/reduce_scatter | solution.py:444
  1396.9 90.1 %reduce-scatter.25.cloned.1.call-done = bf16[64,2816]{1,0:T(8,128)(2,1)} async-done(((bf16[1024,2816]{1,0:T(8,128)(2,1)}), bf16[64,2816]{1,0:T(8,128)(2,1)}) %reduce-scatter.25.cloned.1.call-update) | async-done | bytes 360464 | tf_op jit(solution)/shard_map/reduce_scatter | solution.py:477
  1487.0 89.8 %reduce-scatter.27.cloned.1.call-done = bf16[64,2816]{1,0:T(8,128)(2,1)} async-done(((bf16[1024,2816]{1,0:T(8,128)(2,1)}), bf16[64,2816]{1,0:T(8,128)(2,1)}) %reduce-scatter.27.cloned.1.call-update) | async-done | bytes 360464 | tf_op jit(solution)/shard_map/reduce_scatter | solution.py:483
  1576.8 90.0 %reduce-scatter.29.cloned.1.call-done = bf16[176,1024]{1,0:T(8,128)(2,1)} async-done(((bf16[2816,1024]{1,0:T(8,128)(2,1)}), bf16[176,1024]{1,0:T(8,128)(2,1)}) %reduce-scatter.29.cloned.1.call-update) | async-done | bytes 360464 | tf_op jit(solution)/shard_map/reduce_scatter | solution.py:489
  1666.8 83.3 %reduce-scatter.19.cloned.1.call-done = bf16[64,2048]{1,0:T(8,128)(2,1)} async-done(((bf16[1024,2048]{1,0:T(8,128)(2,1)}), bf16[64,2048]{1,0:T(8,128)(2,1)}) %reduce-scatter.19.cloned.1.call-update) | async-done | bytes 262160 | tf_op jit(solution)/shard_map/reduce_scatter | solution.py:447
  1758.3 35.1 %all-reduce.72 = (bf16[1024]{0:T(1024)(128)(2,1)S(1)}, bf16[1024]{0:T(1024)(128)(2,1)S(1)}, bf16[256]{0:T(256)(128)(2,1)S(1)}) all-reduce(bf16[1024]{0:T(1024)(128)(2,1)S(1)} %get-tuple-element.262, bf16[1024]{0:T(1024)(128)(2,1)S(1)} %copy-done.219, bf16[256]{0:T(256)(128)(2,1)S(1)} %copy-done.239), channel_id=16, replica_groups=mesh['cp'=16,'hd'=8] {'cp'}, use_global_device_ids=true, to_apply=%region_65.66.clone | all-reduce | flops 2304 | bytes 9216
  1793.7 17.7 all-reduce.74
  1815.0 49.3 %all-reduce.78.cloned.1.call-done = (bf16[64,1024]{1,0:T(8,128)(2,1)}, bf16[64,1024]{1,0:T(8,128)(2,1)}, bf16[64,2048]{1,0:T(8,128)(2,1)}, bf16[64,2048]{1,0:T(8...) async-done(((bf16[64,1024]{1,0:T(8,128)(2,1)}, bf16[64,1024]{1,0:T(8,128)(2,1)}, ...) | async-done | bytes 2129936 | tf_op jit(solution)/shard_map/psum | solution.py:506
  (931 shorter events, 467.1 us)
Async XLA Ops:
  7.2 116.4 %copy-start = (bf16[2,64,1024]{2,1,0:T(8,128)(2,1)S(1)}, bf16[2,64,1024]{2,1,0:T(8,128)(2,1)}, u32[]{:S(2)}) copy-start(bf16[2,64,1024]{2,1,0:T(8,128)(2,1)} %param.31) | copy-start | bytes 786436
  7.2 116.4 %all-gather.21.cloned.1.call-start = ((), (), s32[]{:S(2)}) async-start(), calls=%async_computation.23 | async-start | bytes 2228224 | tf_op jit(solution)/shard_map/all_gather | solution.py:233
  7.9 124.0 %all-gather.19.cloned.1.call-start = ((), (), s32[]{:S(2)}) async-start(), calls=%async_computation.22 | async-start | bytes 2228224 | tf_op jit(solution)/shard_map/all_gather | solution.py:232
  74.6 36.9 %all-to-all-start = ((bf16[2,64,8]{1,0,2:T(2,128)(2,1)}), bf16[2,64,8]{1,0,2:T(2,128)(2,1)S(1)}, u32[]{:S(2)}, u32[]{:S(2)}) async-start(bf16[2,64,8]{1,0,2:T(2,128)(2,1)} %copy.533), calls=%async_computation | async-start | bytes 8192 | tf_op jit(solution)/shard_map/all_to_all | solution.py:279
  81.4 121.1 %all-gather.23.cloned.1.call-start = ((), (), s32[]{:S(2)}) async-start(), calls=%async_computation.24 | async-start | bytes 4456448 | tf_op jit(solution)/shard_map/all_gather | solution.py:234
  82.7 87.1 %copy-start.148 = (f32[128,128]{1,0:T(8,128)}, f32[128,128]{1,0:T(8,128)S(1)}, u32[]{:S(2)}) copy-start(f32[128,128]{1,0:T(8,128)S(1)} %fusion.329) | copy-start | bytes 196612
  83.6 69.7 %copy-start.161 = (f32[2,512]{1,0:T(2,128)}, f32[2,512]{1,0:T(2,128)S(1)}, u32[]{:S(2)}) copy-start(f32[2,512]{1,0:T(2,128)S(1)} %get-tuple-element.330) | copy-start | bytes 12292
  84.6 68.8 %copy-start.163 = (f32[2,512]{1,0:T(2,128)}, f32[2,512]{1,0:T(2,128)S(1)}, u32[]{:S(2)}) copy-start(f32[2,512]{1,0:T(2,128)S(1)} %get-tuple-element.365) | copy-start | bytes 12292
  84.6 68.8 %copy-start.165 = (f32[2,512]{1,0:T(2,128)}, f32[2,512]{1,0:T(2,128)S(1)}, u32[]{:S(2)}) copy-start(f32[2,512]{1,0:T(2,128)S(1)} %get-tuple-element.366) | copy-start | bytes 12292
  85.3 68.1 %copy-start.221 = (f32[128]{0:T(128)}, f32[128]{0:T(128)S(1)}, u32[]{:S(2)}) copy-start(f32[128]{0:T(128)S(1)} %get-tuple-element.377) | copy-start | bytes 1540
  85.3 68.1 %copy-start.223 = (f32[128]{0:T(128)}, f32[128]{0:T(128)S(1)}, u32[]{:S(2)}) copy-start(f32[128]{0:T(128)S(1)} %get-tuple-element.378) | copy-start | bytes 1540
  85.3 68.1 %copy-start.225 = (f32[128]{0:T(128)}, f32[128]{0:T(128)S(1)}, u32[]{:S(2)}) copy-start(f32[128]{0:T(128)S(1)} %get-tuple-element.379) | copy-start | bytes 1540
  85.3 68.1 %copy-start.227 = (f32[128]{0:T(128)}, f32[128]{0:T(128)S(1)}, u32[]{:S(2)}) copy-start(f32[128]{0:T(128)S(1)} %get-tuple-element.380) | copy-start | bytes 1540
  111.6 10.3 all-to-all-start.3
  127.2 10.9 all-to-all-start.2
  138.1 12.3 all-to-all-start.1
  142.6 151.5 %all-gather.35.cloned.1.call-start = ((), (), s32[]{:S(2)}) async-start(), calls=%async_computation.38 | async-start | bytes 2228224 | tf_op jit(solution)/shard_map/all_gather | solution.py:21
  143.8 8.7 collective-permute-start.1
  151.2 2.1 collective-permute-start
  173.7 78.0 %copy-start.40 = (f32[2,1,4,128,128]{4,3,2,0,1:T(8,128)}, f32[2,1,4,128,128]{4,3,2,0,1:T(8,128)S(1)}, u32[]{:S(2)}) copy-start(f32[2,1,4,128,128]{4,3,2,0,1:T(8,128)S(1)} %convolution_bitcast_fusion.32) | copy-start | bytes 1572868
  202.4 135.9 %all-gather.37.cloned.1.call-start = ((), (), s32[]{:S(2)}) async-start(), calls=%async_computation.39 | async-start | bytes 4456448 | tf_op jit(solution)/shard_map/all_gather | solution.py:21
  233.4 2.2 collective-permute-start.2
  277.5 122.9 %all-gather.25.cloned.1.call-start = ((), (), s32[]{:S(2)}) async-start(), calls=%async_computation.25 | async-start | bytes 4456448 | tf_op jit(solution)/shard_map/all_gather | solution.py:237
  278.1 185.7 %all-gather.33.cloned.1.call-start = ((), (), s32[]{:S(2)}) async-start(), calls=%async_computation.29 | async-start | bytes 6127616 | tf_op jit(solution)/shard_map/all_gather | solution.py:241
  278.8 242.2 %all-gather.27.cloned.1.call-start = ((), (), s32[]{:S(2)}) async-start(), calls=%async_computation.26 | async-start | bytes 4456448 | tf_op jit(solution)/shard_map/all_gather | solution.py:238
  279.6 304.7 %all-gather.31.cloned.1.call-start = ((), (), s32[]{:S(2)}) async-start(), calls=%async_computation.28 | async-start | bytes 6127616 | tf_op jit(solution)/shard_map/all_gather | solution.py:240
  280.3 366.9 %all-gather.29.cloned.1.call-start = ((), (), s32[]{:S(2)}) async-start(), calls=%async_computation.27 | async-start | bytes 6127616 | tf_op jit(solution)/shard_map/all_gather | solution.py:239
  280.9 439.4 %all-gather.39.cloned.1.call-start = ((), (), s32[]{:S(2)}) async-start(), calls=%async_computation.40 | async-start | bytes 1114112 | tf_op jit(solution)/shard_map/all_gather | solution.py:37
  348.7 120.9 %all-to-all-start.5 = ((bf16[2,512,256]{2,0,1:T(2,128)(2,1)}), bf16[2,512,256]{2,0,1:T(2,128)(2,1)}, u32[]{:S(2)}, u32[]{:S(2)}) async-start(bf16[2,512,256]{2,0,1:T(2,128)(2,1)} %copy.567), calls=%async_computation.5 | async-start | bytes 1048576 | tf_op jit(solution)/shard_map/all_to_all | solution.py:323
  354.6 405.7 %all-gather.41.cloned.1.call-start = ((), (), s32[]{:S(2)}) async-start(), calls=%async_computation.41 | async-start | bytes 2228224 | tf_op jit(solution)/shard_map/all_gather | solution.py:37
  525.4 121.9 %copy-start.86 = (bf16[2,64,1024]{2,1,0:T(8,128)(2,1)}, bf16[2,64,1024]{2,1,0:T(8,128)(2,1)S(1)}, u32[]{:S(2)}) copy-start(bf16[2,64,1024]{2,1,0:T(8,128)(2,1)S(1)} %multiply_convert_fusion.3) | copy-start | bytes 786436
  928.0 12.0 all-to-all-start.11
  940.0 11.8 all-to-all-start.10
  945.6 161.9 %reduce-scatter.33.cloned.1.call-start = ((), (), s32[]{:S(2)}) async-start(), calls=%async_computation.43 | async-start | bytes 278528
  954.2 154.1 %reduce-scatter.31.cloned.1.call-start = ((), (), s32[]{:S(2)}) async-start(), calls=%async_computation.42 | async-start | bytes 278528
  955.3 210.4 %reduce-scatter.23.cloned.1.call-start = ((), (), s32[]{:S(2)}) async-start(), calls=%async_computation.34 | async-start | bytes 4456448 | tf_op jit(solution)/shard_map/reduce_scatter | solution.py:471
  959.9 289.5 %reduce-scatter.21.cloned.1.call-start = ((), (), s32[]{:S(2)}) async-start(), calls=%async_computation.33 | async-start | bytes 4456448 | tf_op jit(solution)/shard_map/reduce_scatter | solution.py:465
  966.4 356.7 %reduce-scatter.15.cloned.1.call-start = ((), (), s32[]{:S(2)}) async-start(), calls=%async_computation.30 | async-start | bytes 2228224 | tf_op jit(solution)/shard_map/reduce_scatter | solution.py:438
  983.9 3.1 collective-permute-start.3
  1005.8 391.1 %reduce-scatter.17.cloned.1.call-start = ((), (), s32[]{:S(2)}) async-start(), calls=%async_computation.31 | async-start | bytes 2228224 | tf_op jit(solution)/shard_map/reduce_scatter | solution.py:444
  1005.9 3.1 collective-permute-start.4
  1024.6 462.4 %reduce-scatter.25.cloned.1.call-start = ((), (), s32[]{:S(2)}) async-start(), calls=%async_computation.35 | async-start | bytes 6127616 | tf_op jit(solution)/shard_map/reduce_scatter | solution.py:477
  1028.9 547.9 %reduce-scatter.27.cloned.1.call-start = ((), (), s32[]{:S(2)}) async-start(), calls=%async_computation.36 | async-start | bytes 6127616 | tf_op jit(solution)/shard_map/reduce_scatter | solution.py:483
  1034.1 632.6 %reduce-scatter.29.cloned.1.call-start = ((), (), s32[]{:S(2)}) async-start(), calls=%async_computation.37 | async-start | bytes 6127616 | tf_op jit(solution)/shard_map/reduce_scatter | solution.py:489
  1039.5 710.6 %reduce-scatter.19.cloned.1.call-start = ((), (), s32[]{:S(2)}) async-start(), calls=%async_computation.32 | async-start | bytes 4456448 | tf_op jit(solution)/shard_map/reduce_scatter | solution.py:447
  1043.3 3.1 collective-permute-start.5
  1066.0 798.3 %all-reduce.78.cloned.1.call-start = ((), (), s32[]{:S(2)}) async-start(), calls=%async_computation.44 | async-start | bytes 4259840 | tf_op jit(solution)/shard_map/psum | solution.py:506
  1071.7 678.4 %copy-start.79 = (bf16[1024,1024]{1,0:T(8,128)(2,1)S(1)}, bf16[1024,1024]{1,0:T(8,128)(2,1)}, u32[]{:S(2)}) copy-start(bf16[1024,1024]{1,0:T(8,128)(2,1)} %all-gather.21.cloned.1.call-done) | copy-start | bytes 6291460
  (231 other events, 1294.2 us)
Sparse Core Ops, SparseCore 0:
  10.5 49.7 all-gather.20
  62.7 47.2 all-gather.18
  112.5 54.9 all-gather.22
  202.6 49.8 all-gather.34
  277.6 60.6 all-gather.36
  340.6 59.7 all-gather.24
  402.8 60.8 all-gather.32
  466.2 54.7 all-gather.26
  523.4 60.7 all-gather.30
  586.5 60.6 all-gather.28
  649.7 46.2 all-gather.38
  713.0 47.3 all-gather.40
  954.3 59.5 reduce-scatter.32
  1018.5 63.9 reduce-scatter.30
  1086.4 79.2 reduce-scatter.22
  1170.2 79.2 reduce-scatter.20
  1253.3 69.8 reduce-scatter.14
  1326.9 69.9 reduce-scatter.16
  1401.0 85.9 reduce-scatter.24
  1491.0 85.8 reduce-scatter.26
  1580.9 85.8 reduce-scatter.28
  1670.8 79.1 reduce-scatter.18
  1753.5 110.7 all-reduce.77
where the time goes:
time: 1890 us; the launch traced here: 1880 us
  waiting for transfers between devices  1070 us (57%)
  blocking collectives  233 us (12%)
  matrix products  232 us (12%)
  local copies, waits for them, and re-layouts  191 us (10%)
  other arithmetic  86.4 us (5%)
  starting transfers between devices  48.4 us (3%)
  between operations  22.8 us (1%)
    reduce_scatter x1, waiting for transfers between devices, on_device(): lax.psum_scatter(weight_grad(ffn_in, grad_gate_low).astype(jnp.bfloat16),...  90.1 us
    reduce_scatter x1, waiting for transfers between devices, on_device(): lax.psum_scatter(weight_grad(inner_act, cotangent).astype(jnp.bfloat16),...  90 us
    reduce_scatter x1, waiting for transfers between devices, on_device(): lax.psum_scatter(weight_grad(ffn_in, grad_up_low).astype(jnp.bfloat16), '...  89.8 us
    pad x22, local copies, waits for them, and re-layouts, block_maps(): maps = lax.associative_scan(compose_local, (step_map, folded_value))  87.8 us
    reduce_scatter x1, waiting for transfers between devices, on_device(): lax.psum_scatter(weight_grad(normed, grad_gate_pre_low).astype(jnp.bfloat...  83.7 us
    reduce_scatter x1, waiting for transfers between devices, on_device(): lax.psum_scatter(weight_grad(normed, tok_value).astype(jnp.bfloat16), 'cp...  83.3 us
    reduce_scatter x1, waiting for transfers between devices, on_device(): lax.psum_scatter(weight_grad(normed, tok_key).astype(jnp.bfloat16), 'cp',...  73.8 us
    reduce_scatter x1, waiting for transfers between devices, on_device(): lax.psum_scatter(weight_grad(normed, tok_query).astype(jnp.bfloat16), 'cp...  73.7 us
  transfers between devices with their start and end apart: 36, of which 26 were waited for; matrix products, arithmetic and copies ran while one was open for 17% of the time, Pallas kernels for 0%

commit v1 on v0

v1 whole, which is shorter than its diff:
```python
import jax
import jax.numpy as jnp
from jax import lax
from jax.experimental import pallas as pl
from jax.experimental.pallas import tpu as pltpu
from jax.sharding import PartitionSpec as P

STRETCH = 64
LANES = 128
HIGHEST = lax.Precision.HIGHEST
EPSILON = 1e-06
bf16, f32 = jnp.bfloat16, jnp.float32
VMEM_LIMIT = 48 * 1024 * 1024


def mm(a, b, ca=1, cb=0):
    return lax.dot_general(
        a, b, (((ca,), (cb,)), ((), ())), precision=HIGHEST, preferred_element_type=f32
    )


def lower_strict():
    rows = lax.broadcasted_iota(jnp.int32, (STRETCH, STRETCH), 0)
    cols = lax.broadcasted_iota(jnp.int32, (STRETCH, STRETCH), 1)
    return (rows > cols).astype(f32), (rows == cols).astype(f32)


def block_rows(n):
    return pl.ds(pl.multiple_of(n * STRETCH, STRETCH), STRETCH)


def maps_kernel(k_ref, v_ref, aux_ref, between_ref, x_ref, end_ref, w_ref, u_ref, inv_ref):
    sequences, length, dk = k_ref.shape
    dv = v_ref.shape[2]
    blocks = length // STRETCH
    strict, unit = lower_strict()

    def prepare_block(n, carry):
        rows = block_rows(n)
        for s in range(sequences):
            k = k_ref[s, rows]
            beta = aux_ref[s, rows, 0:1]
            gamma = aux_ref[s, rows, 1:2]
            power = -beta * (between_ref[s, n] * strict) * mm(k, k, 1, 1)
            inverse = unit + power
            for level in range(STRETCH.bit_length() - 2):
                power = mm(power, power)
                inverse = inverse + mm(inverse, power)
            inv_ref[s, n] = inverse
            w_ref[s, rows] = mm(inverse, beta * gamma * k)
            u_ref[s, rows] = mm(inverse, beta * v_ref[s, rows])
        return carry

    lax.fori_loop(0, blocks, prepare_block, 0)

    wide = (dk, dk + dv)
    start = (
        lax.broadcasted_iota(jnp.int32, wide, 0) == lax.broadcasted_iota(jnp.int32, wide, 1)
    ).astype(f32)

    def chain_block(n, states):
        rows = block_rows(n)
        after = []
        for s in range(sequences):
            x = states[s]
            x_ref[s, n] = x
            gone = mm(w_ref[s, rows], x)
            update = jnp.concatenate([-gone[:, :dk], u_ref[s, rows] - gone[:, dk:]], 1)
            rho = aux_ref[s, rows, 2:3]
            last = aux_ref[s, rows, 1:2][STRETCH - 1 :]
            after.append(last * x + mm(k_ref[s, rows], rho * update, 0, 0))
        return tuple(after)

    ends = lax.fori_loop(0, blocks, chain_block, (start,) * sequences)
    for s in range(sequences):
        end_ref[s] = ends[s].astype(end_ref.dtype)


def run_kernel(
    place_ref, maps_ref, x_ref, q_ref, k_ref, aux_ref, between_ref, w_ref, u_ref,
    out_ref, state_ref, update_ref,
):
    sequences, length, dk = k_ref.shape
    dv = u_ref.shape[2]
    blocks = length // STRETCH

    def enter(hop, states):
        return tuple(
            mm(maps_ref[hop, s, :, :dk].astype(f32), states[s])
            + maps_ref[hop, s, :, dk:].astype(f32)
            for s in range(sequences)
        )

    entry = lax.fori_loop(
        0, place_ref[0], enter, (jnp.zeros((dk, dv), f32),) * sequences
    )

    def run_block(n, carry):
        rows = block_rows(n)
        for s in range(sequences):
            q, k = q_ref[s, rows], k_ref[s, rows]
            state = mm(x_ref[s, n, :, :dk], entry[s]) + x_ref[s, n, :, dk:]
            update = u_ref[s, rows] - mm(w_ref[s, rows], state)
            scores = mm(q, k, 1, 1) * between_ref[s, n]
            out = aux_ref[s, rows, 1:2] * mm(q, state) + mm(scores, update)
            state_ref[s, n] = state
            update_ref[s, rows] = update
            out_ref[s, rows] = out.astype(out_ref.dtype)
        return carry

    lax.fori_loop(0, blocks, run_block, 0)


def back_local_kernel(
    q_ref, k_ref, aux_ref, between_ref, w_ref, grad_ref, through_ref, inflow_ref, local_ref
):
    sequences, length, dk = k_ref.shape
    dv = grad_ref.shape[2]
    blocks = length // STRETCH

    def prepare_block(n, carry):
        rows = block_rows(n)
        for s in range(sequences):
            q, k = q_ref[s, rows], k_ref[s, rows]
            grad = grad_ref[s, rows].astype(f32)
            scores = mm(q, k, 1, 1) * between_ref[s, n]
            through_ref[s, rows] = mm(scores, grad, 0, 0)
            inflow_ref[s, n] = mm(q, aux_ref[s, rows, 1:2] * grad, 0, 0)
        return carry

    lax.fori_loop(0, blocks, prepare_block, 0)

    def chain_block(back, states):
        n = blocks - 1 - back
        rows = block_rows(n)
        after = []
        for s in range(sequences):
            rho = aux_ref[s, rows, 2:3]
            last = aux_ref[s, rows, 1:2][STRETCH - 1 :]
            grad_update = through_ref[s, rows] + rho * mm(k_ref[s, rows], states[s])
            after.append(
                last * states[s] + inflow_ref[s, n] - mm(w_ref[s, rows], grad_update, 0, 0)
            )
        return tuple(after)

    ends = lax.fori_loop(0, blocks, chain_block, (jnp.zeros((dk, dv), f32),) * sequences)
    for s in range(sequences):
        local_ref[s] = ends[s].astype(local_ref.dtype)


def back_kernel(
    place_ref, maps_ref, locals_ref, q_ref, k_ref, v_ref, aux_ref, between_ref, w_ref, inv_ref,
    state_ref, update_ref, grad_ref, through_ref, inflow_ref,
    grad_q_ref, grad_k_ref, grad_v_ref, grad_aux_ref, grad_row_ref,
):
    sequences, length, dk = k_ref.shape
    dv = v_ref.shape[2]
    blocks = length // STRETCH
    segments = maps_ref.shape[0]
    strict, _ = lower_strict()
    at_last = lax.broadcasted_iota(jnp.int32, (STRETCH, 1), 0) == STRETCH - 1
    lane = lax.broadcasted_iota(jnp.int32, (STRETCH, grad_aux_ref.shape[2]), 1)

    def leave(hop, states):
        source = segments - 1 - hop
        return tuple(
            mm(maps_ref[source, s, :, :dk].astype(f32), states[s], 0, 0)
            + locals_ref[source, s].astype(f32)
            for s in range(sequences)
        )

    exits = lax.fori_loop(
        0, segments - 1 - place_ref[0], leave, (jnp.zeros((dk, dv), f32),) * sequences
    )

    def row_sum(a):
        return jnp.sum(a, axis=1, keepdims=True)

    def chain_block(back, states):
        n = blocks - 1 - back
        rows = block_rows(n)
        after = []
        for s in range(sequences):
            grad_next = states[s]
            q, k, v = q_ref[s, rows], k_ref[s, rows], v_ref[s, rows]
            beta, gamma, rho = (aux_ref[s, rows, c : c + 1] for c in range(3))
            last = gamma[STRETCH - 1 :]
            between = between_ref[s, n]
            state, update = state_ref[s, n], update_ref[s, rows]
            grad = grad_ref[s, rows].astype(f32)
            key_next = mm(k, grad_next)
            grad_update = through_ref[s, rows] + rho * key_next
            after.append(last * grad_next + inflow_ref[s, n] - mm(w_ref[s, rows], grad_update, 0, 0))
            grad_target = mm(inv_ref[s, n], grad_update, 0, 0)
            key_state, query_state = mm(k, state), mm(q, state)
            key_key, query_key = mm(k, k, 1, 1), mm(q, k, 1, 1)
            grad_query_key = mm(grad, update, 1, 1) * between
            grad_system = -mm(grad_target, update, 1, 1) * strict * between
            grad_key_key = beta * grad_system
            grad_key_state = -(beta * gamma) * grad_target
            grad_q_ref[s, rows] = gamma * mm(grad, state, 1, 1) + mm(grad_query_key, k)
            grad_k_ref[s, rows] = (
                mm(grad_query_key, q, 0, 0)
                + mm(rho * update, grad_next, 1, 1)
                + mm(grad_key_key, k)
                + mm(grad_key_key, k, 0, 0)
                + mm(grad_key_state, state, 1, 1)
            )
            grad_v_ref[s, rows] = beta * grad_target
            grad_beta = row_sum(grad_system * key_key) + row_sum(
                grad_target * (v - gamma * key_state)
            )
            grad_gamma = row_sum(grad * query_state) - beta * row_sum(grad_target * key_state)
            spread = grad_query_key * query_key + grad_key_key * key_key
            grad_rho = row_sum(key_next * update) * rho
            at_end = jnp.sum(grad_rho) + jnp.sum(row_sum(state * grad_next) * last)
            grad_cumulative = (
                row_sum(spread) + grad_gamma * gamma - grad_rho + jnp.where(at_last, at_end, 0.0)
            )
            grad_row_ref[s, pl.ds(n, 1)] = jnp.sum(spread, axis=0, keepdims=True)
            grad_aux_ref[s, rows] = jnp.where(lane == 0, grad_beta, grad_cumulative)
        return tuple(after)

    lax.fori_loop(0, blocks, chain_block, exits)


def kernel_call(body, out_shape, *operands, scalars=0):
    whole = pl.BlockSpec(memory_space=pltpu.VMEM)
    return pl.pallas_call(
        body,
        out_shape=out_shape,
        in_specs=[pl.BlockSpec(memory_space=pltpu.SMEM)] * scalars
        + [whole] * (len(operands) - scalars),
        out_specs=jax.tree.map(lambda _: whole, out_shape),
        compiler_params=pltpu.CompilerParams(vmem_limit_bytes=VMEM_LIMIT),
    )(*operands)


def shaped(shape, kind=f32):
    return jax.ShapeDtypeStruct(shape, kind)


def norm_gain(source, gain_vec):
    return source * lax.rsqrt(jnp.mean(source * source, -1, keepdims=True) + EPSILON) * gain_vec


def unit_rows(source):
    return source * lax.rsqrt(jnp.sum(source * source, -1, keepdims=True) + EPSILON)


def gated_norm(mixed_head, gate_pre, gain_vec):
    scale = lax.rsqrt(jnp.mean(mixed_head * mixed_head, -1, keepdims=True) + EPSILON)
    return mixed_head * scale * gain_vec * jax.nn.silu(gate_pre)


def conv_core(padded, weight, doc_pad):
    tap_count = weight.shape[0]
    length = padded.shape[1] - (tap_count - 1)
    current = doc_pad[:, tap_count - 1 :]
    summed = jnp.zeros((padded.shape[0], length, padded.shape[2]), f32)
    for offset in range(tap_count):
        first_row = tap_count - 1 - offset
        window = padded[:, first_row : first_row + length]
        same_doc = (doc_pad[:, first_row : first_row + length] == current).astype(f32)
        summed = summed + weight[offset] * window * same_doc[:, :, None]
    return jax.nn.silu(summed)


def prepare(packed_ext, decay_head, beta_head, taps, decay_log, decay_bias, doc_ext, dk):
    mixed = conv_core(packed_ext, taps, doc_ext)
    queries = unit_rows(mixed[:, :, :dk]) * dk ** (-0.5)
    key_rows = unit_rows(mixed[:, :, dk : 2 * dk])
    values = mixed[:, :, 2 * dk :]
    beta_rows = jax.nn.sigmoid(beta_head)
    decays = -jnp.exp(decay_log) * jax.nn.softplus(decay_head + decay_bias)
    sequences, length = decays.shape
    cumulative = jnp.cumsum(decays.reshape(sequences, length // STRETCH, STRETCH), -1)
    return queries, key_rows, values, beta_rows, cumulative


def block_gates(cumulative, doc_blocks, doc_starts):
    places = jnp.arange(STRETCH)
    linked = (places[:, None] >= places[None, :]) & (
        doc_blocks[..., :, None] == doc_blocks[..., None, :]
    )
    apart = cumulative[..., :, None] - cumulative[..., None, :]
    between = jnp.where(linked, jnp.exp(jnp.where(linked, apart, 0.0)), 0.0)
    survive = jnp.exp(cumulative) * (doc_blocks == doc_starts[..., None]).astype(f32)
    return survive, between, between[..., -1, :]


def each_peer(axis, action):
    count, me = lax.axis_size(axis), lax.axis_index(axis)

    def step(distance, carry):
        action(distance, lax.rem(me + distance, count), lax.rem(me + count - distance, count))
        return carry

    lax.fori_loop(1, count, step, 0)


def owner_targets(action):
    hd, me, head = lax.axis_size("hd"), lax.axis_index("cp"), lax.axis_index("hd")
    cp = lax.axis_size("cp")
    share = cp // hd

    def step(turn, carry):
        piece = lax.rem(turn + me, cp)
        to = (share * head + piece // hd, lax.rem(piece, hd))
        action(piece, to, (to[0] == me) & (to[1] == head))
        return carry

    lax.fori_loop(0, cp, step, 0)


def owner_sources(action):
    hd, me, head = lax.axis_size("hd"), lax.axis_index("cp"), lax.axis_index("hd")
    cp = lax.axis_size("cp")
    column = me // (cp // hd)

    def step(source, carry):
        action(source, (source, column), (source == me) & (column == head))
        return carry

    lax.fori_loop(0, cp, step, 0)


def meet(axes, owners=False):
    barrier = pltpu.get_barrier_semaphore()
    total = 0
    for axis in axes:
        each_peer(
            axis,
            lambda _, to, source, axis=axis: pl.semaphore_signal(
                barrier, inc=1, device_id={axis: to}, device_id_type=pl.DeviceIdType.MESH
            ),
        )
        total += lax.axis_size(axis) - 1
    if owners:
        cp, hd = lax.axis_size("cp"), lax.axis_size("hd")

        def greet(source, at, own):
            @pl.when(jnp.logical_not(own))
            def _():
                pl.semaphore_signal(
                    barrier, inc=1, device_id=at, device_id_type=pl.DeviceIdType.MESH
                )

        owner_sources(greet)
        alone = lax.axis_index("cp") // (cp // hd) == lax.axis_index("hd")
        total = total + cp - alone.astype(jnp.int32)
    pl.semaphore_wait(barrier, total)


def remote(src, dst, send, recv, target):
    return pltpu.make_async_remote_copy(
        src_ref=src,
        dst_ref=dst,
        send_sem=send,
        recv_sem=recv,
        device_id=target,
        device_id_type=pl.DeviceIdType.MESH,
    )


class Exchange:
    def __init__(self, axis, source, landing, send, recv, local):
        self.axis, self.source, self.landing = axis, source, landing
        self.send, self.recv = send, recv
        me = lax.axis_index(axis)
        self.own = pltpu.make_async_copy(source(me), landing(me), local)

    def copy(self, distance, block, place, to):
        return remote(
            block, place, self.send.at[distance], self.recv.at[distance], {self.axis: to}
        )

    def start(self):
        me = lax.axis_index(self.axis)
        each_peer(
            self.axis,
            lambda distance, to, source: self.copy(
                distance, self.source(to), self.landing(me), to
            ).start(),
        )
        self.own.start()

    def arrive(self):
        each_peer(
            self.axis,
            lambda distance, to, source: self.copy(
                distance, self.source(to), self.landing(source), to
            ).wait_recv(),
        )
        self.own.wait()

    def leave(self):
        each_peer(
            self.axis,
            lambda distance, to, source: self.copy(
                distance, self.source(to), self.landing(source), to
            ).wait_send(),
        )


class OwnerExchange:
    def __init__(self, source, landing, send, recv, local):
        self.source, self.landing = source, landing
        self.send, self.recv, self.local = send, recv, local

    def start(self):
        me = lax.axis_index("cp")

        def go(piece, to, own):
            @pl.when(own)
            def _():
                pltpu.make_async_copy(self.source(piece), self.landing(me), self.local).start()

            @pl.when(jnp.logical_not(own))
            def _():
                remote(
                    self.source(piece), self.landing(me), self.send.at[piece], self.recv.at[me], to
                ).start()

        owner_targets(go)

    def arrive(self):
        def get(source, at, own):
            @pl.when(own)
            def _():
                pltpu.make_async_copy(
                    self.source(source), self.landing(source), self.local
                ).wait()

            @pl.when(jnp.logical_not(own))
            def _():
                remote(
                    self.source(source),
                    self.landing(source),
                    self.send.at[source],
                    self.recv.at[source],
                    at,
                ).wait_recv()

        owner_sources(get)

    def leave(self):
        def done(piece, to, own):
            @pl.when(jnp.logical_not(own))
            def _():
                remote(
                    self.source(piece), self.landing(piece), self.send.at[piece],
                    self.recv.at[piece], to,
                ).wait_send()

        owner_targets(done)


def sems(*counts):
    found = []
    for count in counts:
        found += [pltpu.SemaphoreType.DMA((count,))] * 2 + [pltpu.SemaphoreType.DMA]
    return found


def token_rows(ref, index, tokens):
    return ref.at[:, pl.ds(pl.multiple_of(index * tokens, tokens), tokens)]


def lead_rows(ref, index, rows):
    return ref.at[pl.ds(pl.multiple_of(index * rows, rows), rows)]


def comm_call(body, out_shape, places, operands, spots, scratch, number):
    kinds = {"any": pl.ANY, "vmem": pltpu.VMEM}
    return pl.pallas_call(
        body,
        out_shape=out_shape,
        in_specs=[pl.BlockSpec(memory_space=kinds[k]) for k in places],
        out_specs=tuple(pl.BlockSpec(memory_space=kinds[k]) for k in spots),
        scratch_shapes=scratch,
        compiler_params=pltpu.CompilerParams(
            collective_id=number, has_side_effects=True, vmem_limit_bytes=VMEM_LIMIT
        ),
    )(*operands)


def open_kernel(hidden_ref, front_ref, hidden_all_ref, front_all_ref, *flags):
    tokens, shard = hidden_ref.shape[1], front_ref.shape[0]
    meet(("hd", "cp"))
    moves = (
        Exchange(
            "hd", lambda to: hidden_ref, lambda at: token_rows(hidden_all_ref, at, tokens), *flags[:3]
        ),
        Exchange(
            "cp", lambda to: front_ref, lambda at: lead_rows(front_all_ref, at, shard), *flags[3:6]
        ),
    )
    for move in moves:
        move.start()
    for move in moves:
        move.arrive()
        move.leave()


def stack_kernel(part_ref, all_ref, *flags):
    meet(("cp",))
    move = Exchange("cp", lambda to: part_ref, lambda at: all_ref.at[at], *flags)
    move.start()
    move.arrive()
    move.leave()


def gather_stack(part, number):
    cp = lax.axis_size("cp")
    return comm_call(
        stack_kernel, (shaped((cp, *part.shape), part.dtype),), ("any",), (part,), ("any",),
        sems(cp), number,
    )[0]


def added(landed_ref):
    total = landed_ref[0].astype(f32)
    for index in range(1, landed_ref.shape[0]):
        total += landed_ref[index].astype(f32)
    return total


def spread_own(own_ref, all_ref, tokens, flags):
    move = Exchange("hd", lambda to: own_ref, lambda at: token_rows(all_ref, at, tokens), *flags)
    move.start()
    return move


def middle_kernel(
    partial_ref, hidden_ref, gain_ref, middle_ref, ffn_all_ref, landed_ref, own_ref, *flags
):
    tokens = hidden_ref.shape[1]
    meet(("hd",))
    move = Exchange(
        "hd", lambda to: token_rows(partial_ref, to, tokens), lambda at: landed_ref.at[at], *flags[:3]
    )
    move.start()
    move.arrive()
    middle = hidden_ref[...].astype(f32) + added(landed_ref)
    middle_ref[...] = middle
    own_ref[...] = norm_gain(middle, gain_ref[...]).astype(bf16)
    after = spread_own(own_ref, ffn_all_ref, tokens, flags[3:6])
    move.leave()
    after.arrive()
    after.leave()


def norm_back(source, gain_vec, grad):
    scale = lax.rsqrt(jnp.mean(source * source, -1, keepdims=True) + EPSILON)
    lifted = grad * gain_vec
    mixed = jnp.mean(source * lifted, -1, keepdims=True)
    return scale * lifted - source * (scale * scale * scale) * mixed, source * scale * grad


def ffn_back_kernel(
    out_part_ref, grad_part_ref, middle_ref, cot_ref, gain_ref,
    block_ref, grad_middle_ref, grad_gain_ref, grad_all_ref,
    out_landed_ref, grad_landed_ref, own_ref, *flags
):
    tokens = middle_ref.shape[1]
    meet(("hd",))
    moves = [
        Exchange(
            "hd",
            lambda to, ref=ref: token_rows(ref, to, tokens),
            lambda at, landed=landed: landed.at[at],
            *flags[3 * n : 3 * n + 3],
        )
        for n, (ref, landed) in enumerate(
            ((grad_part_ref, grad_landed_ref), (out_part_ref, out_landed_ref))
        )
    ]
    for move in moves:
        move.start()
    moves[0].arrive()
    middle = middle_ref[...]
    back, gain_terms = norm_back(middle, gain_ref[...], added(grad_landed_ref))
    grad_middle = cot_ref[...].astype(f32) + back
    grad_middle_ref[...] = grad_middle
    own_ref[...] = grad_middle.astype(bf16)
    after = spread_own(own_ref, grad_all_ref, tokens, flags[6:9])
    grad_gain_ref[...] = jnp.sum(jnp.sum(gain_terms, axis=0), axis=0, keepdims=True)
    moves[1].arrive()
    block_ref[...] = (middle + added(out_landed_ref)).astype(bf16)
    for move in moves:
        move.leave()
    after.arrive()
    after.leave()


def close_kernel(
    normed_part_ref, front_ref, ffn_ref, output_ref, down_ref, small_ref,
    hidden_ref, grad_middle_ref, gain_ref,
    grad_in_ref, front_all_ref, ffn_all_ref, output_all_ref, down_all_ref, small_sum_ref,
    normed_landed, front_landed, ffn_landed, output_landed, down_landed, small_landed,
    front_own, ffn_own, output_own, down_own, *flags
):
    tokens = hidden_ref.shape[1]
    shard = front_own.shape[0]
    meet(("hd", "cp"), owners=True)

    def over_cp(ref, landed, flags):
        return Exchange("cp", lambda to: lead_rows(ref, to, shard), lambda at: landed.at[at], *flags)

    def to_owner(ref, landed, flags):
        return OwnerExchange(lambda piece: ref.at[piece], lambda at: landed.at[at], *flags)

    groups = [flags[3 * n : 3 * n + 3] for n in range(10)]
    normed_move = Exchange(
        "hd",
        lambda to: token_rows(normed_part_ref, to, tokens),
        lambda at: normed_landed.at[at],
        *groups[0],
    )
    weights = [
        (to_owner(down_ref, down_landed, groups[1]), down_landed, down_own, down_all_ref),
        (over_cp(ffn_ref, ffn_landed, groups[2]), ffn_landed, ffn_own, ffn_all_ref),
        (to_owner(output_ref, output_landed, groups[3]), output_landed, output_own, output_all_ref),
        (over_cp(front_ref, front_landed, groups[4]), front_landed, front_own, front_all_ref),
    ]
    small_move = Exchange(
        "cp", lambda to: small_ref, lambda at: small_landed.at[at], *groups[5]
    )
    normed_move.start()
    for move, _, _, _ in weights:
        move.start()
    small_move.start()
    spreads = []
    for n, (move, landed, own, everywhere) in enumerate(weights):
        move.arrive()
        own[...] = added(landed).astype(bf16)
        spread = Exchange(
            "hd",
            lambda to, own=own: own,
            lambda at, everywhere=everywhere: everywhere.at[at],
            *groups[6 + n],
        )
        spread.start()
        spreads.append(spread)
    normed_move.arrive()
    back, _ = norm_back(hidden_ref[...].astype(f32), gain_ref[...], added(normed_landed))
    grad_in_ref[...] = (grad_middle_ref[...] + back).astype(bf16)
    small_move.arrive()
    small_sum_ref[...] = added(small_landed)
    for move in (normed_move, small_move, *(entry[0] for entry in weights)):
        move.leave()
    for spread in spreads:
        spread.arrive()
        spread.leave()


def passed_along(block, axis, distance):
    devices = range(lax.axis_size(axis))
    route = [(i - distance, i) for i in devices if i - distance in devices]
    return lax.ppermute(block, axis, route)


def head_rows(shard, place):
    cp, hd = lax.axis_size("cp"), lax.axis_size("hd")
    share = cp // hd
    got = []
    for turn in range(share):
        route = [
            (i * hd + j, (share * j + (turn + i) % share) * hd + i // share)
            for i in range(cp)
            for j in range(hd)
        ]
        got.append(lax.ppermute(shard, ("cp", "hd"), route))
    stack = jnp.stack(got)
    order = (place - jnp.arange(share)) % share
    return jnp.take(stack, order, axis=0).reshape(share * shard.shape[0], shard.shape[1])


def on_device(
    hidden_in, doc_ids, w_query, w_key, w_value, w_decay, w_beta, w_gate_out, w_output,
    w_ffn_gate, w_ffn_up, w_ffn_down, conv_query, conv_key, conv_value, decay_log, decay_bias,
    gain_attn, gain_ffn, gain_head, cotangent,
):
    place, head = lax.axis_index("cp"), lax.axis_index("hd")
    cp, hd = lax.axis_size("cp"), lax.axis_size("hd")
    sequences, tokens, width = hidden_in.shape
    shard = w_query.shape[0]
    dk, dv = w_query.shape[1] // hd, w_value.shape[1] // hd
    ff = w_ffn_gate.shape[1] // hd
    ffp = -(-ff // LANES) * LANES
    qkv = 2 * dk + dv
    side = qkv + dv
    span = tokens * hd
    blocks = span // STRETCH

    def part(weight):
        cols = weight.shape[1] // hd
        return lax.dynamic_slice_in_dim(weight, head * cols, cols, 1)

    def ff_pad(weight):
        return jnp.pad(part(weight), ((0, 0), (0, ffp - ff)))

    head_share = gain_head.shape[0]
    side_cols = jnp.stack(
        [
            part(w_decay)[:, 0],
            part(w_beta)[:, 0],
            gain_attn,
            gain_ffn,
            jnp.pad(gain_head, (0, shard - head_share)),
        ],
        1,
    )
    front = jnp.concatenate(
        [
            part(w_query),
            part(w_key),
            part(w_value),
            part(w_gate_out),
            jnp.pad(side_cols, ((0, 0), (0, LANES - side_cols.shape[1]))),
        ],
        1,
    )
    hidden_all, front_full = comm_call(
        open_kernel,
        (shaped((sequences, span, width), bf16), shaped((width, front.shape[1]), bf16)),
        ("any", "any"),
        (hidden_in, front),
        ("any", "any"),
        sems(hd, cp),
        1,
    )
    output_part = head_rows(w_output, place)
    ffn_full = lax.all_gather(
        jnp.concatenate([ff_pad(w_ffn_gate), ff_pad(w_ffn_up)], 1), "cp", axis=0, tiled=True
    )
    down_part = jnp.pad(head_rows(w_ffn_down, place), ((0, ffp - ff), (0, 0)))
    cot_all = lax.all_gather(cotangent, "hd", axis=1, tiled=True)

    attn_gain = front_full[:, side + 2].astype(f32)
    ffn_gain = front_full[:, side + 3].astype(f32)
    head_gain = front_full[:, side + 4].reshape(cp, shard)[:, :head_share].reshape(-1).astype(f32)

    def dot(a, b, spec):
        return jnp.einsum(spec, a, b, preferred_element_type=f32)

    inputs_all = hidden_all.astype(f32)
    scale_all = lax.rsqrt(jnp.mean(inputs_all * inputs_all, -1, keepdims=True) + EPSILON)
    normed = (inputs_all * scale_all * attn_gain).astype(bf16)
    projected = dot(normed, front_full, "std,de->ste")
    packed = projected[:, :, :qkv].astype(bf16)
    gate_pre = projected[:, :, qkv:side]
    decay_head = projected[:, :, side].astype(bf16).astype(f32)
    beta_head = projected[:, :, side + 1].astype(bf16).astype(f32)

    margin = conv_query.shape[0] - 1
    rim = passed_along(packed[:, -margin:], "cp", 1)
    doc_pad = jnp.concatenate([jnp.full((sequences, margin), -1, jnp.int32), doc_ids], 1)
    doc_ext = lax.dynamic_slice_in_dim(doc_pad, place * span, span + margin, 1)
    doc_blocks = doc_ext[:, margin:].reshape(sequences, blocks, STRETCH)
    doc_starts = doc_ext[:, margin - 1 : -1].reshape(sequences, blocks, STRETCH)[:, :, 0]
    taps = jnp.concatenate([conv_query, conv_key, conv_value], 1).astype(f32)
    prepared, prepare_pull = jax.vjp(
        lambda *entries: prepare(*entries, doc_ext, dk),
        jnp.concatenate([rim, packed], 1).astype(f32),
        decay_head,
        beta_head,
        taps,
        decay_log.astype(f32),
        decay_bias.astype(f32),
    )
    queries, key_rows, values, beta_rows, cumulative = prepared
    survive, between, rho = block_gates(cumulative, doc_blocks, doc_starts)
    flat = (sequences, span)
    aux = jnp.stack([beta_rows, survive.reshape(flat), rho.reshape(flat)], -1)
    aux = jnp.pad(aux, ((0, 0), (0, 0), (0, 5)))
    prefix, segment, weighted, written, inverse = kernel_call(
        maps_kernel,
        (
            shaped((sequences, blocks, dk, dk + dv)),
            shaped((sequences, dk, dk + dv), bf16),
            shaped((sequences, span, dk)),
            shaped((sequences, span, dv)),
            shaped((sequences, blocks, STRETCH, STRETCH)),
        ),
        key_rows, values, aux, between,
    )
    segments = gather_stack(segment, 2)
    place_vec = place.reshape(1).astype(jnp.int32)
    mixed, states, updates = kernel_call(
        run_kernel,
        (
            shaped((sequences, span, dv), bf16),
            shaped((sequences, blocks, dk, dv)),
            shaped((sequences, span, dv)),
        ),
        place_vec, segments, prefix, queries, key_rows, aux, between, weighted, written,
        scalars=1,
    )
    mixed_float = mixed.astype(f32)
    normed_head, gated_pull = jax.vjp(gated_norm, mixed_float, gate_pre, head_gain)
    normed_head = normed_head.astype(bf16)
    landing = pltpu.VMEM((hd, sequences, tokens, width), bf16)
    own_tokens = pltpu.VMEM((sequences, tokens, width), bf16)
    ffn_gain = ffn_gain[None]
    middle, ffn_all = comm_call(
        middle_kernel,
        (shaped(hidden_in.shape), shaped((sequences, span, width), bf16)),
        ("any", "vmem", "vmem"),
        (dot(normed_head, output_part, "ste,ed->std").astype(bf16), hidden_in, ffn_gain),
        ("vmem", "any"),
        [landing, own_tokens, *sems(hd, hd)],
        4,
    )
    gate_up = dot(ffn_all, ffn_full, "std,df->stf")
    inner, swiglu_pull = jax.vjp(
        lambda both: jax.nn.silu(both[..., :ffp]) * both[..., ffp:], gate_up
    )
    inner = inner.astype(bf16)
    grad_inner = dot(cot_all, down_part, "std,fd->stf")
    grad_gate_up = swiglu_pull(grad_inner)[0].astype(bf16)
    block_out, grad_middle, grad_ffn_gain, grad_attention = comm_call(
        ffn_back_kernel,
        (
            shaped(hidden_in.shape, bf16),
            shaped(hidden_in.shape),
            shaped((1, width)),
            shaped((sequences, span, width), bf16),
        ),
        ("any", "any", "vmem", "vmem", "vmem"),
        (
            dot(inner, down_part, "stf,fd->std").astype(bf16),
            dot(grad_gate_up, ffn_full, "stf,df->std").astype(bf16),
            middle, cotangent, ffn_gain,
        ),
        ("vmem", "vmem", "vmem", "any"),
        [landing, landing, own_tokens, *sems(hd, hd, hd)],
        5,
    )

    def weight_grad(left_side, right_side):
        return dot(left_side, right_side, "std,ste->de")

    def pieces(grad):
        rows = grad.shape[0] // cp
        split = grad.reshape(cp, rows, width)
        return jnp.pad(split, ((0, 0), (0, -rows % 16), (0, 0))).astype(bf16)

    grad_ffn = weight_grad(ffn_all, grad_gate_up).astype(bf16)
    grad_down = pieces(weight_grad(inner, cot_all)[:ff])

    grad_normed_head = dot(grad_attention, output_part, "std,ed->ste")
    grad_output = pieces(weight_grad(normed_head, grad_attention))
    grad_mixed, grad_gate_pre, grad_head_gain = gated_pull(grad_normed_head)
    grad_mixed = grad_mixed.astype(bf16)
    through, inflow, local = kernel_call(
        back_local_kernel,
        (
            shaped((sequences, span, dv)),
            shaped((sequences, blocks, dk, dv)),
            shaped((sequences, dk, dv), bf16),
        ),
        queries, key_rows, aux, between, weighted, grad_mixed,
    )
    locals_all = gather_stack(local, 3)
    grad_q, grad_k, grad_v, grad_aux, grad_row = kernel_call(
        back_kernel,
        (
            shaped((sequences, span, dk)),
            shaped((sequences, span, dk)),
            shaped((sequences, span, dv)),
            shaped((sequences, span, 8)),
            shaped((sequences, blocks, STRETCH)),
        ),
        place_vec, segments, locals_all, queries, key_rows, values, aux, between, weighted,
        inverse, states, updates, grad_mixed, through, inflow,
        scalars=1,
    )
    grad_cumulative = grad_aux[:, :, 1].reshape(sequences, blocks, STRETCH) - grad_row
    grad_ext, grad_decay, grad_beta, grad_taps, grad_log, grad_bias = prepare_pull(
        (grad_q, grad_k, grad_v, grad_aux[:, :, 0], grad_cumulative)
    )
    back = passed_along(grad_ext[:, :margin], "cp", -1)
    grad_packed = grad_ext[:, margin:].at[:, -margin:].add(back).astype(bf16)
    grad_projected = jnp.concatenate(
        [
            grad_packed,
            grad_gate_pre.astype(bf16),
            jnp.pad(
                jnp.stack([grad_decay, grad_beta], -1).astype(bf16),
                ((0, 0), (0, 0), (0, LANES - 2)),
            ),
        ],
        -1,
    )
    partial_normed = dot(grad_projected, front_full, "ste,de->std")
    grad_attn_gain = jnp.sum(inputs_all * scale_all * partial_normed, (0, 1))
    grad_front = weight_grad(normed, grad_projected)
    spread_gain = jnp.pad(
        grad_head_gain.reshape(cp, head_share), ((0, 0), (0, shard - head_share))
    ).reshape(-1)
    gains = jnp.stack([grad_attn_gain, grad_ffn_gain[0], spread_gain], 1)
    grad_front = jnp.concatenate(
        [grad_front[:, : side + 2], gains, grad_front[:, side + 5 :]], 1
    )
    small = jnp.concatenate(
        [
            grad_taps,
            jnp.pad(jnp.stack([grad_log, grad_bias], 1), ((0, 0), (0, qkv - 2))),
        ],
        0,
    )
    small = jnp.pad(small, ((0, -small.shape[0] % 8), (0, 0)))
    weight_parts = (grad_front.astype(bf16), grad_ffn, grad_output, grad_down)
    shares = ((shard, grad_front.shape[1]), (shard, 2 * ffp), grad_output.shape[1:], grad_down.shape[1:])
    grad_in, grad_front, grad_ffn, grad_output, grad_down, small = comm_call(
        close_kernel,
        (shaped(hidden_in.shape, bf16), *(shaped((hd, *share), bf16) for share in shares), shaped(small.shape)),
        ("any",) * 6 + ("vmem",) * 3,
        (partial_normed.astype(bf16), *weight_parts, small, hidden_in, grad_middle, attn_gain[None]),
        ("vmem",) + ("any",) * 4 + ("vmem",),
        [
            landing,
            *(pltpu.VMEM((cp, *share), bf16) for share in shares),
            pltpu.VMEM((cp, *small.shape), f32),
            *(pltpu.VMEM(share, bf16) for share in shares),
            *sems(hd, cp, cp, cp, cp, cp, hd, hd, hd, hd),
        ],
        6,
    )

    def owned(grad, rows):
        return grad[:, : rows // hd].reshape(rows, width).astype(f32)

    taps_rows = margin + 1

    def columns(grad):
        return jnp.swapaxes(grad, 0, 1).reshape(grad.shape[1], -1).astype(f32)

    gain_sums = jnp.sum(grad_front[:, :, side + 2 : side + 5].astype(f32), 0)
    return (
        block_out,
        grad_in,
        columns(grad_front[:, :, :dk]),
        columns(grad_front[:, :, dk : 2 * dk]),
        columns(grad_front[:, :, 2 * dk : qkv]),
        columns(grad_front[:, :, side : side + 1]),
        columns(grad_front[:, :, side + 1 : side + 2]),
        columns(grad_front[:, :, qkv:side]),
        owned(grad_output, w_output.shape[0]),
        columns(grad_ffn[:, :, :ff]),
        columns(grad_ffn[:, :, ffp : ffp + ff]),
        owned(grad_down, w_ffn_down.shape[0]),
        small[:taps_rows, :dk],
        small[:taps_rows, dk : 2 * dk],
        small[:taps_rows, 2 * dk :],
        small[taps_rows, :1],
        small[taps_rows, 1:2],
        gain_sums[:, 0],
        gain_sums[:, 1],
        gain_sums[:head_share, 2],
    )


def solution(mesh):
    tokens, rows, cols = P(None, ("cp", "hd"), None), P("cp", None), P(None, "hd")
    weights = (rows,) * 10
    return jax.shard_map(
        on_device,
        mesh=mesh,
        in_specs=(tokens, P(), *weights, cols, cols, cols, P("hd"), P("hd"))
        + (P("cp"),) * 3
        + (tokens,),
        out_specs=(tokens, tokens, *weights, cols, cols, cols, P("hd"), P("hd"))
        + (P("cp"),) * 3,
        check_vma=False,
    )
```

time: 1890 us -> 757 us (0.40)
  waiting for transfers between devices: 1070 us -> 0.05 us
  Pallas kernels: 0 us -> 589 us
  blocking collectives: 233 us -> 0 us
  matrix products: 232 us -> 39.2 us
  local copies, waits for them, and re-layouts: 191 us -> 52.9 us
  other arithmetic: 86.4 us -> 30.9 us
  starting transfers between devices: 48.4 us -> 12.9 us
    reduce_scatter x8 -> x0, waiting for transfers between devices: 641 us -> none  [the longest x1 90.1 us: on_device(): lax.psum_scatter(weight_grad(ffn_in, grad_gate_low).astype(jnp.bfloat16),...]
    pallas_call x0 -> x10, Pallas kernels: none -> 589 us  [the longest x6 488 us: comm_call(): pl.pallas_call(body, out_shape=out_shape, in_specs=[pl.BlockSpec(memory_s...]
    all_gather x12 -> x2, waiting for transfers between devices: 349 us -> 0.01 us  [the longest x1 0.01 us: on_device(): lax.all_gather(jnp.concatenate([ff_pad(w_ffn_gate), ff_pad(w_ffn_up)], 1)...]
    dot_general x135 -> x12, matrix products: 232 us -> 39.2 us  [dot(): return jnp.einsum(spec, a, b, preferred_element_type=f32)]
    pad x22 -> x2, local copies, waits for them, and re-layouts: 87.8 us -> 0.13 us  [the longest x1 0.12 us: pieces(): return jnp.pad(split, ((0, 0), (0, -rows % 16), (0, 0))).astype(bf16)]
    unnamed x2 -> x0, blocking collectives: 73.5 us -> none
    all_to_all x5 -> x0, blocking collectives: 65.8 us -> none  [the longest x1 15.4 us: on_device(): lax.all_to_all(grad_mixed_low, 'hd', split_axis=2, concat_axis=1, tiled=T...]
    psum x2 -> x0, blocking collectives: 52.6 us -> none  [the longest x1 35 us: on_device(): lax.psum((grads_head[5], grads_head[6], grads_head[7], grads_head[8], gra...]
  transfers between devices with their start and end apart: 36 -> 8, of which waited for: 26 -> 0; matrix products, arithmetic and copies ran while one was open for 17% -> 6% of each run, Pallas kernels for 0% -> 35%
where the time goes in v1:
time: 757 us; the launch traced here: 742 us
  Pallas kernels  589 us (78%)
  local copies, waits for them, and re-layouts  52.9 us (7%)
  matrix products  39.2 us (5%)
  other arithmetic  30.9 us (4%)
  between operations  17.4 us (2%)
  starting transfers between devices  12.9 us (2%)
    pallas_call x6, Pallas kernels, comm_call(): pl.pallas_call(body, out_shape=out_shape, in_specs=[pl.BlockSpec(memory_s...  488 us
    pallas_call x4, Pallas kernels, kernel_call(): pl.pallas_call(body, out_shape=out_shape, in_specs=[pl.BlockSpec(memory_s...  100 us
    dot_general x12, matrix products, dot(): return jnp.einsum(spec, a, b, preferred_element_type=f32)  39.2 us
    unnamed x103, local copies, waits for them, and re-layouts  21.7 us
  transfers between devices with their start and end apart: 8, of which 0 were waited for; matrix products, arithmetic and copies ran while one was open for 6% of the time, Pallas kernels for 35%

profile of v1, /device:TPU:8, one launch (start us, length us, event | category | flops | bytes accessed | tf_op | source)
XLA Modules:
  0.0 742.2 jit_solution(6595420682688120111)
XLA Ops:
  9.8 3.4 collective-permute-start.1
  13.3 1.5 collective-permute-start.4
  14.8 3.4 collective-permute-start.3
  24.4 90.4 %shard_map.356 = (bf16[2,512,1024]{2,1,0:T(8,128)(2,1)S(1)}, bf16[1024,896]{1,0:T(8,128)(2,1)S(1)}) custom-call(bf16[2,64,1024]{2,1,0:T(8,128)(2,1)S(1)} %copy-done.5, bf16[64,896]{1,0:T(8,128)(2,1)S(1)} %pad_dynamic-update-slice_fusion.front_ref), custom_call_target="tpu_custom_call" | custom-call | tf_op jit(solution)/shard_map/pallas_call | solution.py:476
  115.8 4.2 fusion.77
  119.9 1.2 copy-done.32
  121.2 2.0 collective-permute-start
  123.5 1.2 add_divide_fusion.3
  126.6 1.2 fusion.49
  132.1 2.6 fusion.7
  136.0 32.2 %shard_map.357 = (f32[2,8,128,384]{3,2,1,0:T(8,128)}, bf16[2,128,384]{2,1,0:T(8,128)(2,1)S(1)}, f32[2,512,128]{2,1,0:T(8,128)S(1)}, f32[2,512,256]{2,1,0:T(8,128)S(1)}, f32[2,8,64,64]{3,2,1,0:T(8,128)S(1)}) custom-call(f32[2,512,128]{2,1,0:T(8,128)S(1)} %get-tuple-element.130.k_ref, f32[2,512,256]{2,1,0:T(8,128)S(1)} %slice.262.v_ref, ...), custom_call_target="tpu_custom_call" | custom-call | tf_op jit(solution)/shard_map/pallas_call | solution.py:229
  168.2 67.4 %shard_map.358.maps_ref = bf16[16,2,128,384]{3,2,1,0:T(8,128)(2,1)S(1)} custom-call(bf16[2,128,384]{2,1,0:T(8,128)(2,1)S(1)} %get-tuple-element.64.part_ref), custom_call_target="tpu_custom_call" | custom-call | tf_op jit(solution)/shard_map/pallas_call | solution.py:476
  235.7 1.7 copy-done
  237.3 17.0 %shard_map.359 = (bf16[2,512,256]{2,1,0:T(8,128)(2,1)S(1)}, f32[2,8,128,256]{3,2,1,0:T(8,128)}, f32[2,512,256]{2,1,0:T(8,128)S(1)}) custom-call(s32[1]{0:T(128)} %bitcast.place_ref, bf16[16,2,128,384]{3,2,1,0:T(8,128)(2,1)} %copy-done, f32[2,8,128,384]{3,2,1,0:T(8,128)} %get-tuple-element.65.x_ref, f32[2,512,128]{2,1,0:T(8,128)S(1)} %get-tuple-element.129.q_ref, ...), custom_call_target="tpu_custom_call" | custom-call | tf_op jit(solution)/shard_map/pallas_call | solution.py:229
  255.6 1.9 pad_maximum_fusion.4
  257.5 2.4 gather_fusion
  259.9 1.2 bitcast_select_fusion.1
  261.0 2.2 convolution_convert_fusion.1.partial_ref
  263.3 53.8 %shard_map.360 = (f32[2,64,1024]{2,1,0:T(8,128)S(1)}, bf16[2,512,1024]{2,1,0:T(8,128)(2,1)S(1)}) custom-call(bf16[2,512,1024]{2,1,0:T(8,128)(2,1)S(1)} %convolution_convert_fusion.1.partial_ref, bf16[2,64,1024]{2,1,0:T(8,128)(2,1)S(1)} %copy-done.6, f32[1,1024]{1,0:T(1,128)S(1)} %bitcast.127), custom_call_target="tpu_custom_call" | custom-call | tf_op jit(solution)/shard_map/pallas_call | solution.py:476
  317.9 1.3 copy-done.20
  319.2 2.0 pad_maximum_fusion.3
  321.2 2.6 gather_fusion.1
  323.8 2.1 bitcast_select_fusion
  325.9 5.5 fusion.17
  331.4 4.5 bitcast_multiply_fusion.1
  336.0 1.2 convolution_convert_fusion.out_part_ref
  337.8 3.1 bitcast_convert_fusion.1.ffn_ref
  340.9 3.2 convolution_convert_fusion.2.grad_part_ref
  344.2 73.8 %shard_map.361 = (bf16[2,64,1024]{2,1,0:T(8,128)(2,1)S(1)}, f32[2,64,1024]{2,1,0:T(8,128)S(1)}, f32[1,1024]{1,0:T(1,128)S(1)}, bf16[2,512,1024]{2,1,0:T(8,128)(2,1)S(1)}) custom-call(bf16[2,512,1024]{2,1,0:T(8,128)(2,1)S(1)} %convolution_convert_fusion.out_part_ref, bf16[2,512,1024]{2,1,0:T(8,128)(2,1)} %convolution_convert_fusion.2.grad_part_ref, ...), custom_call_target="tpu_custom_call" | custom-call | tf_op jit(solution)/shard_map/pallas_call | solution.py:476
  418.0 1.7 fusion.20
  419.8 2.1 fusion.26
  422.9 15.6 %shard_map.362 = (f32[2,512,256]{2,1,0:T(8,128)S(1)}, f32[2,8,128,256]{3,2,1,0:T(8,128)}, bf16[2,128,256]{2,1,0:T(8,128)(2,1)S(1)}) custom-call(f32[2,512,128]{2,1,0:T(8,128)S(1)} %get-tuple-element.129.q_ref, f32[2,512,128]{2,1,0:T(8,128)S(1)} %get-tuple-element.130.k_ref, f32[2,512,8]{2,1,0:T(8,128)S(1)} %select_maximum_fusion.aux_ref, ...), custom_call_target="tpu_custom_call" | custom-call | tf_op jit(solution)/shard_map/pallas_call | solution.py:229
  439.5 38.3 %shard_map.363.locals_ref = bf16[16,2,128,256]{3,2,1,0:T(8,128)(2,1)S(1)} custom-call(bf16[2,128,256]{2,1,0:T(8,128)(2,1)S(1)} %get-tuple-element.73.part_ref), custom_call_target="tpu_custom_call" | custom-call | tf_op jit(solution)/shard_map/pallas_call | solution.py:476
  477.9 1.3 copy-done.2
  479.2 35.7 %shard_map.364 = (f32[2,512,128]{2,1,0:T(8,128)S(1)}, f32[2,512,128]{2,1,0:T(8,128)S(1)}, f32[2,512,256]{2,1,0:T(8,128)}, f32[2,512,8]{2,1,0:T(8,128)S(1)}, f32[2,8,64]{2,1,0:T(8,128)S(1)}) custom-call(s32[1]{0:T(128)} %bitcast.place_ref, bf16[16,2,128,384]{3,2,1,0:T(8,128)(2,1)} %copy-done, bf16[16,2,128,256]{3,2,1,0:T(8,128)(2,1)} %copy-done.2, ...), custom_call_target="tpu_custom_call" | custom-call | tf_op jit(solution)/shard_map/pallas_call | solution.py:229
  517.4 2.0 multiply_reduce_fusion.3
  520.3 1.3 copy-done.25
  524.0 1.4 slice_reduce_fusion
  526.8 2.2 fusion.71
  529.6 1.5 collective-permute-start.5
  532.8 2.8 convolution_bitcast_fusion
  537.1 1.3 stack_reshape.6
  538.3 1.2 slice.272
  540.5 1.3 scatter-add.4
  541.9 5.9 fusion.3
  547.8 2.6 bitcast_convert_fusion
  551.7 4.6 concatenate.33.front_ref
  556.3 164.6 %shard_map.365 = (bf16[2,64,1024]{2,1,0:T(8,128)(2,1)S(1)}, bf16[8,64,896]{2,1,0:T(8,128)(2,1)S(1)}, bf16[8,64,768]{2,1,0:T(8,128)(2,1)S(1)}, bf16[8,16,1024]{2,...) custom-call(bf16[2,512,1024]{2,1,0:T(8,128)(2,1)} %get-tuple-element.121.normed_part_ref, ...), custom_call_target="tpu_custom_call" | custom-call | tf_op jit(solution)/shard_map/pallas_call | solution.py:476
  (209 shorter events, 46.9 us)
Async XLA Ops:
  7.2 318.7 %all-gather.3.cloned.1.call-start = ((), (), s32[]{:S(2)}) async-start(), calls=%async_computation | async-start | bytes 1671168 | tf_op jit(solution)/shard_map/all_gather | solution.py:735
  8.9 322.5 %all-gather.5.cloned.1.call-start = ((), (), s32[]{:S(2)}) async-start(), calls=%async_computation.1 | async-start | bytes 2359296 | tf_op jit(solution)/shard_map/all_gather | solution.py:739
  9.0 246.6 %collective-permute-start.2 = (bf16[128,1024]{1,0:T(8,128)(2,1)}, bf16[128,1024]{1,0:T(8,128)(2,1)}, u32[]{:S(2)}, u32[]{:S(2)}) collective-permute-start(bf16[128,1024]{1,0:T(8,128)(2,1)} %param.31), channel_id=1, source_target_pairs={{0,8},{1,24},{2,40},{3,56},{4,72},{5,88},{6,104},{7,120},{8,0},{9,... | collective-permute-start | bytes 786440 | tf_op jit(solution)/shard_map/ppermute | solution.py:674
  9.8 245.7 %collective-permute-start.1 = (bf16[128,1024]{1,0:T(8,128)(2,1)}, bf16[128,1024]{1,0:T(8,128)(2,1)}, u32[]{:S(2)}, u32[]{:S(2)}) collective-permute-start(bf16[128,1024]{1,0:T(8,128)(2,1)} %param.31), channel_id=1, source_target_pairs={{0,0},{1,16},{2,32},{3,48},{4,64},{5,80},{6,96},{7,112},{8,8},{9,2... | collective-permute-start | bytes 786440 | tf_op jit(solution)/shard_map/ppermute | solution.py:674
  13.3 305.9 %collective-permute-start.4 = (bf16[176,1024]{1,0:T(8,128)(2,1)}, bf16[176,1024]{1,0:T(8,128)(2,1)}, u32[]{:S(2)}, u32[]{:S(2)}) collective-permute-start(bf16[176,1024]{1,0:T(8,128)(2,1)} %param.34), channel_id=1, source_target_pairs={{0,8},{1,24},{2,40},{3,56},{4,72},{5,88},{6,104},{7,120},{8,0},{9,... | collective-permute-start | bytes 1081352 | tf_op jit(solution)/shard_map/ppermute | solution.py:674
  14.8 304.4 %collective-permute-start.3 = (bf16[176,1024]{1,0:T(8,128)(2,1)}, bf16[176,1024]{1,0:T(8,128)(2,1)}, u32[]{:S(2)}, u32[]{:S(2)}) collective-permute-start(bf16[176,1024]{1,0:T(8,128)(2,1)} %param.34), channel_id=1, source_target_pairs={{0,0},{1,16},{2,32},{3,48},{4,64},{5,80},{6,96},{7,112},{8,8},{9,2... | collective-permute-start | bytes 1081352 | tf_op jit(solution)/shard_map/ppermute | solution.py:674
  114.8 5.1 copy-start.7
  114.8 8.4 %copy-start.17 = (bf16[1024,896]{1,0:T(8,128)(2,1)}, bf16[1024,896]{1,0:T(8,128)(2,1)S(1)}, u32[]{:S(2)}) copy-start(bf16[1024,896]{1,0:T(8,128)(2,1)S(1)} %get-tuple-element.63) | copy-start | bytes 5505028
  115.7 10.4 %copy-start.38 = (s32[2,8192]{1,0:T(2,128)S(1)}, s32[2,8192]{1,0:T(2,128)}, u32[]{:S(2)}) copy-start(s32[2,8192]{1,0:T(2,128)} %param.24) | copy-start | bytes 196612
  115.7 10.8 %copy-start.43 = (bf16[4,256]{1,0:T(4,128)(2,1)S(1)}, bf16[4,256]{1,0:T(4,128)(2,1)}, u32[]{:S(2)}) copy-start(bf16[4,256]{1,0:T(4,128)(2,1)} %param.37) | copy-start | bytes 6148
  115.7 10.8 %copy-start.44 = (bf16[4,128]{1,0:T(4,128)(2,1)S(1)}, bf16[4,128]{1,0:T(4,128)(2,1)}, u32[]{:S(2)}) copy-start(bf16[4,128]{1,0:T(4,128)(2,1)} %param.36) | copy-start | bytes 3076
  115.8 10.8 %copy-start.45 = (bf16[4,128]{1,0:T(4,128)(2,1)S(1)}, bf16[4,128]{1,0:T(4,128)(2,1)}, u32[]{:S(2)}) copy-start(bf16[4,128]{1,0:T(4,128)(2,1)} %param.35) | copy-start | bytes 3076
  121.2 10.6 %collective-permute-start = (bf16[2,3,512]{2,1,0:T(4,128)(2,1)S(1)}, bf16[2,3,512]{2,1,0:T(4,128)(2,1)S(1)}, u32[]{:S(2)}, u32[]{:S(2)}) collective-permute-start(bf16[2,3,512]{2,1,0:T(4,128)(2,1)S(1)} %slice.252), channel_id=1, source_target_pairs={{0,8},{8,16},{16,24},{24,32},{32,40},{40,48},{48,56},{56,64},{64,7... | collective-permute-start | bytes 18440 | tf_op jit(solution)/shard_map/ppermute | solution.py:661
  129.9 1.5 copy-start.33
  132.1 2.6 copy-start.22
  134.6 1.3 copy-start.28
  134.7 33.4 %copy-start.1 = (f32[2,512,256]{2,1,0:T(8,128)}, f32[2,512,256]{2,1,0:T(8,128)S(1)}, u32[]{:S(2)}) copy-start(f32[2,512,256]{2,1,0:T(8,128)S(1)} %slice.262.v_ref) | copy-start | bytes 3145732
  168.2 86.1 %copy-start.3 = (f32[2,512,128]{2,1,0:T(8,128)}, f32[2,512,128]{2,1,0:T(8,128)S(1)}, u32[]{:S(2)}) copy-start(f32[2,512,128]{2,1,0:T(8,128)S(1)} %get-tuple-element.66.w_ref) | copy-start | bytes 1572868
  235.6 1.7 copy-start
  261.0 2.3 copy-start.39
  261.0 2.3 copy-start.6
  317.9 1.3 copy-start.20
  331.4 4.5 copy-start.37
  336.0 1.9 copy-start.21
  337.8 3.1 copy-start.46
  340.9 3.2 copy-start.11
  340.9 3.2 copy-start.16
  344.2 73.8 %copy-start.42 = (f32[2,512,896]{2,1,0:T(8,128)S(1)}, f32[2,512,896]{2,1,0:T(8,128)}, u32[]{:S(2)}) copy-start(f32[2,512,896]{2,1,0:T(8,128)} %get-tuple-element.153) | copy-start | bytes 11010052
  418.0 1.8 copy-start.12
  418.0 1.8 copy-start.18
  418.0 1.8 copy-start.40
  477.9 1.3 copy-start.2
  479.2 35.7 %copy-start.29 = (f32[2,512,512]{2,1,0:T(8,128)S(1)}, f32[2,512,512]{2,1,0:T(8,128)}, u32[]{:S(2)}) copy-start(f32[2,512,512]{2,1,0:T(8,128)} %copy-done.28) | copy-start | bytes 6291460
  514.8 1.6 copy-start.30
  515.2 2.0 copy-start.23
  515.2 2.2 copy-start.34
  520.2 1.3 copy-start.25
  520.2 1.9 copy-start.26
  520.2 2.6 copy-start.27
  520.2 3.7 copy-start.24
  529.6 9.9 %collective-permute-start.5 = (f32[2,3,512]{2,1,0:T(4,128)S(1)}, f32[2,3,512]{2,1,0:T(4,128)S(1)}, u32[]{:S(2)}, u32[]{:S(2)}) collective-permute-start(f32[2,3,512]{2,1,0:T(4,128)S(1)} %pad_add_fusion.1), channel_id=1, source_target_pairs={{8,0},{16,8},{24,16},{32,24},{40,32},{48,40},{56,48},{64,56},{72,6... | collective-permute-start | bytes 36872 | tf_op jit(solution)/shard_map/ppermute | solution.py:661
  539.5 2.3 copy-start.8
  541.9 5.9 copy-start.35
  541.9 5.9 copy-start.41
  541.9 5.9 copy-start.47
  551.7 4.6 copy-start.13
  551.7 4.6 copy-start.14
  730.8 2.7 copy-start.19
  (8 other events, 8.5 us)
Sparse Core Ops, SparseCore 0:
  11.0 90.5 all-gather.2
  123.3 63.2 all-gather.4

commit v2 on v1

--- a/solution.py
+++ b/solution.py
@@ -7,6 +7,7 @@
 
 STRETCH = 64
 LANES = 128
+CORES = 2
 HIGHEST = lax.Precision.HIGHEST
 EPSILON = 1e-06
 bf16, f32 = jnp.bfloat16, jnp.float32
@@ -29,29 +30,35 @@
     return pl.ds(pl.multiple_of(n * STRETCH, STRETCH), STRETCH)
 
 
-def maps_kernel(k_ref, v_ref, aux_ref, between_ref, x_ref, end_ref, w_ref, u_ref, inv_ref):
+def segment_maps(k_ref, v_ref, aux_ref, between_ref, x_ref, end_ref, w_ref, u_ref, inv_ref):
     sequences, length, dk = k_ref.shape
     dv = v_ref.shape[2]
     blocks = length // STRETCH
     strict, unit = lower_strict()
 
-    def prepare_block(n, carry):
-        rows = block_rows(n)
-        for s in range(sequences):
-            k = k_ref[s, rows]
+    def prepare_block(pair, carry):
+        streams = [(s, 2 * pair + half) for s in range(sequences) for half in range(2)]
+        powers, inverses = [], []
+        for s, n in streams:
+            k = k_ref[s, block_rows(n)]
+            beta = aux_ref[s, block_rows(n), 0:1]
+            powers.append(-beta * (between_ref[s, n] * strict) * mm(k, k, 1, 1))
+            inverses.append(unit + powers[-1])
+        for level in range(STRETCH.bit_length() - 2):
+            powers = [mm(power, power) for power in powers]
+            inverses = [
+                inverse + mm(inverse, power) for inverse, power in zip(inverses, powers)
+            ]
+        for (s, n), inverse in zip(streams, inverses):
+            rows = block_rows(n)
             beta = aux_ref[s, rows, 0:1]
             gamma = aux_ref[s, rows, 1:2]
-            power = -beta * (between_ref[s, n] * strict) * mm(k, k, 1, 1)
-            inverse = unit + power
-            for level in range(STRETCH.bit_length() - 2):
-                power = mm(power, power)
-                inverse = inverse + mm(inverse, power)
             inv_ref[s, n] = inverse
-            w_ref[s, rows] = mm(inverse, beta * gamma * k)
+            w_ref[s, rows] = mm(inverse, beta * gamma * k_ref[s, rows])
             u_ref[s, rows] = mm(inverse, beta * v_ref[s, rows])
         return carry
 
-    lax.fori_loop(0, blocks, prepare_block, 0)
+    lax.fori_loop(0, blocks // 2, prepare_block, 0)
 
     wide = (dk, dk + dv)
     start = (
@@ -76,30 +83,18 @@
         end_ref[s] = ends[s].astype(end_ref.dtype)
 
 
-def run_kernel(
-    place_ref, maps_ref, x_ref, q_ref, k_ref, aux_ref, between_ref, w_ref, u_ref,
+def run_segment(
+    entry_ref, x_ref, q_ref, k_ref, aux_ref, between_ref, w_ref, u_ref,
     out_ref, state_ref, update_ref,
 ):
     sequences, length, dk = k_ref.shape
-    dv = u_ref.shape[2]
     blocks = length // STRETCH
-
-    def enter(hop, states):
-        return tuple(
-            mm(maps_ref[hop, s, :, :dk].astype(f32), states[s])
-            + maps_ref[hop, s, :, dk:].astype(f32)
-            for s in range(sequences)
-        )
-
-    entry = lax.fori_loop(
-        0, place_ref[0], enter, (jnp.zeros((dk, dv), f32),) * sequences
-    )
 
     def run_block(n, carry):
         rows = block_rows(n)
         for s in range(sequences):
             q, k = q_ref[s, rows], k_ref[s, rows]
-            state = mm(x_ref[s, n, :, :dk], entry[s]) + x_ref[s, n, :, dk:]
+            state = mm(x_ref[s, n, :, :dk], entry_ref[s]) + x_ref[s, n, :, dk:]
             update = u_ref[s, rows] - mm(w_ref[s, rows], state)
             scores = mm(q, k, 1, 1) * between_ref[s, n]
             out = aux_ref[s, rows, 1:2] * mm(q, state) + mm(scores, update)
@@ -111,7 +106,7 @@
     lax.fori_loop(0, blocks, run_block, 0)
 
 
-def back_local_kernel(
+def segment_local(
     q_ref, k_ref, aux_ref, between_ref, w_ref, grad_ref, through_ref, inflow_ref, local_ref
 ):
     sequences, length, dk = k_ref.shape
@@ -148,30 +143,17 @@
         local_ref[s] = ends[s].astype(local_ref.dtype)
 
 
-def back_kernel(
-    place_ref, maps_ref, locals_ref, q_ref, k_ref, v_ref, aux_ref, between_ref, w_ref, inv_ref,
+def back_blocks(
+    first, count, exits,
+    q_ref, k_ref, v_ref, aux_ref, between_ref, w_ref, inv_ref,
     state_ref, update_ref, grad_ref, through_ref, inflow_ref,
     grad_q_ref, grad_k_ref, grad_v_ref, grad_aux_ref, grad_row_ref,
 ):
     sequences, length, dk = k_ref.shape
-    dv = v_ref.shape[2]
     blocks = length // STRETCH
-    segments = maps_ref.shape[0]
     strict, _ = lower_strict()
     at_last = lax.broadcasted_iota(jnp.int32, (STRETCH, 1), 0) == STRETCH - 1
     lane = lax.broadcasted_iota(jnp.int32, (STRETCH, grad_aux_ref.shape[2]), 1)
-
-    def leave(hop, states):
-        source = segments - 1 - hop
-        return tuple(
-            mm(maps_ref[source, s, :, :dk].astype(f32), states[s], 0, 0)
-            + locals_ref[source, s].astype(f32)
-            for s in range(sequences)
-        )
-
-    exits = lax.fori_loop(
-        0, segments - 1 - place_ref[0], leave, (jnp.zeros((dk, dv), f32),) * sequences
-    )
 
     def row_sum(a):
         return jnp.sum(a, axis=1, keepdims=True)
@@ -221,19 +203,7 @@
             grad_aux_ref[s, rows] = jnp.where(lane == 0, grad_beta, grad_cumulative)
         return tuple(after)
 
-    lax.fori_loop(0, blocks, chain_block, exits)
-
-
-def kernel_call(body, out_shape, *operands, scalars=0):
-    whole = pl.BlockSpec(memory_space=pltpu.VMEM)
-    return pl.pallas_call(
-        body,
-        out_shape=out_shape,
-        in_specs=[pl.BlockSpec(memory_space=pltpu.SMEM)] * scalars
-        + [whole] * (len(operands) - scalars),
-        out_specs=jax.tree.map(lambda _: whole, out_shape),
-        compiler_params=pltpu.CompilerParams(vmem_limit_bytes=VMEM_LIMIT),
-    )(*operands)
+    return lax.fori_loop(first, first + count, chain_block, exits)
 
 
 def shaped(shape, kind=f32):
@@ -299,57 +269,92 @@
     lax.fori_loop(1, count, step, 0)
 
 
-def owner_targets(action):
-    hd, me, head = lax.axis_size("hd"), lax.axis_index("cp"), lax.axis_index("hd")
-    cp = lax.axis_size("cp")
-    share = cp // hd
-
+def chip_devices(action):
+    count, me = lax.axis_size("cp") // CORES, lax.axis_index("cp")
+    chip, core = me // CORES, lax.rem(me, CORES)
+
+    def step(distance, carry):
+        ahead, behind = lax.rem(chip + distance, count), lax.rem(chip + count - distance, count)
+        action(distance, ahead * CORES + core, behind * CORES + core)
+        return carry
+
+    lax.fori_loop(1, count, step, 0)
+
+
+def sibling():
+    me = lax.axis_index("cp")
+    return me + 1 - 2 * lax.rem(me, CORES)
+
+
+def owner_target(turn):
+    hd = lax.axis_size("hd")
+    share = lax.axis_size("cp") // hd
+    piece = CORES * turn + lax.rem(lax.axis_index("cp"), CORES)
+    return share * lax.axis_index("hd") + piece // hd, lax.rem(piece, hd)
+
+
+def owner_source(chip):
+    share = lax.axis_size("cp") // lax.axis_size("hd")
+    core = lax.rem(lax.axis_index("hd"), CORES)
+    return CORES * chip + core, lax.axis_index("cp") // share
+
+
+def column_target(turn):
+    return CORES * turn + lax.rem(lax.axis_index("cp"), CORES), lax.axis_index("hd")
+
+
+def row_target(turn):
+    share = lax.axis_size("cp") // lax.axis_size("hd")
+    return share * lax.axis_index("hd") + turn, lax.axis_index("cp") // share
+
+
+def is_me(at):
+    return (at[0] == lax.axis_index("cp")) & (at[1] == lax.axis_index("hd"))
+
+
+def each(count, action):
     def step(turn, carry):
-        piece = lax.rem(turn + me, cp)
-        to = (share * head + piece // hd, lax.rem(piece, hd))
-        action(piece, to, (to[0] == me) & (to[1] == head))
+        action(turn)
         return carry
 
-    lax.fori_loop(0, cp, step, 0)
-
-
-def owner_sources(action):
-    hd, me, head = lax.axis_size("hd"), lax.axis_index("cp"), lax.axis_index("hd")
-    cp = lax.axis_size("cp")
-    column = me // (cp // hd)
-
-    def step(source, carry):
-        action(source, (source, column), (source == me) & (column == head))
-        return carry
-
-    lax.fori_loop(0, cp, step, 0)
-
-
-def meet(axes, owners=False):
-    barrier = pltpu.get_barrier_semaphore()
-    total = 0
-    for axis in axes:
-        each_peer(
-            axis,
-            lambda _, to, source, axis=axis: pl.semaphore_signal(
-                barrier, inc=1, device_id={axis: to}, device_id_type=pl.DeviceIdType.MESH
-            ),
-        )
-        total += lax.axis_size(axis) - 1
-    if owners:
-        cp, hd = lax.axis_size("cp"), lax.axis_size("hd")
-
-        def greet(source, at, own):
-            @pl.when(jnp.logical_not(own))
-            def _():
-                pl.semaphore_signal(
-                    barrier, inc=1, device_id=at, device_id_type=pl.DeviceIdType.MESH
-                )
-
-        owner_sources(greet)
-        alone = lax.axis_index("cp") // (cp // hd) == lax.axis_index("hd")
-        total = total + cp - alone.astype(jnp.int32)
-    pl.semaphore_wait(barrier, total)
+    lax.fori_loop(0, count, step, 0)
+
+
+def signal(target):
+    pl.semaphore_signal(
+        pltpu.get_barrier_semaphore(), inc=1, device_id=target,
+        device_id_type=pl.DeviceIdType.MESH,
+    )
+
+
+def meet(heads=False, chips=False, owners=False, rows=False):
+    cp, hd = lax.axis_size("cp"), lax.axis_size("hd")
+    total = jnp.int32(0)
+    if heads:
+        each_peer("hd", lambda _, to, source: signal({"hd": to}))
+        total += hd - 1
+    if chips:
+        chip_devices(lambda _, to, source: signal({"cp": to}))
+        signal({"cp": sibling()})
+        total += cp // CORES
+    for wanted, count, source_of, target_of in (
+        (owners, cp // CORES, owner_source, owner_target),
+        (rows, cp // hd, row_target, row_target),
+    ):
+        if wanted:
+
+            def greet(turn, source_of=source_of):
+                at = source_of(turn)
+
+                @pl.when(jnp.logical_not(is_me(at)))
+                def _():
+                    signal(at)
+
+            each(count, greet)
+            total += count
+            for turn in range(count):
+                total -= is_me(target_of(turn)).astype(jnp.int32)
+    pl.semaphore_wait(pltpu.get_barrier_semaphore(), total)
 
 
 def remote(src, dst, send, recv, target):
@@ -403,57 +408,160 @@
         )
 
 
-class OwnerExchange:
+class PairGather:
     def __init__(self, source, landing, send, recv, local):
-        self.source, self.landing = source, landing
+        self.source, self.landing, self.send, self.recv = source, landing, send, recv
+        self.me = lax.axis_index("cp")
+        self.count = lax.axis_size("cp") // CORES
+        self.own = pltpu.make_async_copy(source, landing(self.me), local)
+
+    def copy(self, block, index, slot, to):
+        return remote(
+            block, self.landing(index), self.send.at[slot], self.recv.at[index], {"cp": to}
+        )
+
+    def start(self):
+        chip_devices(lambda d, to, source: self.copy(self.source, self.me, d, to).start())
+        self.copy(self.source, self.me, 0, sibling()).start()
+        self.own.start()
+
+    def arrive(self):
+        def hand_on(d, to, source):
+            self.copy(self.source, source, d, to).wait_recv()
+            self.copy(self.landing(source), source, self.count + d, sibling()).start()
+
+        chip_devices(hand_on)
+        other = sibling()
+        self.copy(self.source, other, 0, other).wait_recv()
+        shift = other - self.me
+        chip_devices(
+            lambda d, to, source: self.copy(self.source, source + shift, d, other).wait_recv()
+        )
+        self.own.wait()
+
+    def leave(self):
+        chip_devices(lambda d, to, source: self.copy(self.source, self.me, d, to).wait_send())
+        self.copy(self.source, self.me, 0, sibling()).wait_send()
+        chip_devices(
+            lambda d, to, source: self.copy(
+                self.source, source, self.count + d, sibling()
+            ).wait_send()
+        )
+
+
+class PairReduce:
+    def __init__(self, parts, inbox, sums, landed, swap, send, recv, local, target, source):
+        self.parts, self.inbox, self.sums, self.landed = parts, inbox, sums, landed
         self.send, self.recv, self.local = send, recv, local
+        self.target, self.source = target, source
+        me = lax.axis_index("cp")
+        self.chip, self.core = me // CORES, lax.rem(me, CORES)
+        self.swap = remote(
+            parts.at[:, 1 - self.core], inbox, swap.at[0], swap.at[1], {"cp": sibling()}
+        )
 
     def start(self):
-        me = lax.axis_index("cp")
-
-        def go(piece, to, own):
-            @pl.when(own)
-            def _():
-                pltpu.make_async_copy(self.source(piece), self.landing(me), self.local).start()
-
-            @pl.when(jnp.logical_not(own))
-            def _():
-                remote(
-                    self.source(piece), self.landing(me), self.send.at[piece], self.recv.at[me], to
-                ).start()
-
-        owner_targets(go)
-
-    def arrive(self):
-        def get(source, at, own):
+        self.swap.start()
+
+    def move(self, turn, slot, to):
+        return remote(
+            self.sums.at[turn], self.landed.at[slot], self.send.at[turn], self.recv.at[slot], to
+        )
+
+    def add_pairs(self):
+        self.swap.wait()
+
+        def go(turn):
+            total = self.parts[turn, self.core].astype(f32) + self.inbox[turn].astype(f32)
+            self.sums[turn] = total.astype(bf16)
+            to = self.target(turn)
+            own = is_me(to)
+
             @pl.when(own)
             def _():
                 pltpu.make_async_copy(
-                    self.source(source), self.landing(source), self.local
-                ).wait()
+                    self.sums.at[turn], self.landed.at[self.chip], self.local
+                ).start()
 
             @pl.when(jnp.logical_not(own))
             def _():
-                remote(
-                    self.source(source),
-                    self.landing(source),
-                    self.send.at[source],
-                    self.recv.at[source],
-                    at,
-                ).wait_recv()
-
-        owner_sources(get)
-
-    def leave(self):
-        def done(piece, to, own):
+                self.move(turn, self.chip, to).start()
+
+        each(self.sums.shape[0], go)
+
+    def total(self):
+        def get(chip):
+            at = self.source(chip)
+            own = is_me(at)
+
+            @pl.when(own)
+            def _():
+                pltpu.make_async_copy(
+                    self.sums.at[chip], self.landed.at[chip], self.local
+                ).wait()
+
             @pl.when(jnp.logical_not(own))
             def _():
-                remote(
-                    self.source(piece), self.landing(piece), self.send.at[piece],
-                    self.recv.at[piece], to,
-                ).wait_send()
-
-        owner_targets(done)
+                self.move(chip, chip, at).wait_recv()
+
+        each(self.landed.shape[0], get)
+        return added(self.landed).astype(bf16)
+
+    def leave(self):
+        def done(turn):
+            to = self.target(turn)
+
+            @pl.when(jnp.logical_not(is_me(to)))
+            def _():
+                self.move(turn, turn, to).wait_send()
+
+        each(self.sums.shape[0], done)
+
+
+class RowMove:
+    def __init__(self, rows, landing, send, recv, local):
+        self.rows, self.send, self.recv, self.local = rows, send, recv, local
+        self.count = lax.axis_size("cp") // lax.axis_size("hd")
+        self.slot = lax.rem(lax.axis_index("cp"), self.count)
+        self.landing = lambda slot: lead_rows(landing, slot, rows.shape[0])
+
+    def copy(self, turn, slot, to):
+        return remote(self.rows, self.landing(slot), self.send.at[turn], self.recv.at[slot], to)
+
+    def kept(self):
+        return pltpu.make_async_copy(self.rows, self.landing(self.slot), self.local)
+
+    def start(self):
+        def go(turn):
+            to = row_target(turn)
+
+            @pl.when(is_me(to))
+            def _():
+                self.kept().start()
+
+            @pl.when(jnp.logical_not(is_me(to)))
+            def _():
+                self.copy(turn, self.slot, to).start()
+
+        each(self.count, go)
+
+    def arrive(self):
+        def get(turn):
+            at = row_target(turn)
+
+            @pl.when(is_me(at))
+            def _():
+                self.kept().wait()
+
+            @pl.when(jnp.logical_not(is_me(at)))
+            def _():
+                self.copy(turn, turn, at).wait_recv()
+                self.copy(turn, turn, at).wait_send()
+
+        each(self.count, get)
+
+    def leave(self):
+        pass
 
 
 def sems(*counts):
@@ -461,6 +569,13 @@
     for count in counts:
         found += [pltpu.SemaphoreType.DMA((count,))] * 2 + [pltpu.SemaphoreType.DMA]
     return found
+
+
+def reduce_scratch(parts):
+    half = (parts.shape[0], *parts.shape[2:])
+    return [pltpu.VMEM(half, bf16)] * 3 + [
+        pltpu.SemaphoreType.DMA((2,)), *sems(parts.shape[0])
+    ]
 
 
 def token_rows(ref, index, tokens):
@@ -487,36 +602,177 @@
 
 def open_kernel(hidden_ref, front_ref, hidden_all_ref, front_all_ref, *flags):
     tokens, shard = hidden_ref.shape[1], front_ref.shape[0]
-    meet(("hd", "cp"))
+    meet(heads=True, chips=True)
     moves = (
         Exchange(
             "hd", lambda to: hidden_ref, lambda at: token_rows(hidden_all_ref, at, tokens), *flags[:3]
         ),
-        Exchange(
-            "cp", lambda to: front_ref, lambda at: lead_rows(front_all_ref, at, shard), *flags[3:6]
-        ),
+        PairGather(front_ref, lambda at: lead_rows(front_all_ref, at, shard), *flags[3:6]),
     )
     for move in moves:
         move.start()
-    for move in moves:
+    for move in reversed(moves):
         move.arrive()
         move.leave()
 
 
-def stack_kernel(part_ref, all_ref, *flags):
-    meet(("cp",))
-    move = Exchange("cp", lambda to: part_ref, lambda at: all_ref.at[at], *flags)
-    move.start()
-    move.arrive()
-    move.leave()
-
-
-def gather_stack(part, number):
-    cp = lax.axis_size("cp")
-    return comm_call(
-        stack_kernel, (shaped((cp, *part.shape), part.dtype),), ("any",), (part,), ("any",),
-        sems(cp), number,
-    )[0]
+def place_of():
+    me = lax.axis_index("cp")
+    return me // CORES, lax.rem(me, CORES)
+
+
+def forward_kernel(
+    q_ref, k_ref, v_ref, aux_ref, between_ref, cot_ref, ffn_ref, output_ref, down_ref,
+    mixed_ref, state_ref, update_ref, w_ref, inv_ref, maps_ref, both_ref,
+    cot_all_ref, ffn_all_ref, output_part_ref, down_part_ref,
+    x_ref, u_ref, own_ref, other_ref, entry_ref, give_ref, pair_sems, *flags
+):
+    sequences, _, dk = k_ref.shape
+    dv = v_ref.shape[2]
+    tokens, shard = cot_ref.shape[1], ffn_ref.shape[0]
+    chip, core = place_of()
+    early = core == 0
+    meet(heads=True, chips=True, rows=True)
+    carried = (
+        PairGather(ffn_ref, lambda at: lead_rows(ffn_all_ref, at, shard), *flags[:3]),
+        RowMove(output_ref, output_part_ref, *flags[3:6]),
+        RowMove(down_ref, down_part_ref, *flags[6:9]),
+        Exchange(
+            "hd", lambda to: cot_ref, lambda at: token_rows(cot_all_ref, at, tokens), *flags[9:12]
+        ),
+    )
+    for move in carried:
+        move.start()
+    segment_maps(k_ref, v_ref, aux_ref, between_ref, x_ref, own_ref, w_ref, u_ref, inv_ref)
+    swap = remote(
+        own_ref.at[1 - core], other_ref, pair_sems.at[0], pair_sems.at[1], {"cp": sibling()}
+    )
+    swap.start()
+    swap.wait()
+    mine, theirs = own_ref[core], other_ref[...]
+    both_ref[0] = jnp.where(early, mine, theirs)
+    both_ref[1] = jnp.where(early, theirs, mine)
+    first, second = both_ref[0].astype(f32), both_ref[1].astype(f32)
+    pair = mm(second[:, :dk], first)
+    pair = jnp.concatenate([pair[:, :dk], pair[:, dk:] + second[:, dk:]], 1)
+    maps_ref[chip] = pair.astype(bf16)
+    spread_chips(maps_ref, flags[12], flags[13])
+
+    def enter(hop, state):
+        return mm(maps_ref[hop, :, :dk].astype(f32), state) + maps_ref[hop, :, dk:].astype(f32)
+
+    entered = lax.fori_loop(0, chip, enter, jnp.zeros((dk, dv), f32))
+    halfway = mm(first[:, :dk], entered) + first[:, dk:]
+    entry_ref[core] = jnp.where(early, entered, halfway)
+    give_ref[...] = jnp.where(early, halfway, entered)
+    give = remote(
+        give_ref, entry_ref.at[core], pair_sems.at[2], pair_sems.at[3], {"cp": sibling()}
+    )
+    give.start()
+    remote(
+        give_ref, entry_ref.at[1 - core], pair_sems.at[2], pair_sems.at[3], {"cp": sibling()}
+    ).wait()
+    run_segment(
+        entry_ref, x_ref, q_ref, k_ref, aux_ref, between_ref, w_ref, u_ref,
+        mixed_ref, state_ref, update_ref,
+    )
+    for move in carried:
+        move.arrive()
+    for move in carried:
+        move.leave()
+
+
+def spread_chips(ref, send, recv):
+    chip, _ = place_of()
+
+    def copy(distance, index, to):
+        return remote(ref.at[index], ref.at[index], send.at[distance], recv.at[distance], {"cp": to})
+
+    chip_devices(lambda d, to, source: copy(d, chip, to).start())
+    chip_devices(lambda d, to, source: copy(d, source // CORES, to).wait_recv())
+    chip_devices(lambda d, to, source: copy(d, chip, to).wait_send())
+
+
+def backward_kernel(
+    q_ref, k_ref, v_ref, aux_ref, between_ref, w_ref, inv_ref, state_ref, update_ref, grad_ref,
+    maps_ref, both_ref, ffn_ref, down_ref,
+    grad_q_ref, grad_k_ref, grad_v_ref, grad_aux_ref, grad_row_ref, ffn_all_ref, down_all_ref,
+    through_ref, inflow_ref, own_ref, other_ref, locals_ref, exit_ref, give_ref,
+    ffn_own_ref, down_own_ref, pair_sems, chip_send, chip_recv, *flags
+):
+    sequences, length, dk = k_ref.shape
+    dv = v_ref.shape[2]
+    blocks = length // STRETCH
+    chip, core = place_of()
+    chips = locals_ref.shape[0]
+    late = core == CORES - 1
+    meet(heads=True, chips=True, owners=True)
+    reduces = (
+        PairReduce(ffn_ref, *flags[:7], column_target, column_source),
+        PairReduce(down_ref, *flags[7:14], owner_target, owner_source),
+    )
+    for move in reduces:
+        move.start()
+    segment_local(
+        q_ref, k_ref, aux_ref, between_ref, w_ref, grad_ref, through_ref, inflow_ref, own_ref
+    )
+    swap = remote(
+        own_ref.at[1 - core], other_ref, pair_sems.at[0], pair_sems.at[1], {"cp": sibling()}
+    )
+    swap.start()
+    swap.wait()
+    mine, theirs = own_ref[core].astype(f32), other_ref[...].astype(f32)
+    first, second = jnp.where(late, theirs, mine), jnp.where(late, mine, theirs)
+    locals_ref[chip] = (mm(both_ref[0, :, :dk].astype(f32), second, 0, 0) + first).astype(bf16)
+    spread_chips(locals_ref, chip_send, chip_recv)
+    for move in reduces:
+        move.add_pairs()
+
+    def leave(hop, state):
+        source = chips - 1 - hop
+        return mm(maps_ref[source, :, :dk].astype(f32), state, 0, 0) + locals_ref[
+            source
+        ].astype(f32)
+
+    left = lax.fori_loop(0, chips - 1 - chip, leave, jnp.zeros((dk, dv), f32))
+    halfway = mm(both_ref[1, :, :dk].astype(f32), left, 0, 0) + second
+    exit_ref[core] = jnp.where(late, left, halfway)
+    give_ref[...] = jnp.where(late, halfway, left)
+    remote(
+        give_ref, exit_ref.at[core], pair_sems.at[2], pair_sems.at[3], {"cp": sibling()}
+    ).start()
+    remote(
+        give_ref, exit_ref.at[1 - core], pair_sems.at[2], pair_sems.at[3], {"cp": sibling()}
+    ).wait()
+    refs = (
+        q_ref, k_ref, v_ref, aux_ref, between_ref, w_ref, inv_ref, state_ref, update_ref,
+        grad_ref, through_ref, inflow_ref,
+        grad_q_ref, grad_k_ref, grad_v_ref, grad_aux_ref, grad_row_ref,
+    )
+    exits = tuple(exit_ref[s] for s in range(sequences))
+    exits = back_blocks(0, blocks // 2, exits, *refs)
+    spreads = []
+    for n, (move, own, everywhere) in enumerate(
+        zip(reduces, (ffn_own_ref, down_own_ref), (ffn_all_ref, down_all_ref))
+    ):
+        own[...] = move.total()
+        spreads.append(spread_piece(own, everywhere, flags[14 + 3 * n : 17 + 3 * n]))
+    back_blocks(blocks // 2, blocks - blocks // 2, exits, *refs)
+    for move in reduces:
+        move.leave()
+    for spread in spreads:
+        spread.arrive()
+        spread.leave()
+
+
+def column_source(chip):
+    return column_target(chip)
+
+
+def spread_piece(own, everywhere, flags):
+    spread = Exchange("hd", lambda to: own, lambda at: everywhere.at[at], *flags)
+    spread.start()
+    return spread
 
 
 def added(landed_ref):
@@ -536,7 +792,7 @@
     partial_ref, hidden_ref, gain_ref, middle_ref, ffn_all_ref, landed_ref, own_ref, *flags
 ):
     tokens = hidden_ref.shape[1]
-    meet(("hd",))
+    meet(heads=True)
     move = Exchange(
         "hd", lambda to: token_rows(partial_ref, to, tokens), lambda at: landed_ref.at[at], *flags[:3]
     )
@@ -564,7 +820,7 @@
     out_landed_ref, grad_landed_ref, own_ref, *flags
 ):
     tokens = middle_ref.shape[1]
-    meet(("hd",))
+    meet(heads=True)
     moves = [
         Exchange(
             "hd",
@@ -595,60 +851,41 @@
 
 
 def close_kernel(
-    normed_part_ref, front_ref, ffn_ref, output_ref, down_ref, small_ref,
-    hidden_ref, grad_middle_ref, gain_ref,
-    grad_in_ref, front_all_ref, ffn_all_ref, output_all_ref, down_all_ref, small_sum_ref,
-    normed_landed, front_landed, ffn_landed, output_landed, down_landed, small_landed,
-    front_own, ffn_own, output_own, down_own, *flags
+    normed_part_ref, front_ref, output_ref, small_ref, hidden_ref, grad_middle_ref, gain_ref,
+    grad_in_ref, front_all_ref, output_all_ref, small_sum_ref,
+    normed_landed, small_landed, front_own, output_own, *flags
 ):
     tokens = hidden_ref.shape[1]
-    shard = front_own.shape[0]
-    meet(("hd", "cp"), owners=True)
-
-    def over_cp(ref, landed, flags):
-        return Exchange("cp", lambda to: lead_rows(ref, to, shard), lambda at: landed.at[at], *flags)
-
-    def to_owner(ref, landed, flags):
-        return OwnerExchange(lambda piece: ref.at[piece], lambda at: landed.at[at], *flags)
-
-    groups = [flags[3 * n : 3 * n + 3] for n in range(10)]
+    meet(heads=True, chips=True, owners=True)
+    reduces = (
+        PairReduce(front_ref, *flags[:7], column_target, column_source),
+        PairReduce(output_ref, *flags[7:14], owner_target, owner_source),
+    )
     normed_move = Exchange(
         "hd",
         lambda to: token_rows(normed_part_ref, to, tokens),
         lambda at: normed_landed.at[at],
-        *groups[0],
-    )
-    weights = [
-        (to_owner(down_ref, down_landed, groups[1]), down_landed, down_own, down_all_ref),
-        (over_cp(ffn_ref, ffn_landed, groups[2]), ffn_landed, ffn_own, ffn_all_ref),
-        (to_owner(output_ref, output_landed, groups[3]), output_landed, output_own, output_all_ref),
-        (over_cp(front_ref, front_landed, groups[4]), front_landed, front_own, front_all_ref),
-    ]
-    small_move = Exchange(
-        "cp", lambda to: small_ref, lambda at: small_landed.at[at], *groups[5]
-    )
+        *flags[14:17],
+    )
+    small_move = PairGather(small_ref, lambda at: small_landed.at[at], *flags[17:20])
+    for move in reduces:
+        move.start()
     normed_move.start()
-    for move, _, _, _ in weights:
-        move.start()
+    for move in reduces:
+        move.add_pairs()
     small_move.start()
     spreads = []
-    for n, (move, landed, own, everywhere) in enumerate(weights):
-        move.arrive()
-        own[...] = added(landed).astype(bf16)
-        spread = Exchange(
-            "hd",
-            lambda to, own=own: own,
-            lambda at, everywhere=everywhere: everywhere.at[at],
-            *groups[6 + n],
-        )
-        spread.start()
-        spreads.append(spread)
+    for n, (move, own, everywhere) in enumerate(
+        zip(reduces, (front_own, output_own), (front_all_ref, output_all_ref))
+    ):
+        own[...] = move.total()
+        spreads.append(spread_piece(own, everywhere, flags[20 + 3 * n : 23 + 3 * n]))
     normed_move.arrive()
     back, _ = norm_back(hidden_ref[...].astype(f32), gain_ref[...], added(normed_landed))
     grad_in_ref[...] = (grad_middle_ref[...] + back).astype(bf16)
     small_move.arrive()
     small_sum_ref[...] = added(small_landed)
-    for move in (normed_move, small_move, *(entry[0] for entry in weights)):
+    for move in (normed_move, small_move, *reduces):
         move.leave()
     for spread in spreads:
         spread.arrive()
@@ -659,22 +896,6 @@
     devices = range(lax.axis_size(axis))
     route = [(i - distance, i) for i in devices if i - distance in devices]
     return lax.ppermute(block, axis, route)
-
-
-def head_rows(shard, place):
-    cp, hd = lax.axis_size("cp"), lax.axis_size("hd")
-    share = cp // hd
-    got = []
-    for turn in range(share):
-        route = [
-            (i * hd + j, (share * j + (turn + i) % share) * hd + i // share)
-            for i in range(cp)
-            for j in range(hd)
-        ]
-        got.append(lax.ppermute(shard, ("cp", "hd"), route))
-    stack = jnp.stack(got)
-    order = (place - jnp.arange(share)) % share
-    return jnp.take(stack, order, axis=0).reshape(share * shard.shape[0], shard.shape[1])
 
 
 def on_device(
@@ -731,12 +952,7 @@
         sems(hd, cp),
         1,
     )
-    output_part = head_rows(w_output, place)
-    ffn_full = lax.all_gather(
-        jnp.concatenate([ff_pad(w_ffn_gate), ff_pad(w_ffn_up)], 1), "cp", axis=0, tiled=True
-    )
-    down_part = jnp.pad(head_rows(w_ffn_down, place), ((0, ffp - ff), (0, 0)))
-    cot_all = lax.all_gather(cotangent, "hd", axis=1, tiled=True)
+    ffn_front = jnp.concatenate([ff_pad(w_ffn_gate), ff_pad(w_ffn_up)], 1)
 
     attn_gain = front_full[:, side + 2].astype(f32)
     ffn_gain = front_full[:, side + 3].astype(f32)
@@ -775,29 +991,46 @@
     flat = (sequences, span)
     aux = jnp.stack([beta_rows, survive.reshape(flat), rho.reshape(flat)], -1)
     aux = jnp.pad(aux, ((0, 0), (0, 0), (0, 5)))
-    prefix, segment, weighted, written, inverse = kernel_call(
-        maps_kernel,
-        (
-            shaped((sequences, blocks, dk, dk + dv)),
-            shaped((sequences, dk, dk + dv), bf16),
-            shaped((sequences, span, dk)),
-            shaped((sequences, span, dv)),
-            shaped((sequences, blocks, STRETCH, STRETCH)),
-        ),
-        key_rows, values, aux, between,
-    )
-    segments = gather_stack(segment, 2)
-    place_vec = place.reshape(1).astype(jnp.int32)
-    mixed, states, updates = kernel_call(
-        run_kernel,
+    chips = cp // CORES
+    share = cp // hd
+    (
+        mixed, states, updates, weighted, inverse, maps, both,
+        cot_all, ffn_full, output_part, down_part,
+    ) = comm_call(
+        forward_kernel,
         (
             shaped((sequences, span, dv), bf16),
             shaped((sequences, blocks, dk, dv)),
             shaped((sequences, span, dv)),
+            shaped((sequences, span, dk)),
+            shaped((sequences, blocks, STRETCH, STRETCH)),
+            shaped((chips, dk, dk + dv), bf16),
+            shaped((CORES, dk, dk + dv), bf16),
+            shaped((sequences, span, width), bf16),
+            shaped((width, 2 * ffp), bf16),
+            shaped((share * w_output.shape[0], width), bf16),
+            shaped((share * w_ffn_down.shape[0], width), bf16),
         ),
-        place_vec, segments, prefix, queries, key_rows, aux, between, weighted, written,
-        scalars=1,
-    )
+        ("vmem",) * 5 + ("any",) * 4,
+        (
+            queries, key_rows, values, aux, between, cotangent, ffn_front, w_output, w_ffn_down,
+        ),
+        ("vmem",) * 7 + ("any",) * 4,
+        [
+            pltpu.VMEM((sequences, blocks, dk, dk + dv), f32),
+            pltpu.VMEM((sequences, span, dv), f32),
+            pltpu.VMEM((sequences, dk, dk + dv), bf16),
+            pltpu.VMEM((dk, dk + dv), bf16),
+            pltpu.VMEM((sequences, dk, dv), f32),
+            pltpu.VMEM((dk, dv), f32),
+            pltpu.SemaphoreType.DMA((4,)),
+            *sems(cp, share, share, hd),
+            pltpu.SemaphoreType.DMA((chips,)),
+            pltpu.SemaphoreType.DMA((chips,)),
+        ],
+        2,
+    )
+    down_part = jnp.pad(down_part, ((0, ffp - ff), (0, 0)))
     mixed_float = mixed.astype(f32)
     normed_head, gated_pull = jax.vjp(gated_norm, mixed_float, gate_pre, head_gain)
     normed_head = normed_head.astype(bf16)
@@ -844,38 +1077,55 @@
 
     def pieces(grad):
         rows = grad.shape[0] // cp
-        split = grad.reshape(cp, rows, width)
-        return jnp.pad(split, ((0, 0), (0, -rows % 16), (0, 0))).astype(bf16)
-
-    grad_ffn = weight_grad(ffn_all, grad_gate_up).astype(bf16)
+        split = grad.reshape(chips, CORES, rows, width)
+        return jnp.pad(split, ((0, 0), (0, 0), (0, -rows % 16), (0, 0))).astype(bf16)
+
+    def by_owner(grad):
+        return grad.reshape(chips, CORES, shard, grad.shape[1]).astype(bf16)
+
+    grad_ffn = by_owner(weight_grad(ffn_all, grad_gate_up))
     grad_down = pieces(weight_grad(inner, cot_all)[:ff])
 
     grad_normed_head = dot(grad_attention, output_part, "std,ed->ste")
     grad_output = pieces(weight_grad(normed_head, grad_attention))
     grad_mixed, grad_gate_pre, grad_head_gain = gated_pull(grad_normed_head)
     grad_mixed = grad_mixed.astype(bf16)
-    through, inflow, local = kernel_call(
-        back_local_kernel,
-        (
-            shaped((sequences, span, dv)),
-            shaped((sequences, blocks, dk, dv)),
-            shaped((sequences, dk, dv), bf16),
-        ),
-        queries, key_rows, aux, between, weighted, grad_mixed,
-    )
-    locals_all = gather_stack(local, 3)
-    grad_q, grad_k, grad_v, grad_aux, grad_row = kernel_call(
-        back_kernel,
+    ffn_share, down_share = (entry.shape[2:] for entry in (grad_ffn, grad_down))
+    grad_q, grad_k, grad_v, grad_aux, grad_row, grad_ffn, grad_down = comm_call(
+        backward_kernel,
         (
             shaped((sequences, span, dk)),
             shaped((sequences, span, dk)),
             shaped((sequences, span, dv)),
             shaped((sequences, span, 8)),
             shaped((sequences, blocks, STRETCH)),
+            shaped((hd, *ffn_share), bf16),
+            shaped((hd, *down_share), bf16),
         ),
-        place_vec, segments, locals_all, queries, key_rows, values, aux, between, weighted,
-        inverse, states, updates, grad_mixed, through, inflow,
-        scalars=1,
+        ("vmem",) * 14,
+        (
+            queries, key_rows, values, aux, between, weighted, inverse, states, updates,
+            grad_mixed, maps, both, grad_ffn, grad_down,
+        ),
+        ("vmem",) * 5 + ("any",) * 2,
+        [
+            pltpu.VMEM((sequences, span, dv), f32),
+            pltpu.VMEM((sequences, blocks, dk, dv), f32),
+            pltpu.VMEM((sequences, dk, dv), bf16),
+            pltpu.VMEM((dk, dv), bf16),
+            pltpu.VMEM((chips, dk, dv), bf16),
+            pltpu.VMEM((sequences, dk, dv), f32),
+            pltpu.VMEM((dk, dv), f32),
+            pltpu.VMEM(ffn_share, bf16),
+            pltpu.VMEM(down_share, bf16),
+            pltpu.SemaphoreType.DMA((4,)),
+            pltpu.SemaphoreType.DMA((chips,)),
+            pltpu.SemaphoreType.DMA((chips,)),
+            *reduce_scratch(grad_ffn),
+            *reduce_scratch(grad_down),
+            *sems(hd, hd),
+        ],
+        3,
     )
     grad_cumulative = grad_aux[:, :, 1].reshape(sequences, blocks, STRETCH) - grad_row
     grad_ext, grad_decay, grad_beta, grad_taps, grad_log, grad_bias = prepare_pull(
@@ -912,20 +1162,30 @@
         0,
     )
     small = jnp.pad(small, ((0, -small.shape[0] % 8), (0, 0)))
-    weight_parts = (grad_front.astype(bf16), grad_ffn, grad_output, grad_down)
-    shares = ((shard, grad_front.shape[1]), (shard, 2 * ffp), grad_output.shape[1:], grad_down.shape[1:])
-    grad_in, grad_front, grad_ffn, grad_output, grad_down, small = comm_call(
+    grad_front = by_owner(grad_front)
+    front_share, output_share = (entry.shape[2:] for entry in (grad_front, grad_output))
+    grad_in, grad_front, grad_output, small = comm_call(
         close_kernel,
-        (shaped(hidden_in.shape, bf16), *(shaped((hd, *share), bf16) for share in shares), shaped(small.shape)),
-        ("any",) * 6 + ("vmem",) * 3,
-        (partial_normed.astype(bf16), *weight_parts, small, hidden_in, grad_middle, attn_gain[None]),
-        ("vmem",) + ("any",) * 4 + ("vmem",),
+        (
+            shaped(hidden_in.shape, bf16),
+            shaped((hd, *front_share), bf16),
+            shaped((hd, *output_share), bf16),
+            shaped(small.shape),
+        ),
+        ("any", "vmem", "vmem", "any") + ("vmem",) * 3,
+        (
+            partial_normed.astype(bf16), grad_front, grad_output, small, hidden_in, grad_middle,
+            attn_gain[None],
+        ),
+        ("vmem", "any", "any", "vmem"),
         [
             landing,
-            *(pltpu.VMEM((cp, *share), bf16) for share in shares),
             pltpu.VMEM((cp, *small.shape), f32),
-            *(pltpu.VMEM(share, bf16) for share in shares),
-            *sems(hd, cp, cp, cp, cp, cp, hd, hd, hd, hd),
+            pltpu.VMEM(front_share, bf16),
+            pltpu.VMEM(output_share, bf16),
+            *reduce_scratch(grad_front),
+            *reduce_scratch(grad_output),
+            *sems(hd, cp, hd, hd),
         ],
         6,
     )

time: 757 us -> 597 us (0.79)
  Pallas kernels: 589 us -> 476 us
  between operations: 17.4 us -> 3.87 us
  matrix products: 39.2 us -> 29.7 us
  starting transfers between devices: 12.9 us -> 3.86 us
    pallas_call x4 -> x0, Pallas kernels: 100 us -> none  [kernel_call(): pl.pallas_call(body, out_shape=out_shape, in_specs=[pl.BlockSpec(memory_s...]
    pallas_call x6, Pallas kernels: 488 us -> 476 us  [comm_call(): pl.pallas_call(body, out_shape=out_shape, in_specs=[pl.BlockSpec(memory_s...]
    dot_general x12, matrix products: 39.2 us -> 29.7 us  [dot(): return jnp.einsum(spec, a, b, preferred_element_type=f32)]
    unnamed x103 -> x91, local copies, waits for them, and re-layouts: 21.7 us -> 12.2 us
    ppermute x4 -> x0, starting transfers between devices: 9.28 us -> none  [head_rows(): got.append(lax.ppermute(shard, ('cp', 'hd'), route))]
  transfers between devices with their start and end apart: 8 -> 2, of which waited for: 0 -> 0; matrix products, arithmetic and copies ran while one was open for 6% -> 3% of each run, Pallas kernels for 35% -> 0%
where the time goes in v2:
time: 597 us; the launch traced here: 589 us
  Pallas kernels  476 us (80%)
  local copies, waits for them, and re-layouts  49 us (8%)
  matrix products  29.7 us (5%)
  other arithmetic  26.3 us (4%)
    pallas_call x6, Pallas kernels, comm_call(): pl.pallas_call(body, out_shape=out_shape, in_specs=[pl.BlockSpec(memory_s...  476 us
    dot_general x12, matrix products, dot(): return jnp.einsum(spec, a, b, preferred_element_type=f32)  29.7 us
    unnamed x91, local copies, waits for them, and re-layouts  12.2 us
  transfers between devices with their start and end apart: 2, of which 0 were waited for; matrix products, arithmetic and copies ran while one was open for 3% of the time, Pallas kernels for 0%

profile of v2, /device:TPU:8, one launch (start us, length us, event | category | flops | bytes accessed | tf_op | source)
XLA Modules:
  0.0 588.7 jit_solution(4998826899467411183)
XLA Ops:
  5.9 0.9 copy-done
  6.8 42.6 %shard_map.356 = (bf16[2,512,1024]{2,1,0:T(8,128)(2,1)S(1)}, bf16[1024,896]{1,0:T(8,128)(2,1)S(1)}) custom-call(bf16[2,64,1024]{2,1,0:T(8,128)(2,1)S(1)} %copy-done, bf16[64,896]{1,0:T(8,128)(2,1)S(1)} %pad_dynamic-update-slice_fusion.front_ref), custom_call_target="tpu_custom_call" | custom-call | tf_op jit(solution)/shard_map/pallas_call | solution.py:591
  50.4 4.2 fusion.75
  54.6 2.4 collective-permute-start
  59.3 1.2 fusion.49
  62.6 1.1 constant_dynamic-slice_fusion
  64.7 2.6 fusion.7
  67.7 1.1 slice.259.v_ref
  69.4 108.6 %shard_map.357 = (bf16[2,512,256]{2,1,0:T(8,128)(2,1)S(1)}, f32[2,8,128,256]{3,2,1,0:T(8,128)}, f32[2,512,256]{2,1,0:T(8,128)}, f32[2,512,128]{2,1,0:T(8,128)S(1...) custom-call(f32[2,512,128]{2,1,0:T(8,128)S(1)} %get-tuple-element.13, ...), custom_call_target="tpu_custom_call" | custom-call | tf_op jit(solution)/shard_map/pallas_call | solution.py:591
  180.0 75.2 %shard_map.358 = (f32[2,64,1024]{2,1,0:T(8,128)S(1)}, bf16[2,512,1024]{2,1,0:T(8,128)(2,1)S(1)}) custom-call(bf16[2,512,1024]{2,1,0:T(8,128)(2,1)S(1)} %convolution_convert_fusion.1.partial_ref, bf16[2,64,1024]{2,1,0:T(8,128)(2,1)S(1)} %copy-done.1, f32[1,1024]{1,0:T(1,128)S(1)} %bitcast.110), custom_call_target="tpu_custom_call" | custom-call | tf_op jit(solution)/shard_map/pallas_call | solution.py:591
  255.3 1.8 fusion.17
  257.1 1.8 fusion.53
  258.9 3.1 bitcast_convert_fusion.1
  261.9 3.2 convolution_convert_fusion.2.grad_part_ref
  265.1 1.0 convolution_bitcast_fusion
  266.1 1.2 convolution_convert_fusion.out_part_ref
  267.4 82.3 %shard_map.359 = (bf16[2,64,1024]{2,1,0:T(8,128)(2,1)S(1)}, f32[2,64,1024]{2,1,0:T(8,128)S(1)}, f32[1,1024]{1,0:T(1,128)S(1)}, bf16[2,512,1024]{2,1,0:T(8,128)(2,1)S(1)}) custom-call(bf16[2,512,1024]{2,1,0:T(8,128)(2,1)S(1)} %convolution_convert_fusion.out_part_ref, bf16[2,512,1024]{2,1,0:T(8,128)(2,1)} %convolution_convert_fusion.2.grad_part_ref, ...), custom_call_target="tpu_custom_call" | custom-call | tf_op jit(solution)/shard_map/pallas_call | solution.py:591
  349.7 1.9 fusion.20
  351.6 2.5 fusion.26
  354.1 0.9 slice.338
  355.0 2.1 reshape.310
  357.1 2.4 pad.95.down_ref
  359.5 1.6 fusion.27.grad_ref
  361.1 89.7 %shard_map.360 = (f32[2,512,128]{2,1,0:T(8,128)S(1)}, f32[2,512,128]{2,1,0:T(8,128)S(1)}, f32[2,512,256]{2,1,0:T(8,128)}, f32[2,512,8]{2,1,0:T(8,128)S(1)}, f32[...) custom-call(f32[2,512,128]{2,1,0:T(8,128)S(1)} %get-tuple-element.130.q_ref, ...), custom_call_target="tpu_custom_call" | custom-call | tf_op jit(solution)/shard_map/pallas_call | solution.py:591
  453.4 2.1 multiply_reduce_fusion.3
  456.2 1.3 copy-done.19
  459.5 2.1 pad_add_fusion
  461.6 1.4 slice_reduce_fusion
  464.4 2.2 fusion.69
  467.4 2.2 convert_bitcast_fusion
  469.6 1.5 collective-permute-start.1
  471.1 0.9 fusion.50
  472.7 1.1 concatenate.52
  473.9 0.9 copy.215
  474.9 0.9 reshape.328
  475.8 1.6 copy.223
  477.4 1.1 reshape.327
  479.0 1.1 reshape.326
  480.1 1.2 slice.269
  482.9 1.3 scatter-add.4
  484.2 5.9 fusion.3
  490.1 2.4 bitcast_convert_fusion
  492.7 1.1 concatenate.51
  494.7 2.4 copy.211
  497.1 3.9 concatenate.49.front_ref
  501.0 77.6 %shard_map.361 = (bf16[2,64,1024]{2,1,0:T(8,128)(2,1)S(1)}, bf16[8,64,896]{2,1,0:T(8,128)(2,1)S(1)}, bf16[8,16,1024]{2,1,0:T(8,128)(2,1)S(1)}, f32[8,512]{1,0:T(8,128)S(1)}) custom-call(bf16[2,512,1024]{2,1,0:T(8,128)(2,1)} %get-tuple-element.121.normed_part_ref, bf16[8,2,64,896]{3,2,1,0:T(8,128)(2,1)S(1)} %concatenate.49.front_ref, ...), custom_call_target="tpu_custom_call" | custom-call | tf_op jit(solution)/shard_map/pallas_call | solution.py:591
  580.3 0.9 bitcast_reduce_fusion
  582.9 0.9 bitcast_convert_fusion.2
  (170 shorter events, 31.5 us)
Async XLA Ops:
  5.9 1.0 copy-start
  49.4 5.1 copy-start.2
  49.4 7.5 %copy-start.11 = (bf16[1024,896]{1,0:T(8,128)(2,1)}, bf16[1024,896]{1,0:T(8,128)(2,1)S(1)}, u32[]{:S(2)}) copy-start(bf16[1024,896]{1,0:T(8,128)(2,1)S(1)} %get-tuple-element.63) | copy-start | bytes 5505028
  50.3 8.5 %copy-start.34 = (s32[2,8192]{1,0:T(2,128)S(1)}, s32[2,8192]{1,0:T(2,128)}, u32[]{:S(2)}) copy-start(s32[2,8192]{1,0:T(2,128)} %param.24) | copy-start | bytes 196612
  50.3 8.9 %copy-start.37 = (bf16[4,256]{1,0:T(4,128)(2,1)S(1)}, bf16[4,256]{1,0:T(4,128)(2,1)}, u32[]{:S(2)}) copy-start(bf16[4,256]{1,0:T(4,128)(2,1)} %param.37) | copy-start | bytes 6148
  50.3 8.9 %copy-start.38 = (bf16[4,128]{1,0:T(4,128)(2,1)S(1)}, bf16[4,128]{1,0:T(4,128)(2,1)}, u32[]{:S(2)}) copy-start(bf16[4,128]{1,0:T(4,128)(2,1)} %param.36) | copy-start | bytes 3076
  50.3 8.9 %copy-start.39 = (bf16[4,128]{1,0:T(4,128)(2,1)S(1)}, bf16[4,128]{1,0:T(4,128)(2,1)}, u32[]{:S(2)}) copy-start(bf16[4,128]{1,0:T(4,128)(2,1)} %param.35) | copy-start | bytes 3076
  54.5 2.7 copy-start.29
  54.6 9.8 %collective-permute-start = (bf16[2,3,512]{2,1,0:T(4,128)(2,1)S(1)}, bf16[2,3,512]{2,1,0:T(4,128)(2,1)S(1)}, u32[]{:S(2)}, u32[]{:S(2)}) collective-permute-start(bf16[2,3,512]{2,1,0:T(4,128)(2,1)S(1)} %slice.248), channel_id=1, source_target_pairs={{0,8},{8,16},{16,24},{24,32},{32,40},{40,48},{48,56},{56,64},{64,7... | collective-permute-start | bytes 18440 | tf_op jit(solution)/shard_map/ppermute | solution.py:898
  62.6 1.6 copy-start.30
  64.7 2.6 copy-start.17
  67.3 1.9 copy-start.24
  67.6 1.5 copy-start.4
  67.6 1.5 copy-start.10
  67.6 1.8 copy-start.12
  69.4 109.5 %copy-start.36 = (f32[2,512,896]{2,1,0:T(8,128)S(1)}, f32[2,512,896]{2,1,0:T(8,128)}, u32[]{:S(2)}) copy-start(f32[2,512,896]{2,1,0:T(8,128)} %get-tuple-element.153) | copy-start | bytes 11010052
  178.0 0.7 copy-start.15
  178.7 1.1 copy-start.6
  178.7 1.1 copy-start.8
  179.0 1.1 copy-start.1
  179.8 75.4 %copy-start.40 = (bf16[1024,768]{1,0:T(8,128)(2,1)S(1)}, bf16[1024,768]{1,0:T(8,128)(2,1)}, u32[]{:S(2)}) copy-start(bf16[1024,768]{1,0:T(8,128)(2,1)} %get-tuple-element.67) | copy-start | bytes 4718596
  255.3 1.8 copy-start.28
  349.7 1.9 copy-start.13
  357.1 4.0 copy-start.7
  357.1 4.0 copy-start.9
  357.1 4.0 copy-start.16
  361.1 89.7 %copy-start.25 = (f32[2,512,512]{2,1,0:T(8,128)S(1)}, f32[2,512,512]{2,1,0:T(8,128)}, u32[]{:S(2)}) copy-start(f32[2,512,512]{2,1,0:T(8,128)} %copy-done.24) | copy-start | bytes 6291460
  450.8 1.6 copy-start.26
  451.2 1.9 copy-start.18
  451.2 2.2 copy-start.31
  456.2 1.4 copy-start.19
  456.2 2.0 copy-start.21
  456.2 2.8 copy-start.22
  456.2 3.3 copy-start.23
  469.6 11.8 %collective-permute-start.1 = (f32[2,3,512]{2,1,0:T(4,128)S(1)}, f32[2,3,512]{2,1,0:T(4,128)S(1)}, u32[]{:S(2)}, u32[]{:S(2)}) collective-permute-start(f32[2,3,512]{2,1,0:T(4,128)S(1)} %pad_add_fusion.1), channel_id=1, source_target_pairs={{8,0},{16,8},{24,16},{32,24},{40,32},{48,40},{56,48},{64,56},{72,6... | collective-permute-start | bytes 36872 | tf_op jit(solution)/shard_map/ppermute | solution.py:898
  477.4 2.7 copy-start.27
  480.1 2.0 copy-start.20
  481.3 2.9 copy-start.3
  481.3 2.9 copy-start.35
  484.2 5.9 copy-start.33
  484.2 5.9 copy-start.41
  492.7 4.4 copy-start.32
  497.1 3.9 copy-start.5
  582.9 4.0 copy-start.14

commit v3 on v2

--- a/solution.py
+++ b/solution.py
@@ -30,7 +30,9 @@
     return pl.ds(pl.multiple_of(n * STRETCH, STRETCH), STRETCH)
 
 
-def segment_maps(k_ref, v_ref, aux_ref, between_ref, x_ref, end_ref, w_ref, u_ref, inv_ref):
+def segment_maps(
+    k_ref, v_ref, aux_ref, between_ref, x_ref, end_ref, w_ref, u_ref, inv_ref, halfway
+):
     sequences, length, dk = k_ref.shape
     dv = v_ref.shape[2]
     blocks = length // STRETCH
@@ -58,7 +60,9 @@
             u_ref[s, rows] = mm(inverse, beta * v_ref[s, rows])
         return carry
 
-    lax.fori_loop(0, blocks // 2, prepare_block, 0)
+    lax.fori_loop(0, blocks // 4, prepare_block, 0)
+    halfway()
+    lax.fori_loop(blocks // 4, blocks // 2, prepare_block, 0)
 
     wide = (dk, dk + dv)
     start = (
@@ -269,21 +273,29 @@
     lax.fori_loop(1, count, step, 0)
 
 
+def far_devices(axis, action):
+    count, me = lax.axis_size(axis) // CORES, lax.axis_index(axis)
+    group, place = me // CORES, lax.rem(me, CORES)
+
+    def step(distance, carry):
+        ahead, behind = lax.rem(group + distance, count), lax.rem(group + count - distance, count)
+        action(distance, ahead * CORES + place, behind * CORES + place)
+        return carry
+
+    lax.fori_loop(1, count, step, 0)
+
+
 def chip_devices(action):
-    count, me = lax.axis_size("cp") // CORES, lax.axis_index("cp")
-    chip, core = me // CORES, lax.rem(me, CORES)
-
-    def step(distance, carry):
-        ahead, behind = lax.rem(chip + distance, count), lax.rem(chip + count - distance, count)
-        action(distance, ahead * CORES + core, behind * CORES + core)
-        return carry
-
-    lax.fori_loop(1, count, step, 0)
+    far_devices("cp", action)
+
+
+def near(axis):
+    me = lax.axis_index(axis)
+    return me + 1 - 2 * lax.rem(me, CORES)
 
 
 def sibling():
-    me = lax.axis_index("cp")
-    return me + 1 - 2 * lax.rem(me, CORES)
+    return near("cp")
 
 
 def owner_target(turn):
@@ -304,8 +316,8 @@
 
 
 def row_target(turn):
-    share = lax.axis_size("cp") // lax.axis_size("hd")
-    return share * lax.axis_index("hd") + turn, lax.axis_index("cp") // share
+    me = lax.axis_index("cp")
+    return CORES * lax.axis_index("hd") + lax.rem(me, CORES), me // CORES
 
 
 def is_me(at):
@@ -339,7 +351,7 @@
         total += cp // CORES
     for wanted, count, source_of, target_of in (
         (owners, cp // CORES, owner_source, owner_target),
-        (rows, cp // hd, row_target, row_target),
+        (rows, 1, row_target, row_target),
     ):
         if wanted:
 
@@ -409,42 +421,61 @@
 
 
 class PairGather:
-    def __init__(self, source, landing, send, recv, local):
+    def __init__(self, axis, source, landing, send, recv, local, near_first=False):
+        self.axis, self.near_first = axis, near_first
         self.source, self.landing, self.send, self.recv = source, landing, send, recv
-        self.me = lax.axis_index("cp")
-        self.count = lax.axis_size("cp") // CORES
+        self.me, self.near = lax.axis_index(axis), near(axis)
+        self.count = lax.axis_size(axis) // CORES
         self.own = pltpu.make_async_copy(source, landing(self.me), local)
 
     def copy(self, block, index, slot, to):
         return remote(
-            block, self.landing(index), self.send.at[slot], self.recv.at[index], {"cp": to}
+            block, self.landing(index), self.send.at[slot], self.recv.at[index], {self.axis: to}
         )
 
+    def far(self, action):
+        far_devices(self.axis, action)
+
     def start(self):
-        chip_devices(lambda d, to, source: self.copy(self.source, self.me, d, to).start())
-        self.copy(self.source, self.me, 0, sibling()).start()
+        self.copy(self.source, self.me, 0, self.near).start()
+        self.far(lambda d, to, source: self.copy(self.source, self.me, d, to).start())
         self.own.start()
 
+    def hand_on(self):
+        if self.near_first:
+            self.copy(self.source, self.near, 0, self.near).wait_recv()
+            self.far(
+                lambda d, to, source: self.copy(
+                    self.landing(self.near), self.near, self.count + d, to
+                ).start()
+            )
+        else:
+
+            def pass_far(d, to, source):
+                self.copy(self.source, source, d, to).wait_recv()
+                self.copy(self.landing(source), source, self.count + d, self.near).start()
+
+            self.far(pass_far)
+
     def arrive(self):
-        def hand_on(d, to, source):
-            self.copy(self.source, source, d, to).wait_recv()
-            self.copy(self.landing(source), source, self.count + d, sibling()).start()
-
-        chip_devices(hand_on)
-        other = sibling()
-        self.copy(self.source, other, 0, other).wait_recv()
-        shift = other - self.me
-        chip_devices(
-            lambda d, to, source: self.copy(self.source, source + shift, d, other).wait_recv()
+        shift = self.near - self.me
+        if self.near_first:
+            self.far(lambda d, to, source: self.copy(self.source, source, d, to).wait_recv())
+        else:
+            self.copy(self.source, self.near, 0, self.near).wait_recv()
+        self.far(
+            lambda d, to, source: self.copy(
+                self.source, source + shift, d, self.near
+            ).wait_recv()
         )
         self.own.wait()
 
     def leave(self):
-        chip_devices(lambda d, to, source: self.copy(self.source, self.me, d, to).wait_send())
-        self.copy(self.source, self.me, 0, sibling()).wait_send()
-        chip_devices(
+        self.copy(self.source, self.me, 0, self.near).wait_send()
+        self.far(lambda d, to, source: self.copy(self.source, self.me, d, to).wait_send())
+        self.far(
             lambda d, to, source: self.copy(
-                self.source, source, self.count + d, sibling()
+                self.source, source, self.count + d, self.near
             ).wait_send()
         )
 
@@ -521,47 +552,48 @@
 class RowMove:
     def __init__(self, rows, landing, send, recv, local):
         self.rows, self.send, self.recv, self.local = rows, send, recv, local
-        self.count = lax.axis_size("cp") // lax.axis_size("hd")
-        self.slot = lax.rem(lax.axis_index("cp"), self.count)
+        self.slot = lax.rem(lax.axis_index("cp"), CORES)
         self.landing = lambda slot: lead_rows(landing, slot, rows.shape[0])
-
-    def copy(self, turn, slot, to):
-        return remote(self.rows, self.landing(slot), self.send.at[turn], self.recv.at[slot], to)
-
-    def kept(self):
-        return pltpu.make_async_copy(self.rows, self.landing(self.slot), self.local)
+        self.to = row_target(0)
+        self.own = is_me(self.to)
+        self.move = remote(self.rows, self.landing(self.slot), send.at[0], recv.at[0], self.to)
+        self.kept = pltpu.make_async_copy(rows, self.landing(self.slot), local)
+
+    def shared(self, slot):
+        return remote(
+            self.landing(self.slot), self.landing(slot), self.send.at[1], self.recv.at[1],
+            {"cp": sibling()},
+        )
 
     def start(self):
-        def go(turn):
-            to = row_target(turn)
-
-            @pl.when(is_me(to))
-            def _():
-                self.kept().start()
-
-            @pl.when(jnp.logical_not(is_me(to)))
-            def _():
-                self.copy(turn, self.slot, to).start()
-
-        each(self.count, go)
+        @pl.when(self.own)
+        def _():
+            self.kept.start()
+
+        @pl.when(jnp.logical_not(self.own))
+        def _():
+            self.move.start()
+
+    def hand_on(self):
+        @pl.when(self.own)
+        def _():
+            self.kept.wait()
+
+        @pl.when(jnp.logical_not(self.own))
+        def _():
+            self.move.wait_recv()
+
+        self.shared(self.slot).start()
 
     def arrive(self):
-        def get(turn):
-            at = row_target(turn)
-
-            @pl.when(is_me(at))
-            def _():
-                self.kept().wait()
-
-            @pl.when(jnp.logical_not(is_me(at)))
-            def _():
-                self.copy(turn, turn, at).wait_recv()
-                self.copy(turn, turn, at).wait_send()
-
-        each(self.count, get)
+        self.shared(1 - self.slot).wait_recv()
 
     def leave(self):
-        pass
+        self.shared(self.slot).wait_send()
+
+        @pl.when(jnp.logical_not(self.own))
+        def _():
+            self.move.wait_send()
 
 
 def sems(*counts):
@@ -604,14 +636,17 @@
     tokens, shard = hidden_ref.shape[1], front_ref.shape[0]
     meet(heads=True, chips=True)
     moves = (
-        Exchange(
-            "hd", lambda to: hidden_ref, lambda at: token_rows(hidden_all_ref, at, tokens), *flags[:3]
+        PairGather(
+            "hd", hidden_ref, lambda at: token_rows(hidden_all_ref, at, tokens), *flags[:3],
+            near_first=True,
         ),
-        PairGather(front_ref, lambda at: lead_rows(front_all_ref, at, shard), *flags[3:6]),
+        PairGather("cp", front_ref, lambda at: lead_rows(front_all_ref, at, shard), *flags[3:6]),
     )
     for move in moves:
         move.start()
-    for move in reversed(moves):
+    for move in moves:
+        move.hand_on()
+    for move in moves:
         move.arrive()
         move.leave()
 
@@ -634,16 +669,21 @@
     early = core == 0
     meet(heads=True, chips=True, rows=True)
     carried = (
-        PairGather(ffn_ref, lambda at: lead_rows(ffn_all_ref, at, shard), *flags[:3]),
         RowMove(output_ref, output_part_ref, *flags[3:6]),
         RowMove(down_ref, down_part_ref, *flags[6:9]),
-        Exchange(
-            "hd", lambda to: cot_ref, lambda at: token_rows(cot_all_ref, at, tokens), *flags[9:12]
-        ),
-    )
-    for move in carried:
+        PairGather("cp", ffn_ref, lambda at: lead_rows(ffn_all_ref, at, shard), *flags[:3]),
+    )
+    cot_move = PairGather(
+        "hd", cot_ref, lambda at: token_rows(cot_all_ref, at, tokens), *flags[9:12],
+        near_first=True,
+    )
+    cot_move.start()
+    for move in reversed(carried):
         move.start()
-    segment_maps(k_ref, v_ref, aux_ref, between_ref, x_ref, own_ref, w_ref, u_ref, inv_ref)
+    segment_maps(
+        k_ref, v_ref, aux_ref, between_ref, x_ref, own_ref, w_ref, u_ref, inv_ref,
+        cot_move.hand_on,
+    )
     swap = remote(
         own_ref.at[1 - core], other_ref, pair_sems.at[0], pair_sems.at[1], {"cp": sibling()}
     )
@@ -656,7 +696,10 @@
     pair = mm(second[:, :dk], first)
     pair = jnp.concatenate([pair[:, :dk], pair[:, dk:] + second[:, dk:]], 1)
     maps_ref[chip] = pair.astype(bf16)
-    spread_chips(maps_ref, flags[12], flags[13])
+    settle = spread_chips(maps_ref, flags[12], flags[13])
+    for move in carried:
+        move.hand_on()
+    settle()
 
     def enter(hop, state):
         return mm(maps_ref[hop, :, :dk].astype(f32), state) + maps_ref[hop, :, dk:].astype(f32)
@@ -676,9 +719,8 @@
         entry_ref, x_ref, q_ref, k_ref, aux_ref, between_ref, w_ref, u_ref,
         mixed_ref, state_ref, update_ref,
     )
-    for move in carried:
+    for move in (*carried, cot_move):
         move.arrive()
-    for move in carried:
         move.leave()
 
 
@@ -689,16 +731,22 @@
         return remote(ref.at[index], ref.at[index], send.at[distance], recv.at[distance], {"cp": to})
 
     chip_devices(lambda d, to, source: copy(d, chip, to).start())
-    chip_devices(lambda d, to, source: copy(d, source // CORES, to).wait_recv())
-    chip_devices(lambda d, to, source: copy(d, chip, to).wait_send())
+
+    def settle():
+        chip_devices(lambda d, to, source: copy(d, source // CORES, to).wait_recv())
+        chip_devices(lambda d, to, source: copy(d, chip, to).wait_send())
+
+    return settle
 
 
 def backward_kernel(
     q_ref, k_ref, v_ref, aux_ref, between_ref, w_ref, inv_ref, state_ref, update_ref, grad_ref,
-    maps_ref, both_ref, ffn_ref, down_ref,
+    maps_ref, both_ref, ffn_ref, down_ref, output_ref, out_part_ref, middle_ref,
     grad_q_ref, grad_k_ref, grad_v_ref, grad_aux_ref, grad_row_ref, ffn_all_ref, down_all_ref,
+    output_all_ref, block_ref,
     through_ref, inflow_ref, own_ref, other_ref, locals_ref, exit_ref, give_ref,
-    ffn_own_ref, down_own_ref, pair_sems, chip_send, chip_recv, *flags
+    ffn_own_ref, down_own_ref, output_own_ref, out_landed_ref, pair_sems, chip_send, chip_recv,
+    *flags
 ):
     sequences, length, dk = k_ref.shape
     dv = v_ref.shape[2]
@@ -710,8 +758,16 @@
     reduces = (
         PairReduce(ffn_ref, *flags[:7], column_target, column_source),
         PairReduce(down_ref, *flags[7:14], owner_target, owner_source),
-    )
-    for move in reduces:
+        PairReduce(output_ref, *flags[14:21], owner_target, owner_source),
+    )
+    tokens = middle_ref.shape[1]
+    out_move = Exchange(
+        "hd",
+        lambda to: token_rows(out_part_ref, to, tokens),
+        lambda at: out_landed_ref.at[at],
+        *flags[30:33],
+    )
+    for move in (*reduces, out_move):
         move.start()
     segment_local(
         q_ref, k_ref, aux_ref, between_ref, w_ref, grad_ref, through_ref, inflow_ref, own_ref
@@ -724,9 +780,10 @@
     mine, theirs = own_ref[core].astype(f32), other_ref[...].astype(f32)
     first, second = jnp.where(late, theirs, mine), jnp.where(late, mine, theirs)
     locals_ref[chip] = (mm(both_ref[0, :, :dk].astype(f32), second, 0, 0) + first).astype(bf16)
-    spread_chips(locals_ref, chip_send, chip_recv)
+    settle = spread_chips(locals_ref, chip_send, chip_recv)
     for move in reduces:
         move.add_pairs()
+    settle()
 
     def leave(hop, state):
         source = chips - 1 - hop
@@ -753,12 +810,20 @@
     exits = back_blocks(0, blocks // 2, exits, *refs)
     spreads = []
     for n, (move, own, everywhere) in enumerate(
-        zip(reduces, (ffn_own_ref, down_own_ref), (ffn_all_ref, down_all_ref))
+        zip(
+            reduces,
+            (ffn_own_ref, down_own_ref, output_own_ref),
+            (ffn_all_ref, down_all_ref, output_all_ref),
+        )
     ):
         own[...] = move.total()
-        spreads.append(spread_piece(own, everywhere, flags[14 + 3 * n : 17 + 3 * n]))
+        spreads.append(spread_piece(own, everywhere, flags[21 + 3 * n : 24 + 3 * n]))
+    out_move.arrive()
+    block_ref[...] = (middle_ref[...] + added(out_landed_ref)).astype(bf16)
+    for spread in spreads:
+        spread.hand_on()
     back_blocks(blocks // 2, blocks - blocks // 2, exits, *refs)
-    for move in reduces:
+    for move in (*reduces, out_move):
         move.leave()
     for spread in spreads:
         spread.arrive()
@@ -770,7 +835,7 @@
 
 
 def spread_piece(own, everywhere, flags):
-    spread = Exchange("hd", lambda to: own, lambda at: everywhere.at[at], *flags)
+    spread = PairGather("hd", own, lambda at: everywhere.at[at], *flags, near_first=True)
     spread.start()
     return spread
 
@@ -783,9 +848,27 @@
 
 
 def spread_own(own_ref, all_ref, tokens, flags):
-    move = Exchange("hd", lambda to: own_ref, lambda at: token_rows(all_ref, at, tokens), *flags)
-    move.start()
-    return move
+    moves = [
+        PairGather(
+            "hd",
+            own_ref.at[s],
+            lambda at, s=s: all_ref.at[s, pl.ds(pl.multiple_of(at * tokens, tokens), tokens)],
+            *flags[3 * s : 3 * s + 3],
+            near_first=s % 2 == 0,
+        )
+        for s in range(own_ref.shape[0])
+    ]
+    for move in moves:
+        move.start()
+    return moves
+
+
+def settle_all(moves):
+    for move in moves:
+        move.hand_on()
+    for move in moves:
+        move.arrive()
+        move.leave()
 
 
 def middle_kernel(
@@ -801,10 +884,9 @@
     middle = hidden_ref[...].astype(f32) + added(landed_ref)
     middle_ref[...] = middle
     own_ref[...] = norm_gain(middle, gain_ref[...]).astype(bf16)
-    after = spread_own(own_ref, ffn_all_ref, tokens, flags[3:6])
+    after = spread_own(own_ref, ffn_all_ref, tokens, flags[3:])
+    settle_all(after)
     move.leave()
-    after.arrive()
-    after.leave()
 
 
 def norm_back(source, gain_vec, grad):
@@ -815,81 +897,61 @@
 
 
 def ffn_back_kernel(
-    out_part_ref, grad_part_ref, middle_ref, cot_ref, gain_ref,
-    block_ref, grad_middle_ref, grad_gain_ref, grad_all_ref,
-    out_landed_ref, grad_landed_ref, own_ref, *flags
+    grad_part_ref, middle_ref, cot_ref, gain_ref,
+    grad_middle_ref, grad_gain_ref, grad_all_ref, grad_landed_ref, own_ref, *flags
 ):
     tokens = middle_ref.shape[1]
     meet(heads=True)
-    moves = [
-        Exchange(
-            "hd",
-            lambda to, ref=ref: token_rows(ref, to, tokens),
-            lambda at, landed=landed: landed.at[at],
-            *flags[3 * n : 3 * n + 3],
-        )
-        for n, (ref, landed) in enumerate(
-            ((grad_part_ref, grad_landed_ref), (out_part_ref, out_landed_ref))
-        )
-    ]
-    for move in moves:
-        move.start()
-    moves[0].arrive()
-    middle = middle_ref[...]
-    back, gain_terms = norm_back(middle, gain_ref[...], added(grad_landed_ref))
+    move = Exchange(
+        "hd",
+        lambda to: token_rows(grad_part_ref, to, tokens),
+        lambda at: grad_landed_ref.at[at],
+        *flags[:3],
+    )
+    move.start()
+    move.arrive()
+    back, gain_terms = norm_back(middle_ref[...], gain_ref[...], added(grad_landed_ref))
     grad_middle = cot_ref[...].astype(f32) + back
+    own_ref[...] = grad_middle.astype(bf16)
+    after = spread_own(own_ref, grad_all_ref, tokens, flags[3:])
     grad_middle_ref[...] = grad_middle
-    own_ref[...] = grad_middle.astype(bf16)
-    after = spread_own(own_ref, grad_all_ref, tokens, flags[6:9])
     grad_gain_ref[...] = jnp.sum(jnp.sum(gain_terms, axis=0), axis=0, keepdims=True)
-    moves[1].arrive()
-    block_ref[...] = (middle + added(out_landed_ref)).astype(bf16)
-    for move in moves:
-        move.leave()
-    after.arrive()
-    after.leave()
+    settle_all(after)
+    move.leave()
 
 
 def close_kernel(
-    normed_part_ref, front_ref, output_ref, small_ref, hidden_ref, grad_middle_ref, gain_ref,
-    grad_in_ref, front_all_ref, output_all_ref, small_sum_ref,
-    normed_landed, small_landed, front_own, output_own, *flags
+    normed_part_ref, front_ref, small_ref, hidden_ref, grad_middle_ref, gain_ref,
+    grad_in_ref, front_all_ref, small_sum_ref,
+    normed_landed, small_landed, front_own, *flags
 ):
     tokens = hidden_ref.shape[1]
-    meet(heads=True, chips=True, owners=True)
-    reduces = (
-        PairReduce(front_ref, *flags[:7], column_target, column_source),
-        PairReduce(output_ref, *flags[7:14], owner_target, owner_source),
-    )
+    meet(heads=True, chips=True)
+    reduce = PairReduce(front_ref, *flags[:7], column_target, column_source)
     normed_move = Exchange(
         "hd",
         lambda to: token_rows(normed_part_ref, to, tokens),
         lambda at: normed_landed.at[at],
-        *flags[14:17],
-    )
-    small_move = PairGather(small_ref, lambda at: small_landed.at[at], *flags[17:20])
-    for move in reduces:
-        move.start()
+        *flags[7:10],
+    )
+    small_move = PairGather("cp", small_ref, lambda at: small_landed.at[at], *flags[10:13])
+    reduce.start()
+    small_move.start()
     normed_move.start()
-    for move in reduces:
-        move.add_pairs()
-    small_move.start()
-    spreads = []
-    for n, (move, own, everywhere) in enumerate(
-        zip(reduces, (front_own, output_own), (front_all_ref, output_all_ref))
-    ):
-        own[...] = move.total()
-        spreads.append(spread_piece(own, everywhere, flags[20 + 3 * n : 23 + 3 * n]))
+    reduce.add_pairs()
+    small_move.hand_on()
+    front_own[...] = reduce.total()
+    spread = spread_piece(front_own, front_all_ref, flags[13:16])
     normed_move.arrive()
+    spread.hand_on()
     back, _ = norm_back(hidden_ref[...].astype(f32), gain_ref[...], added(normed_landed))
     grad_in_ref[...] = (grad_middle_ref[...] + back).astype(bf16)
     small_move.arrive()
     small_sum_ref[...] = added(small_landed)
-    for move in (normed_move, small_move, *reduces):
+    for move in (normed_move, small_move, reduce):
         move.leave()
-    for spread in spreads:
-        spread.arrive()
-        spread.leave()
+    spread.arrive()
+    spread.leave()
 
 
 def passed_along(block, axis, distance):
@@ -911,7 +973,7 @@
     ff = w_ffn_gate.shape[1] // hd
     ffp = -(-ff // LANES) * LANES
     qkv = 2 * dk + dv
-    side = qkv + dv
+    side, gate_at = qkv, qkv + LANES
     span = tokens * hd
     blocks = span // STRETCH
 
@@ -938,8 +1000,8 @@
             part(w_query),
             part(w_key),
             part(w_value),
+            jnp.pad(side_cols, ((0, 0), (0, LANES - side_cols.shape[1]))),
             part(w_gate_out),
-            jnp.pad(side_cols, ((0, 0), (0, LANES - side_cols.shape[1]))),
         ],
         1,
     )
@@ -966,7 +1028,7 @@
     normed = (inputs_all * scale_all * attn_gain).astype(bf16)
     projected = dot(normed, front_full, "std,de->ste")
     packed = projected[:, :, :qkv].astype(bf16)
-    gate_pre = projected[:, :, qkv:side]
+    gate_pre = projected[:, :, gate_at:]
     decay_head = projected[:, :, side].astype(bf16).astype(f32)
     beta_head = projected[:, :, side + 1].astype(bf16).astype(f32)
 
@@ -1024,7 +1086,7 @@
             pltpu.VMEM((sequences, dk, dv), f32),
             pltpu.VMEM((dk, dv), f32),
             pltpu.SemaphoreType.DMA((4,)),
-            *sems(cp, share, share, hd),
+            *sems(cp, CORES, CORES, hd),
             pltpu.SemaphoreType.DMA((chips,)),
             pltpu.SemaphoreType.DMA((chips,)),
         ],
@@ -1043,7 +1105,7 @@
         ("any", "vmem", "vmem"),
         (dot(normed_head, output_part, "ste,ed->std").astype(bf16), hidden_in, ffn_gain),
         ("vmem", "any"),
-        [landing, own_tokens, *sems(hd, hd)],
+        [landing, own_tokens, *sems(hd, *(hd,) * sequences)],
         4,
     )
     gate_up = dot(ffn_all, ffn_full, "std,df->stf")
@@ -1053,22 +1115,17 @@
     inner = inner.astype(bf16)
     grad_inner = dot(cot_all, down_part, "std,fd->stf")
     grad_gate_up = swiglu_pull(grad_inner)[0].astype(bf16)
-    block_out, grad_middle, grad_ffn_gain, grad_attention = comm_call(
+    out_partial = dot(inner, down_part, "stf,fd->std").astype(bf16)
+    grad_middle, grad_ffn_gain, grad_attention = comm_call(
         ffn_back_kernel,
+        (shaped(hidden_in.shape), shaped((1, width)), shaped((sequences, span, width), bf16)),
+        ("any", "vmem", "vmem", "vmem"),
         (
-            shaped(hidden_in.shape, bf16),
-            shaped(hidden_in.shape),
-            shaped((1, width)),
-            shaped((sequences, span, width), bf16),
-        ),
-        ("any", "any", "vmem", "vmem", "vmem"),
-        (
-            dot(inner, down_part, "stf,fd->std").astype(bf16),
             dot(grad_gate_up, ffn_full, "stf,df->std").astype(bf16),
             middle, cotangent, ffn_gain,
         ),
-        ("vmem", "vmem", "vmem", "any"),
-        [landing, landing, own_tokens, *sems(hd, hd, hd)],
+        ("vmem", "vmem", "any"),
+        [landing, own_tokens, *sems(hd, *(hd,) * sequences)],
         5,
     )
 
@@ -1083,15 +1140,28 @@
     def by_owner(grad):
         return grad.reshape(chips, CORES, shard, grad.shape[1]).astype(bf16)
 
-    grad_ffn = by_owner(weight_grad(ffn_all, grad_gate_up))
     grad_down = pieces(weight_grad(inner, cot_all)[:ff])
 
     grad_normed_head = dot(grad_attention, output_part, "std,ed->ste")
     grad_output = pieces(weight_grad(normed_head, grad_attention))
     grad_mixed, grad_gate_pre, grad_head_gain = gated_pull(grad_normed_head)
     grad_mixed = grad_mixed.astype(bf16)
-    ffn_share, down_share = (entry.shape[2:] for entry in (grad_ffn, grad_down))
-    grad_q, grad_k, grad_v, grad_aux, grad_row, grad_ffn, grad_down = comm_call(
+    grad_gate_pre = grad_gate_pre.astype(bf16)
+    grad_ffn = by_owner(
+        jnp.concatenate(
+            [
+                weight_grad(ffn_all, grad_gate_up).astype(bf16),
+                weight_grad(normed, grad_gate_pre).astype(bf16),
+            ],
+            1,
+        )
+    )
+    ffn_share, down_share, output_share = (
+        entry.shape[2:] for entry in (grad_ffn, grad_down, grad_output)
+    )
+    (
+        grad_q, grad_k, grad_v, grad_aux, grad_row, grad_ffn, grad_down, new_output, block_out,
+    ) = comm_call(
         backward_kernel,
         (
             shaped((sequences, span, dk)),
@@ -1101,13 +1171,15 @@
             shaped((sequences, blocks, STRETCH)),
             shaped((hd, *ffn_share), bf16),
             shaped((hd, *down_share), bf16),
+            shaped((hd, *output_share), bf16),
+            shaped(hidden_in.shape, bf16),
         ),
-        ("vmem",) * 14,
+        ("vmem",) * 15 + ("any", "vmem"),
         (
             queries, key_rows, values, aux, between, weighted, inverse, states, updates,
-            grad_mixed, maps, both, grad_ffn, grad_down,
+            grad_mixed, maps, both, grad_ffn, grad_down, grad_output, out_partial, middle,
         ),
-        ("vmem",) * 5 + ("any",) * 2,
+        ("vmem",) * 5 + ("any",) * 3 + ("vmem",),
         [
             pltpu.VMEM((sequences, span, dv), f32),
             pltpu.VMEM((sequences, blocks, dk, dv), f32),
@@ -1118,12 +1190,15 @@
             pltpu.VMEM((dk, dv), f32),
             pltpu.VMEM(ffn_share, bf16),
             pltpu.VMEM(down_share, bf16),
+            pltpu.VMEM(output_share, bf16),
+            landing,
             pltpu.SemaphoreType.DMA((4,)),
             pltpu.SemaphoreType.DMA((chips,)),
             pltpu.SemaphoreType.DMA((chips,)),
             *reduce_scratch(grad_ffn),
             *reduce_scratch(grad_down),
-            *sems(hd, hd),
+            *reduce_scratch(grad_output),
+            *sems(hd, hd, hd, hd),
         ],
         3,
     )
@@ -1136,24 +1211,23 @@
     grad_projected = jnp.concatenate(
         [
             grad_packed,
-            grad_gate_pre.astype(bf16),
             jnp.pad(
                 jnp.stack([grad_decay, grad_beta], -1).astype(bf16),
                 ((0, 0), (0, 0), (0, LANES - 2)),
             ),
+            grad_gate_pre,
         ],
         -1,
     )
     partial_normed = dot(grad_projected, front_full, "ste,de->std")
     grad_attn_gain = jnp.sum(inputs_all * scale_all * partial_normed, (0, 1))
-    grad_front = weight_grad(normed, grad_projected)
+    grad_front = weight_grad(normed, grad_projected[:, :, :gate_at])
     spread_gain = jnp.pad(
         grad_head_gain.reshape(cp, head_share), ((0, 0), (0, shard - head_share))
     ).reshape(-1)
     gains = jnp.stack([grad_attn_gain, grad_ffn_gain[0], spread_gain], 1)
-    grad_front = jnp.concatenate(
-        [grad_front[:, : side + 2], gains, grad_front[:, side + 5 :]], 1
-    )
+    grad_front += jnp.pad(gains, ((0, 0), (side + 2, LANES - 2 - gains.shape[1])))
+
     small = jnp.concatenate(
         [
             grad_taps,
@@ -1163,29 +1237,22 @@
     )
     small = jnp.pad(small, ((0, -small.shape[0] % 8), (0, 0)))
     grad_front = by_owner(grad_front)
-    front_share, output_share = (entry.shape[2:] for entry in (grad_front, grad_output))
-    grad_in, grad_front, grad_output, small = comm_call(
+    front_share = grad_front.shape[2:]
+    grad_in, grad_front, small = comm_call(
         close_kernel,
+        (shaped(hidden_in.shape, bf16), shaped((hd, *front_share), bf16), shaped(small.shape)),
+        ("any", "vmem", "any") + ("vmem",) * 3,
         (
-            shaped(hidden_in.shape, bf16),
-            shaped((hd, *front_share), bf16),
-            shaped((hd, *output_share), bf16),
-            shaped(small.shape),
-        ),
-        ("any", "vmem", "vmem", "any") + ("vmem",) * 3,
-        (
-            partial_normed.astype(bf16), grad_front, grad_output, small, hidden_in, grad_middle,
+            partial_normed.astype(bf16), grad_front, small, hidden_in, grad_middle,
             attn_gain[None],
         ),
-        ("vmem", "any", "any", "vmem"),
+        ("vmem", "any", "vmem"),
         [
             landing,
             pltpu.VMEM((cp, *small.shape), f32),
             pltpu.VMEM(front_share, bf16),
-            pltpu.VMEM(output_share, bf16),
             *reduce_scratch(grad_front),
-            *reduce_scratch(grad_output),
-            *sems(hd, cp, hd, hd),
+            *sems(hd, cp, hd),
         ],
         6,
     )
@@ -1207,8 +1274,8 @@
         columns(grad_front[:, :, 2 * dk : qkv]),
         columns(grad_front[:, :, side : side + 1]),
         columns(grad_front[:, :, side + 1 : side + 2]),
-        columns(grad_front[:, :, qkv:side]),
-        owned(grad_output, w_output.shape[0]),
+        columns(grad_ffn[:, :, 2 * ffp :]),
+        owned(new_output, w_output.shape[0]),
         columns(grad_ffn[:, :, :ff]),
         columns(grad_ffn[:, :, ffp : ffp + ff]),
         owned(grad_down, w_ffn_down.shape[0]),

time: 597 us -> 518 us (0.87)
  Pallas kernels: 476 us -> 384 us
  matrix products: 29.7 us -> 36.6 us
  other arithmetic: 26.3 us -> 33.1 us
    pallas_call x6, Pallas kernels: 476 us -> 384 us  [comm_call(): pl.pallas_call(body, out_shape=out_shape, in_specs=[pl.BlockSpec(memory_s...]
    dot_general x12 -> x13, matrix products: 29.7 us -> 36.6 us  [dot(): return jnp.einsum(spec, a, b, preferred_element_type=f32)]
    unnamed x91 -> x87, local copies, waits for them, and re-layouts: 12.2 us -> 10.5 us
  transfers between devices with their start and end apart: 2 -> 2, of which waited for: 0 -> 0; matrix products, arithmetic and copies ran while one was open for 3% -> 4% of each run, Pallas kernels for 0% -> 0%
where the time goes in v3:
time: 518 us; the launch traced here: 509 us
  Pallas kernels  384 us (74%)
  local copies, waits for them, and re-layouts  49 us (9%)
  matrix products  36.6 us (7%)
  other arithmetic  33.1 us (6%)
    pallas_call x6, Pallas kernels, comm_call(): pl.pallas_call(body, out_shape=out_shape, in_specs=[pl.BlockSpec(memory_s...  384 us
    dot_general x13, matrix products, dot(): return jnp.einsum(spec, a, b, preferred_element_type=f32)  36.6 us
    convert_element_type x8, local copies, waits for them, and re-layouts, columns(): return jnp.swapaxes(grad, 0, 1).reshape(grad.shape[1], -1).astype(f32)  12.5 us
    unnamed x87, local copies, waits for them, and re-layouts  10.5 us
  transfers between devices with their start and end apart: 2, of which 0 were waited for; matrix products, arithmetic and copies ran while one was open for 4% of the time, Pallas kernels for 0%

profile of v3, /device:TPU:8, one launch (start us, length us, event | category | flops | bytes accessed | tf_op | source)
XLA Modules:
  0.0 508.9 jit_solution(2874777653080268821)
XLA Ops:
  5.8 0.9 copy-done
  6.8 35.6 %shard_map.356 = (bf16[2,512,1024]{2,1,0:T(8,128)(2,1)S(1)}, bf16[1024,896]{1,0:T(8,128)(2,1)S(1)}) custom-call(bf16[2,64,1024]{2,1,0:T(8,128)(2,1)S(1)} %copy-done, bf16[64,896]{1,0:T(8,128)(2,1)S(1)} %dynamic-slice_dynamic-update-slice_fusion.front_ref), custom_call_target="tpu_custom_call" | custom-call | tf_op jit(solution)/shard_map/pallas_call | solution.py:623
  43.4 4.2 fusion.86
  47.6 1.3 collective-permute-start
  51.3 1.2 fusion.60
  54.6 1.1 constant_dynamic-slice_fusion
  56.6 2.6 fusion.8
  59.6 1.1 slice.251.v_ref
  61.3 76.0 %shard_map.357 = (bf16[2,512,256]{2,1,0:T(8,128)(2,1)S(1)}, f32[2,8,128,256]{3,2,1,0:T(8,128)}, f32[2,512,256]{2,1,0:T(8,128)}, f32[2,512,128]{2,1,0:T(8,128)S(1...) custom-call(f32[2,512,128]{2,1,0:T(8,128)S(1)} %get-tuple-element.13, ...), custom_call_target="tpu_custom_call" | custom-call | tf_op jit(solution)/shard_map/pallas_call | solution.py:623
  138.9 2.1 convolution_convert_fusion.1.partial_ref
  141.0 59.2 %shard_map.358 = (f32[2,64,1024]{2,1,0:T(8,128)S(1)}, bf16[2,512,1024]{2,1,0:T(8,128)(2,1)S(1)}) custom-call(bf16[2,512,1024]{2,1,0:T(8,128)(2,1)S(1)} %convolution_convert_fusion.1.partial_ref, bf16[2,64,1024]{2,1,0:T(8,128)(2,1)S(1)} %copy-done.1, f32[1,1024]{1,0:T(1,128)S(1)} %bitcast.117), custom_call_target="tpu_custom_call" | custom-call | tf_op jit(solution)/shard_map/pallas_call | solution.py:623
  200.2 1.8 fusion.21
  202.0 1.8 fusion.64
  203.8 3.0 bitcast_convert_fusion
  206.8 1.8 convolution_convert_fusion.2.grad_part_ref
  208.7 47.0 %shard_map.359 = (f32[2,64,1024]{2,1,0:T(8,128)S(1)}, f32[1,1024]{1,0:T(1,128)S(1)}, bf16[2,512,1024]{2,1,0:T(8,128)(2,1)S(1)}) custom-call(bf16[2,512,1024]{2,1,0:T(8,128)(2,1)S(1)} %convolution_convert_fusion.2.grad_part_ref, f32[2,64,1024]{2,1,0:T(8,128)S(1)} %get-tuple-element.74.middle_ref, bf16[2,64,1024]{2,1,0:T(8,128)(2,1)S(1)} %copy-done.4, ...), custom_call_target="tpu_custom_call" | custom-call | tf_op jit(solution)/shard_map/pallas_call | solution.py:623
  255.7 3.2 fusion.28
  258.9 3.7 fusion.37
  262.5 1.0 convolution_bitcast_fusion
  263.5 2.6 convolution_convert_fusion.out_part_ref
  267.0 2.1 reshape.299
  269.1 2.7 fusion.27
  271.8 1.5 pad_maximum_fusion
  273.3 3.9 copy.199
  277.2 2.4 pad.98.down_ref
  279.6 2.4 fusion.38.grad_ref
  282.0 105.1 %shard_map.360 = (f32[2,512,128]{2,1,0:T(8,128)S(1)}, f32[2,512,128]{2,1,0:T(8,128)S(1)}, f32[2,512,256]{2,1,0:T(8,128)}, f32[2,512,8]{2,1,0:T(8,128)S(1)}, f32[...) custom-call(f32[2,512,128]{2,1,0:T(8,128)S(1)} %get-tuple-element.13, ...), custom_call_target="tpu_custom_call" | custom-call | tf_op jit(solution)/shard_map/pallas_call | solution.py:623
  387.1 1.9 convert_bitcast_fusion.2
  389.0 2.5 convert_bitcast_fusion
  394.1 2.0 multiply_reduce_fusion.3
  396.9 1.3 copy-done.18
  399.5 2.1 pad_add_fusion
  401.6 1.9 slice_reduce_fusion
  404.5 1.3 reshape.327
  405.8 3.1 fusion.80
  410.4 1.0 slice_convert_fusion.2
  411.4 1.7 collective-permute-start.1
  414.9 1.9 copy.224
  416.8 1.3 copy.213
  418.1 2.3 reshape.316
  420.4 2.5 copy.212
  422.9 2.2 reshape.315
  425.1 0.9 reshape.317
  426.1 2.6 slice.261
  429.5 1.4 scatter-add.4
  430.9 5.0 fusion.3
  436.2 3.9 fusion.5
  440.1 60.7 %shard_map.361 = (bf16[2,64,1024]{2,1,0:T(8,128)(2,1)S(1)}, bf16[8,64,640]{2,1,0:T(8,128)(2,1)S(1)}, f32[8,512]{1,0:T(8,128)S(1)}) custom-call(bf16[2,512,1024]{2,1,0:T(8,128)(2,1)S(1)} %get-tuple-element.121.normed_part_ref, bf16[8,2,64,640]{3,2,1,0:T(8,128)(2,1)S(1)} %bitcast.116, f32[8,512]{1,0:T(8,128)S(1)} %select_maximum_fusion.2.small_ref, ...), custom_call_target="tpu_custom_call" | custom-call | tf_op jit(solution)/shard_map/pallas_call | solution.py:623
  (164 shorter events, 30.7 us)
Async XLA Ops:
  5.8 0.9 copy-start
  42.4 5.1 %copy-start.2 = (bf16[2,512,1024]{2,1,0:T(8,128)(2,1)}, bf16[2,512,1024]{2,1,0:T(8,128)(2,1)S(1)}, u32[]{:S(2)}) copy-start(bf16[2,512,1024]{2,1,0:T(8,128)(2,1)S(1)} %get-tuple-element.62) | copy-start | bytes 6291460
  42.4 6.5 %copy-start.12 = (bf16[1024,896]{1,0:T(8,128)(2,1)}, bf16[1024,896]{1,0:T(8,128)(2,1)S(1)}, u32[]{:S(2)}) copy-start(bf16[1024,896]{1,0:T(8,128)(2,1)S(1)} %get-tuple-element.63) | copy-start | bytes 5505028
  43.3 7.4 %copy-start.34 = (s32[2,8192]{1,0:T(2,128)S(1)}, s32[2,8192]{1,0:T(2,128)}, u32[]{:S(2)}) copy-start(s32[2,8192]{1,0:T(2,128)} %param.24) | copy-start | bytes 196612
  43.3 7.8 %copy-start.36 = (bf16[4,256]{1,0:T(4,128)(2,1)S(1)}, bf16[4,256]{1,0:T(4,128)(2,1)}, u32[]{:S(2)}) copy-start(bf16[4,256]{1,0:T(4,128)(2,1)} %param.37) | copy-start | bytes 6148
  43.3 7.8 %copy-start.37 = (bf16[4,128]{1,0:T(4,128)(2,1)S(1)}, bf16[4,128]{1,0:T(4,128)(2,1)}, u32[]{:S(2)}) copy-start(bf16[4,128]{1,0:T(4,128)(2,1)} %param.36) | copy-start | bytes 3076
  43.4 7.8 %copy-start.38 = (bf16[4,128]{1,0:T(4,128)(2,1)S(1)}, bf16[4,128]{1,0:T(4,128)(2,1)}, u32[]{:S(2)}) copy-start(bf16[4,128]{1,0:T(4,128)(2,1)} %param.35) | copy-start | bytes 3076
  47.6 1.6 copy-start.29
  47.6 8.7 %collective-permute-start = (bf16[2,3,512]{2,1,0:T(4,128)(2,1)S(1)}, bf16[2,3,512]{2,1,0:T(4,128)(2,1)S(1)}, u32[]{:S(2)}, u32[]{:S(2)}) collective-permute-start(bf16[2,3,512]{2,1,0:T(4,128)(2,1)S(1)} %slice.240), channel_id=1, source_target_pairs={{0,8},{8,16},{16,24},{24,32},{32,40},{40,48},{48,56},{56,64},{64,7... | collective-permute-start | bytes 18440 | tf_op jit(solution)/shard_map/ppermute | solution.py:960
  54.5 1.6 copy-start.30
  56.6 2.6 copy-start.16
  59.2 1.8 copy-start.22
  59.6 1.5 copy-start.4
  59.6 1.5 copy-start.11
  59.6 1.8 copy-start.13
  137.3 0.8 copy-start.9
  138.1 0.8 copy-start.7
  138.1 2.9 copy-start.14
  138.9 2.1 copy-start.1
  141.0 59.2 %copy-start.39 = (bf16[1024,768]{1,0:T(8,128)(2,1)S(1)}, bf16[1024,768]{1,0:T(8,128)(2,1)}, u32[]{:S(2)}) copy-start(bf16[1024,768]{1,0:T(8,128)(2,1)} %get-tuple-element.71) | copy-start | bytes 4718596
  200.2 8.5 %copy-start.3 = (f32[2,64,1024]{2,1,0:T(8,128)}, f32[2,64,1024]{2,1,0:T(8,128)S(1)}, u32[]{:S(2)}) copy-start(f32[2,64,1024]{2,1,0:T(8,128)S(1)} %get-tuple-element.74.middle_ref) | copy-start | bytes 1572868
  200.2 1.8 copy-start.27
  255.7 3.2 copy-start.5
  269.1 2.7 copy-start.28
  277.2 4.7 copy-start.8
  277.2 4.7 copy-start.10
  277.2 4.7 copy-start.15
  387.1 4.4 copy-start.23
  391.5 1.6 copy-start.24
  391.9 1.9 copy-start.17
  391.9 2.2 copy-start.31
  396.8 1.3 copy-start.18
  396.9 2.1 copy-start.20
  396.9 2.7 copy-start.21
  409.5 3.6 copy-start.32
  409.5 3.6 copy-start.33
  411.4 5.4 %copy-start.26 = (f32[64,8,352]{2,0,1:T(8,128)S(1)}, f32[64,8,352]{2,0,1:T(8,128)}, u32[]{:S(2)}) copy-start(f32[64,8,352]{2,0,1:T(8,128)} %get-tuple-element.131) | copy-start | bytes 2162692
  411.4 17.3 %collective-permute-start.1 = (f32[2,3,512]{2,1,0:T(4,128)S(1)}, f32[2,3,512]{2,1,0:T(4,128)S(1)}, u32[]{:S(2)}, u32[]{:S(2)}) collective-permute-start(f32[2,3,512]{2,1,0:T(4,128)S(1)} %pad_add_fusion.1), channel_id=1, source_target_pairs={{8,0},{16,8},{24,16},{32,24},{40,32},{48,40},{56,48},{64,56},{72,6... | collective-permute-start | bytes 36872 | tf_op jit(solution)/shard_map/ppermute | solution.py:960
  418.1 7.0 %copy-start.25 = (f32[8,22,1024]{2,1,0:T(8,128)S(1)}, f32[8,22,1024]{2,1,0:T(8,128)}, u32[]{:S(2)}) copy-start(f32[8,22,1024]{2,1,0:T(8,128)} %slice_convert_fusion.2) | copy-start | bytes 2162692
  426.1 2.6 copy-start.19
  428.7 2.2 copy-start.35
  436.2 3.9 copy-start.6

commit v4 on v3

--- a/solution.py
+++ b/solution.py
@@ -767,7 +767,7 @@
         lambda at: out_landed_ref.at[at],
         *flags[30:33],
     )
-    for move in (*reduces, out_move):
+    for move in reduces:
         move.start()
     segment_local(
         q_ref, k_ref, aux_ref, between_ref, w_ref, grad_ref, through_ref, inflow_ref, own_ref
@@ -784,6 +784,7 @@
     for move in reduces:
         move.add_pairs()
     settle()
+    out_move.start()
 
     def leave(hop, state):
         source = chips - 1 - hop
@@ -818,11 +819,13 @@
     ):
         own[...] = move.total()
         spreads.append(spread_piece(own, everywhere, flags[21 + 3 * n : 24 + 3 * n]))
+    quarter = (blocks - blocks // 2) // 2
+    exits = back_blocks(blocks // 2, quarter, exits, *refs)
+    for spread in spreads:
+        spread.hand_on()
+    back_blocks(blocks // 2 + quarter, blocks - blocks // 2 - quarter, exits, *refs)
     out_move.arrive()
     block_ref[...] = (middle_ref[...] + added(out_landed_ref)).astype(bf16)
-    for spread in spreads:
-        spread.hand_on()
-    back_blocks(blocks // 2, blocks - blocks // 2, exits, *refs)
     for move in (*reduces, out_move):
         move.leave()
     for spread in spreads:

time: 518 us -> 521 us (level)
  no operation moved by 1% of the time
where the time goes in v4:
time: 521 us; the launch traced here: 514 us
  Pallas kernels  388 us (74%)
  local copies, waits for them, and re-layouts  49 us (9%)
  matrix products  36.6 us (7%)
  other arithmetic  33.3 us (6%)
    pallas_call x6, Pallas kernels, comm_call(): pl.pallas_call(body, out_shape=out_shape, in_specs=[pl.BlockSpec(memory_s...  388 us
    dot_general x13, matrix products, dot(): return jnp.einsum(spec, a, b, preferred_element_type=f32)  36.6 us
    convert_element_type x8, local copies, waits for them, and re-layouts, columns(): return jnp.swapaxes(grad, 0, 1).reshape(grad.shape[1], -1).astype(f32)  12.5 us
    unnamed x87, local copies, waits for them, and re-layouts  10.5 us
  transfers between devices with their start and end apart: 2, of which 0 were waited for; matrix products, arithmetic and copies ran while one was open for 4% of the time, Pallas kernels for 0%

profile of v4, /device:TPU:8, one launch (start us, length us, event | category | flops | bytes accessed | tf_op | source)
XLA Modules:
  0.0 514.0 jit_solution(3863455888646359460)
XLA Ops:
  5.8 0.9 copy-done
  6.8 35.6 %shard_map.356 = (bf16[2,512,1024]{2,1,0:T(8,128)(2,1)S(1)}, bf16[1024,896]{1,0:T(8,128)(2,1)S(1)}) custom-call(bf16[2,64,1024]{2,1,0:T(8,128)(2,1)S(1)} %copy-done, bf16[64,896]{1,0:T(8,128)(2,1)S(1)} %dynamic-slice_dynamic-update-slice_fusion.front_ref), custom_call_target="tpu_custom_call" | custom-call | tf_op jit(solution)/shard_map/pallas_call | solution.py:623
  43.4 4.2 fusion.86
  47.6 1.3 collective-permute-start
  51.3 1.2 fusion.60
  54.6 1.1 constant_dynamic-slice_fusion
  56.6 2.6 fusion.8
  59.6 1.1 slice.251.v_ref
  61.3 76.0 %shard_map.357 = (bf16[2,512,256]{2,1,0:T(8,128)(2,1)S(1)}, f32[2,8,128,256]{3,2,1,0:T(8,128)}, f32[2,512,256]{2,1,0:T(8,128)}, f32[2,512,128]{2,1,0:T(8,128)S(1...) custom-call(f32[2,512,128]{2,1,0:T(8,128)S(1)} %get-tuple-element.13, ...), custom_call_target="tpu_custom_call" | custom-call | tf_op jit(solution)/shard_map/pallas_call | solution.py:623
  138.9 2.1 convolution_convert_fusion.1.partial_ref
  141.0 59.2 %shard_map.358 = (f32[2,64,1024]{2,1,0:T(8,128)S(1)}, bf16[2,512,1024]{2,1,0:T(8,128)(2,1)S(1)}) custom-call(bf16[2,512,1024]{2,1,0:T(8,128)(2,1)S(1)} %convolution_convert_fusion.1.partial_ref, bf16[2,64,1024]{2,1,0:T(8,128)(2,1)S(1)} %copy-done.1, f32[1,1024]{1,0:T(1,128)S(1)} %bitcast.117), custom_call_target="tpu_custom_call" | custom-call | tf_op jit(solution)/shard_map/pallas_call | solution.py:623
  200.2 1.8 fusion.21
  202.0 1.8 fusion.64
  203.8 3.0 bitcast_convert_fusion
  206.8 1.8 convolution_convert_fusion.2.grad_part_ref
  208.7 47.0 %shard_map.359 = (f32[2,64,1024]{2,1,0:T(8,128)S(1)}, f32[1,1024]{1,0:T(1,128)S(1)}, bf16[2,512,1024]{2,1,0:T(8,128)(2,1)S(1)}) custom-call(bf16[2,512,1024]{2,1,0:T(8,128)(2,1)S(1)} %convolution_convert_fusion.2.grad_part_ref, f32[2,64,1024]{2,1,0:T(8,128)S(1)} %get-tuple-element.74.middle_ref, bf16[2,64,1024]{2,1,0:T(8,128)(2,1)S(1)} %copy-done.4, ...), custom_call_target="tpu_custom_call" | custom-call | tf_op jit(solution)/shard_map/pallas_call | solution.py:623
  255.7 3.2 fusion.28
  258.9 3.7 fusion.37
  262.5 1.0 convolution_bitcast_fusion
  263.5 2.6 convolution_convert_fusion.out_part_ref
  267.0 2.1 reshape.299
  269.1 2.7 fusion.27
  271.8 1.5 pad_maximum_fusion
  273.3 3.9 copy.199
  277.2 2.4 pad.98.down_ref
  279.6 2.4 fusion.38.grad_ref
  282.0 121.8 %shard_map.360 = (f32[2,512,128]{2,1,0:T(8,128)S(1)}, f32[2,512,128]{2,1,0:T(8,128)S(1)}, f32[2,512,256]{2,1,0:T(8,128)}, f32[2,512,8]{2,1,0:T(8,128)S(1)}, f32[...) custom-call(f32[2,512,128]{2,1,0:T(8,128)S(1)} %get-tuple-element.13, ...), custom_call_target="tpu_custom_call" | custom-call | tf_op jit(solution)/shard_map/pallas_call | solution.py:623
  403.8 1.9 convert_bitcast_fusion.2
  405.7 2.5 convert_bitcast_fusion
  410.8 2.0 multiply_reduce_fusion.3
  413.6 1.3 copy-done.18
  416.2 2.1 pad_add_fusion
  418.3 1.9 slice_reduce_fusion
  420.4 1.1 reduce_window_sum.23
  421.5 1.3 reshape.327
  422.7 3.1 fusion.80
  427.3 1.0 slice_convert_fusion.2
  428.4 1.4 collective-permute-start.1
  431.6 1.9 copy.224
  433.5 1.3 copy.213
  434.8 2.3 reshape.316
  437.1 2.5 copy.212
  439.6 2.2 reshape.315
  442.8 2.6 slice.261
  446.2 1.4 scatter-add.4
  447.6 5.0 fusion.3
  452.9 3.9 fusion.5
  456.8 48.9 %shard_map.361 = (bf16[2,64,1024]{2,1,0:T(8,128)(2,1)S(1)}, bf16[8,64,640]{2,1,0:T(8,128)(2,1)S(1)}, f32[8,512]{1,0:T(8,128)S(1)}) custom-call(bf16[2,512,1024]{2,1,0:T(8,128)(2,1)S(1)} %get-tuple-element.121.normed_part_ref, bf16[8,2,64,640]{3,2,1,0:T(8,128)(2,1)S(1)} %bitcast.116, f32[8,512]{1,0:T(8,128)S(1)} %select_maximum_fusion.2.small_ref, ...), custom_call_target="tpu_custom_call" | custom-call | tf_op jit(solution)/shard_map/pallas_call | solution.py:623
  (164 shorter events, 30.8 us)
Async XLA Ops:
  5.8 0.9 copy-start
  42.4 5.1 copy-start.2
  42.4 6.5 %copy-start.12 = (bf16[1024,896]{1,0:T(8,128)(2,1)}, bf16[1024,896]{1,0:T(8,128)(2,1)S(1)}, u32[]{:S(2)}) copy-start(bf16[1024,896]{1,0:T(8,128)(2,1)S(1)} %get-tuple-element.63) | copy-start | bytes 5505028
  43.3 7.4 %copy-start.34 = (s32[2,8192]{1,0:T(2,128)S(1)}, s32[2,8192]{1,0:T(2,128)}, u32[]{:S(2)}) copy-start(s32[2,8192]{1,0:T(2,128)} %param.24) | copy-start | bytes 196612
  43.3 7.8 %copy-start.36 = (bf16[4,256]{1,0:T(4,128)(2,1)S(1)}, bf16[4,256]{1,0:T(4,128)(2,1)}, u32[]{:S(2)}) copy-start(bf16[4,256]{1,0:T(4,128)(2,1)} %param.37) | copy-start | bytes 6148
  43.3 7.8 %copy-start.37 = (bf16[4,128]{1,0:T(4,128)(2,1)S(1)}, bf16[4,128]{1,0:T(4,128)(2,1)}, u32[]{:S(2)}) copy-start(bf16[4,128]{1,0:T(4,128)(2,1)} %param.36) | copy-start | bytes 3076
  43.4 7.8 %copy-start.38 = (bf16[4,128]{1,0:T(4,128)(2,1)S(1)}, bf16[4,128]{1,0:T(4,128)(2,1)}, u32[]{:S(2)}) copy-start(bf16[4,128]{1,0:T(4,128)(2,1)} %param.35) | copy-start | bytes 3076
  47.6 1.6 copy-start.29
  47.6 8.7 %collective-permute-start = (bf16[2,3,512]{2,1,0:T(4,128)(2,1)S(1)}, bf16[2,3,512]{2,1,0:T(4,128)(2,1)S(1)}, u32[]{:S(2)}, u32[]{:S(2)}) collective-permute-start(bf16[2,3,512]{2,1,0:T(4,128)(2,1)S(1)} %slice.240), channel_id=1, source_target_pairs={{0,8},{8,16},{16,24},{24,32},{32,40},{40,48},{48,56},{56,64},{64,7... | collective-permute-start | bytes 18440 | tf_op jit(solution)/shard_map/ppermute | solution.py:963
  54.5 1.6 copy-start.30
  56.6 2.6 copy-start.16
  59.2 1.8 copy-start.22
  59.6 1.5 copy-start.4
  59.6 1.5 copy-start.11
  59.6 1.8 copy-start.13
  137.3 0.8 copy-start.9
  138.1 0.8 copy-start.7
  138.1 2.9 copy-start.14
  138.9 2.1 copy-start.1
  141.0 59.2 %copy-start.39 = (bf16[1024,768]{1,0:T(8,128)(2,1)S(1)}, bf16[1024,768]{1,0:T(8,128)(2,1)}, u32[]{:S(2)}) copy-start(bf16[1024,768]{1,0:T(8,128)(2,1)} %get-tuple-element.71) | copy-start | bytes 4718596
  200.2 8.5 %copy-start.3 = (f32[2,64,1024]{2,1,0:T(8,128)}, f32[2,64,1024]{2,1,0:T(8,128)S(1)}, u32[]{:S(2)}) copy-start(f32[2,64,1024]{2,1,0:T(8,128)S(1)} %get-tuple-element.74.middle_ref) | copy-start | bytes 1572868
  200.2 1.8 copy-start.27
  255.7 3.2 copy-start.5
  269.1 2.7 copy-start.28
  277.2 4.7 copy-start.8
  277.2 4.7 copy-start.10
  277.2 4.7 copy-start.15
  403.8 4.4 copy-start.23
  408.2 1.6 copy-start.24
  408.6 1.9 copy-start.17
  408.6 2.2 copy-start.31
  413.6 1.3 copy-start.18
  413.6 2.1 copy-start.20
  413.6 2.7 copy-start.21
  426.5 3.3 copy-start.32
  426.5 3.3 copy-start.33
  428.4 5.1 copy-start.26
  428.4 17.0 %collective-permute-start.1 = (f32[2,3,512]{2,1,0:T(4,128)S(1)}, f32[2,3,512]{2,1,0:T(4,128)S(1)}, u32[]{:S(2)}, u32[]{:S(2)}) collective-permute-start(f32[2,3,512]{2,1,0:T(4,128)S(1)} %pad_add_fusion.1), channel_id=1, source_target_pairs={{8,0},{16,8},{24,16},{32,24},{40,32},{48,40},{56,48},{64,56},{72,6... | collective-permute-start | bytes 36872 | tf_op jit(solution)/shard_map/ppermute | solution.py:963
  434.8 7.0 %copy-start.25 = (f32[8,22,1024]{2,1,0:T(8,128)S(1)}, f32[8,22,1024]{2,1,0:T(8,128)}, u32[]{:S(2)}) copy-start(f32[8,22,1024]{2,1,0:T(8,128)} %slice_convert_fusion.2) | copy-start | bytes 2162692
  442.8 2.6 copy-start.19
  445.4 2.2 copy-start.35
  452.9 3.9 copy-start.6
